TPU v7x, 128 devices: a whole 4x4x4 slice. The times are simulated.
128 devices in a mesh: band: 4 (over y_hi, core), space: 32 (over z, y_lo, x).
Axes of the slice: x: 4, y: 4 (y_hi: 2, y_lo: 2; y = y_hi * 2 + y_lo), z: 4, core: 2. Of those that a mesh axis runs over, the one named last changes fastest.
Arguments:
- orbitals: float32 [4, 32, 24, 192, 128], P('band', 'space'), may hold values from -3200 to 3200
- potential: float32 [32, 24, 192, 128], P('space'), may hold values from -0.5 to 0.5
Outputs:
- filtered: float32 [4, 32, 24, 192, 128], P('band', 'space')
- correlation: float32 [4, 4], replicated
All inputs are finite; a program needn't handle non-finite values.
Results may differ from a plain program's by a relative error of at most 0.00095.
Values sent between devices are 32-bit elements; how exact they have to be, the bound alone decides.
No kernel may reach another device: no remote copies, remote signals or barrier semaphores. Data moves between devices by JAX's collectives and lax.ppermute only.
A program may use at most 64 MiB of HBM per device.

v0:
```python
import math

import jax
import jax.numpy as jnp
from jax import lax
from jax.sharding import PartitionSpec as P


def swapped(array, axis, distance):
    return lax.ppermute(array, axis, [(i, i ^ 1 << distance) for i in range(lax.axis_size(axis))])


def from_behind(array, axis, by):
    peers = lax.axis_size(axis)
    return lax.ppermute(array, axis, [(i, (i + by) % peers) for i in range(peers)])


def stencil_weights():
    weights = []
    for offset in range(1, 7):
        value = (
            2.0
            * (-1.0) ** (offset + 1)
            * math.factorial(6) ** 2
            / (offset * offset * math.factorial(6 - offset) * math.factorial(6 + offset))
        )
        weights.append(value)
    return [-2.0 * sum(weights)] + weights


def partner_faces(face_planes, bit_index):
    return swapped(face_planes, "space", bit_index)


def neighbour_faces(source):
    below_x = from_behind(source[:, -6:], "space", 4)
    above_x = from_behind(source[:, :6], "space", -4)
    along_x = jnp.concatenate([below_x, source, above_x], axis=1)
    y_planes = jnp.concatenate([source[:, :, :6], source[:, :, -6:]], axis=2)
    y_partner = partner_faces(y_planes, 1)
    along_y = jnp.concatenate([y_partner[:, :, 6:], source, y_partner[:, :, :6]], axis=2)
    z_planes = jnp.concatenate([source[:, :, :, :6], source[:, :, :, -6:]], axis=3).transpose(
        0, 3, 1, 2
    )
    z_partner = partner_faces(z_planes, 0).transpose(0, 2, 3, 1)
    along_z = jnp.concatenate([z_partner[:, :, :, 6:], source, z_partner[:, :, :, :6]], axis=3)
    return (along_x, along_y, along_z)


def kinetic(source):
    weights = stencil_weights()
    along_x, along_y, along_z = neighbour_faces(source)
    span_x, span_y, span_z = (source.shape[1], source.shape[2], source.shape[3])
    summed_terms = 3.0 * weights[0] * source
    for offset in range(1, 7):
        beside_all = (
            along_x[:, 6 + offset : 6 + offset + span_x]
            + along_x[:, 6 - offset : 6 - offset + span_x]
        )
        beside_all = (
            beside_all
            + along_y[:, :, 6 + offset : 6 + offset + span_y]
            + along_y[:, :, 6 - offset : 6 - offset + span_y]
        )
        beside_all = (
            beside_all
            + along_z[:, :, :, 6 + offset : 6 + offset + span_z]
            + along_z[:, :, :, 6 - offset : 6 - offset + span_z]
        )
        summed_terms = summed_terms + weights[offset] * beside_all
    return -0.5 * summed_terms


def on_device(orbitals, potential):
    source = orbitals[:, 0]
    local_potential = potential[0][None]
    first_step = (kinetic(source) + local_potential * source - 9.0 * source) / 7.0
    filtered = (
        2.0 * (kinetic(first_step) + local_potential * first_step - 9.0 * first_step) / 7.0 - source
    )
    cell_count = filtered.shape[1] * filtered.shape[2] * filtered.shape[3] * lax.axis_size("space")
    gathered = lax.all_gather(filtered, "band", axis=0, tiled=True)
    flat_rows = gathered.reshape(gathered.shape[0], -1)
    partial_gram = jnp.dot(
        flat_rows, flat_rows.T, precision=lax.Precision.HIGHEST, preferred_element_type=jnp.float32
    )
    summed_gram = lax.psum(partial_gram, "space")
    return (filtered[:, None], summed_gram / jnp.float32(cell_count))


def solution(mesh):
    placed = (P("band", "space", None, None, None), P("space", None, None, None))
    return jax.shard_map(
        on_device,
        mesh=mesh,
        in_specs=placed,
        out_specs=(P("band", "space", None, None, None), P()),
        check_vma=False,
    )
```

profile of v0, /device:TPU:0, one launch (start us, length us, event | category | flops | bytes accessed | tf_op | source)
XLA Modules:
  0.0 372.5 jit_solution(6484525869524856842)
XLA Ops:
  7.2 0.0 copy-start
  7.2 0.0 all-gather.2.cloned.1.call-start
  7.2 1.1 fusion.162
  8.4 3.2 collective-permute-start.2
  11.6 2.1 fusion.161
  13.7 5.0 %collective-permute-start = (f32[1,6,192,128]{3,2,1,0:T(8,128)}, f32[1,6,192,128]{3,2,1,0:T(8,128)}, u32[]{:S(2)}, u32[]{:S(2)}) collective-permute-start(f32[1,6,192,128]{3,2,1,0:T(8,128)} %get-tuple-element.10), channel_id=1, source_target_pairs={{0,28},{1,29},{2,30},{3,31},{4,0},{5,1},{6,2},{7,3},{8,4},{9,5},{1... | collective-permute-start | bytes 1769480 | tf_op jit(solution)/shard_map/ppermute | solution.py:15
  18.7 0.0 collective-permute-start.1
  18.8 0.0 copy-done
  18.8 3.0 fusion.163
  21.8 2.6 copy.6
  24.3 2.6 copy.7
  27.0 0.7 collective-permute-start.3
  27.6 0.0 collective-permute-done.2
  27.7 1.0 fusion.167
  28.7 6.6 %collective-permute-done.3 = f32[1,12,24,192]{3,2,1,0:T(8,128)S(1)} collective-permute-done((f32[1,12,24,192]{3,2,1,0:T(8,128)S(1)}, f32[1,12,24,192]{3,2,1,0:T(8,128)S(1)}, u32[]{:S(2)}, u32[]{:S(2)}) %collective-permute-start.3) | collective-permute-done | bytes 221216 | tf_op jit(solution)/shard_map/ppermute | solution.py:10
  35.3 2.2 copy.8
  37.5 2.2 copy.9
  39.7 0.0 collective-permute-done
  39.7 5.3 %collective-permute-done.1 = f32[1,6,192,128]{3,2,1,0:T(8,128)} collective-permute-done((f32[1,6,192,128]{3,2,1,0:T(8,128)S(1)}, f32[1,6,192,128]{3,2,1,0:T(8,128)}, u32[]{:S(2)}, u32[]{:S(2)}) %collective-permute-start.1) | collective-permute-done | bytes 589856 | tf_op jit(solution)/shard_map/ppermute | solution.py:15
  44.9 20.9 %broadcast_multiply_fusion = (f32[1,24,192,128]{3,2,1,0:T(8,128)S(1)}, f32[1,24,192,128]{3,2,1,0:T(8,128)}) fusion(f32[1,24,192,128]{3,2,1,0:T(8,128)S(1)} %bitcast.16, f32[1,24,192,128]{3,2,1,0:T(8,128)} %param.3, f32[1,24,192,6]{3,2,1,0:T(8,128)} %copy.9, f32[1,24,192,6]{3,2,1,0:T(8,128)} %copy.8, f32[1,24,6,128]{3,2,1,0:T(8,128)S(1)} %get-tuple-element.23, ...), kind=kLoop, calls=%fused_computation.278 | loop fusion | flops 50135040 | bytes 10985472 | tf_op jit(solution)/shard_map/div | solution.py:77
  65.8 0.0 copy-start.1
  65.9 1.2 fusion.159
  67.1 0.7 pad_maximum_fusion.13
  67.8 0.5 collective-permute-start.6
  68.3 1.4 collective-permute-start.4
  69.7 0.6 collective-permute-start.5
  70.3 3.1 fusion.158
  73.4 0.0 copy-done.1
  73.4 3.2 copy.10
  76.7 3.2 copy.11
  79.9 1.0 maximum_bitcast_fusion.1
  80.9 1.8 collective-permute-start.7
  82.7 0.0 collective-permute-done.6
  82.7 1.7 fusion.166
  84.4 3.5 collective-permute-done.7
  87.9 0.7 fusion.164
  88.6 3.2 copy.12
  91.8 3.1 copy.13
  94.9 0.0 collective-permute-done.4
  94.9 0.0 collective-permute-done.5
  94.9 60.9 %fusion.15 = f32[1,24,192,128]{3,2,1,0:T(8,128)} fusion(f32[1,24,192,128]{3,2,1,0:T(8,128)} %copy-done.1, f32[1,24,6,128]{3,2,1,0:T(8,128)} %get-tuple-element.21, f32[1,24,6,128]{3,2,1,0:T(8,128)} %get-tuple-element.20, f32[1,6,192,128]{3,2,1,0:T(8,128)S(1)} %collective-permute-done.5, f32[1,6,192,128]{3,2,1,0:T(8,128)S(1)} %collective-permute-done.4, ...), kind=kLoop, calls=%fused_computation.115 | loop fusion | flops 50724864 | bytes 13344768 | tf_op jit(solution)/shard_map/sub | solution.py:79
  155.8 0.0 all-gather.2.cloned.1.call-update
  155.8 69.1 %all-gather.2.cloned.1.call-done = f32[4,24,192,128]{3,2,1,0:T(8,128)} async-done(((f32[1,24,192,128]{3,2,1,0:T(8,128)}), f32[4,24,192,128]{3,2,1,0:T(8,128)}) %all-gather.2.cloned.1.call-update) | async-done | bytes 9437200 | tf_op jit(solution)/shard_map/all_gather | solution.py:82
  225.0 58.2 %fusion.154 = f32[4,4]{1,0:T(4,128)S(1)} fusion(f32[4,24,192,128]{3,2,1,0:T(8,128)} %all-gather.2.cloned.1.call-done), kind=kOutput, calls=%fused_computation.279 | convolution fusion | flops 113246208 | bytes 9437248 | tf_op jit(solution)/shard_map/dot_general | solution.py:84
  283.1 81.9 %psum.7 = f32[4,4]{1,0:T(4,128)S(1)} all-reduce(f32[4,4]{1,0:T(4,128)S(1)} %fusion.154), channel_id=1, replica_groups=mesh['band'=4,'space'=32] {'space'}, use_global_device_ids=true, to_apply=%region_0.0 | all-reduce | flops 16 | bytes 128 | tf_op jit(solution)/shard_map/psum | solution.py:87
  365.1 0.6 broadcast_multiply_fusion.1
  (4 shorter events, 0.1 us)
Async XLA Ops:
  7.2 11.6 %copy-start = (f32[1,1,24,192,128]{4,3,2,1,0:T(8,128)S(1)}, f32[1,1,24,192,128]{4,3,2,1,0:T(8,128)}, u32[]{:S(2)}) copy-start(f32[1,1,24,192,128]{4,3,2,1,0:T(8,128)} %param.2) | copy-start | bytes 7077892
  7.2 217.8 %all-gather.2.cloned.1.call-start = ((), (), s32[]{:S(2)}) async-start(), calls=%async_computation | async-start | bytes 11796480 | tf_op jit(solution)/shard_map/all_gather | solution.py:82
  8.4 19.3 %collective-permute-start.2 = (f32[1,24,12,128]{3,2,1,0:T(8,128)S(1)}, f32[1,24,12,128]{3,2,1,0:T(8,128)}, u32[]{:S(2)}, u32[]{:S(2)}) collective-permute-start(f32[1,24,12,128]{3,2,1,0:T(8,128)S(1)} %pad_maximum_fusion.12), channel_id=1, source_target_pairs={{0,2},{1,3},{2,0},{3,1},{4,6},{5,7},{6,4},{7,5},{8,10},{9,11},{10,... | collective-permute-start | bytes 442376 | tf_op jit(solution)/shard_map/ppermute | solution.py:10
  13.7 26.0 %collective-permute-start = (f32[1,6,192,128]{3,2,1,0:T(8,128)}, f32[1,6,192,128]{3,2,1,0:T(8,128)}, u32[]{:S(2)}, u32[]{:S(2)}) collective-permute-start(f32[1,6,192,128]{3,2,1,0:T(8,128)} %get-tuple-element.10), channel_id=1, source_target_pairs={{0,28},{1,29},{2,30},{3,31},{4,0},{5,1},{6,2},{7,3},{8,4},{9,5},{1... | collective-permute-start | bytes 1769480 | tf_op jit(solution)/shard_map/ppermute | solution.py:15
  18.7 26.2 %collective-permute-start.1 = (f32[1,6,192,128]{3,2,1,0:T(8,128)S(1)}, f32[1,6,192,128]{3,2,1,0:T(8,128)}, u32[]{:S(2)}, u32[]{:S(2)}) collective-permute-start(f32[1,6,192,128]{3,2,1,0:T(8,128)S(1)} %get-tuple-element.11), channel_id=1, source_target_pairs={{0,4},{1,5},{2,6},{3,7},{4,8},{5,9},{6,10},{7,11},{8,12},{9,13},{1... | collective-permute-start | bytes 1769480 | tf_op jit(solution)/shard_map/ppermute | solution.py:15
  27.0 8.3 %collective-permute-start.3 = (f32[1,12,24,192]{3,2,1,0:T(8,128)S(1)}, f32[1,12,24,192]{3,2,1,0:T(8,128)S(1)}, u32[]{:S(2)}, u32[]{:S(2)}) collective-permute-start(f32[1,12,24,192]{3,2,1,0:T(8,128)S(1)} %maximum_bitcast_fusion), channel_id=1, source_target_pairs={{0,1},{1,0},{2,3},{3,2},{4,5},{5,4},{6,7},{7,6},{8,9},{9,8},{10,11... | collective-permute-start | bytes 663560 | tf_op jit(solution)/shard_map/ppermute | solution.py:10
  65.8 7.6 %copy-start.1 = (f32[1,24,192,128]{3,2,1,0:T(8,128)}, f32[1,24,192,128]{3,2,1,0:T(8,128)S(1)}, u32[]{:S(2)}) copy-start(f32[1,24,192,128]{3,2,1,0:T(8,128)S(1)} %get-tuple-element.2) | copy-start | bytes 7077892
  67.8 14.9 %collective-permute-start.6 = (f32[1,24,12,128]{3,2,1,0:T(8,128)}, f32[1,24,12,128]{3,2,1,0:T(8,128)}, u32[]{:S(2)}, u32[]{:S(2)}) collective-permute-start(f32[1,24,12,128]{3,2,1,0:T(8,128)} %pad_maximum_fusion.13), channel_id=1, source_target_pairs={{0,2},{1,3},{2,0},{3,1},{4,6},{5,7},{6,4},{7,5},{8,10},{9,11},{10,... | collective-permute-start | bytes 442376 | tf_op jit(solution)/shard_map/ppermute | solution.py:10
  68.3 26.6 %collective-permute-start.4 = (f32[1,6,192,128]{3,2,1,0:T(8,128)}, f32[1,6,192,128]{3,2,1,0:T(8,128)S(1)}, u32[]{:S(2)}, u32[]{:S(2)}) collective-permute-start(f32[1,6,192,128]{3,2,1,0:T(8,128)} %get-tuple-element.6), channel_id=1, source_target_pairs={{0,28},{1,29},{2,30},{3,31},{4,0},{5,1},{6,2},{7,3},{8,4},{9,5},{1... | collective-permute-start | bytes 1769480 | tf_op jit(solution)/shard_map/ppermute | solution.py:15
  69.7 25.2 %collective-permute-start.5 = (f32[1,6,192,128]{3,2,1,0:T(8,128)}, f32[1,6,192,128]{3,2,1,0:T(8,128)S(1)}, u32[]{:S(2)}, u32[]{:S(2)}) collective-permute-start(f32[1,6,192,128]{3,2,1,0:T(8,128)} %get-tuple-element.7), channel_id=1, source_target_pairs={{0,4},{1,5},{2,6},{3,7},{4,8},{5,9},{6,10},{7,11},{8,12},{9,13},{1... | collective-permute-start | bytes 1769480 | tf_op jit(solution)/shard_map/ppermute | solution.py:15
  80.9 7.0 %collective-permute-start.7 = (f32[1,12,24,192]{3,2,1,0:T(8,128)S(1)}, f32[1,12,24,192]{3,2,1,0:T(8,128)S(1)}, u32[]{:S(2)}, u32[]{:S(2)}) collective-permute-start(f32[1,12,24,192]{3,2,1,0:T(8,128)S(1)} %maximum_bitcast_fusion.1), channel_id=1, source_target_pairs={{0,1},{1,0},{2,3},{3,2},{4,5},{5,4},{6,7},{7,6},{8,9},{9,8},{10,11... | collective-permute-start | bytes 663560 | tf_op jit(solution)/shard_map/ppermute | solution.py:10
Sparse Core Ops, SparseCore 0:
  156.0 68.9 all-gather.1
where the time goes:
time: 373 us
  waiting for transfers between devices  84.5 us (23%)
  other arithmetic  84.2 us (23%)
  blocking collectives  81.9 us (22%)
  matrix products  58.2 us (16%)
  local copies, waits for them, and re-layouts  36.4 us (10%)
  between operations  14.1 us (4%)
  starting transfers between devices  13.2 us (4%)
    psum x1, blocking collectives, on_device(): summed_gram = lax.psum(partial_gram, 'space')  81.9 us
    all_gather x1, waiting for transfers between devices, on_device(): gathered = lax.all_gather(filtered, 'band', axis=0, tiled=True)  69.1 us
    sub x1, other arithmetic, on_device(): 2.0 * (kinetic(first_step) + local_potential * first_step - 9.0 * first_s...  60.9 us
    dot_general x1, matrix products, on_device(): jnp.dot(flat_rows, flat_rows.T, precision=lax.Precision.HIGHEST, preferre...  58.2 us
    div x1, other arithmetic, on_device(): (kinetic(source) + local_potential * source - 9.0 * source) / 7.0  20.9 us
    slice x4, local copies, waits for them, and re-layouts, neighbour_faces(): source[:, :, :, :6]  11.9 us
    ppermute x4, waiting for transfers between devices, swapped(): lax.ppermute(array, axis, [(i, i ^ 1 << distance) for i in range(lax.axis...  10.1 us
  transfers between devices with their start and end apart: 9, of which 4 were waited for; matrix products, arithmetic and copies ran while one was open for 9% of the time, Pallas kernels for 0%

commit v1 on v0

v1 whole, which is shorter than its diff:
```python
import functools
import math

import jax
import jax.numpy as jnp
import ml_dtypes
import numpy as np
from jax import lax
from jax.experimental import pallas as pl
from jax.experimental.pallas import tpu as pltpu
from jax.sharding import PartitionSpec as P

REACH = 6
ROWS = 24
LANES = 128
SLOT = 16


def stencil_weights():
    weights = []
    for offset in range(1, 7):
        value = (
            2.0
            * (-1.0) ** (offset + 1)
            * math.factorial(6) ** 2
            / (offset * offset * math.factorial(6 - offset) * math.factorial(6 + offset))
        )
        weights.append(value)
    return [-2.0 * sum(weights)] + weights


WEIGHTS = stencil_weights()
CENTER = (-1.5 * WEIGHTS[0] - 9.0) / 7.0
SIDE = [0.0] + [-0.5 * w / 7.0 for w in WEIGHTS[1:]]


def side_weight(distance):
    distance = abs(distance)
    return SIDE[distance] if 1 <= distance <= REACH else 0.0


def z_matrices(groups):
    whole = np.zeros((groups, 2 * LANES, LANES))
    for z in range(LANES):
        for other in range(max(0, z - REACH), min(LANES, z + REACH + 1)):
            whole[:, other, z] = side_weight(other - z)
        for c in range(2 * REACH):
            position = LANES + c if c < REACH else c - 2 * REACH
            for group in range(groups):
                whole[group, LANES + SLOT * group + c, z] = side_weight(position - z)
    high = whole.astype(ml_dtypes.bfloat16)
    low = (whole - high.astype(np.float64)).astype(ml_dtypes.bfloat16)
    return high, low


def selection(groups):
    chosen = np.zeros((groups, 2 * LANES, LANES), ml_dtypes.bfloat16)
    for group in range(groups):
        for c in range(2 * REACH):
            lane = c if c < REACH else LANES - 2 * REACH + c
            chosen[group, lane, SLOT * group + c] = 1
            chosen[group, LANES + lane, SLOT * group + c] = 1
    return chosen


def split(values):
    high = values.astype(jnp.bfloat16)
    low = (values - high.astype(jnp.float32)).astype(jnp.bfloat16)
    return high, low


def pack_kernel(counts, *refs):
    pieces, choose_ref, y_ref, z_ref = refs[: len(counts)], refs[-3], refs[-2], refs[-1]
    rows = pieces[0].shape[1]
    at = 0
    for count, piece in zip(counts, pieces):
        y_ref[at : at + count, 0:8, :] = piece[:, 0:8, :]
        y_ref[at : at + count, 8:16, :] = piece[:, rows - 8 : rows, :]
        total = None
        for group in range(rows // ROWS):
            block = piece[:, group * ROWS : (group + 1) * ROWS, :].reshape(count * ROWS, LANES)
            high, low = split(block)
            part = jnp.dot(
                jnp.concatenate([high, low], axis=1),
                choose_ref[group],
                preferred_element_type=jnp.float32,
            )
            total = part if total is None else total + part
        z_ref[at : at + count, :, :] = total.reshape(count, ROWS, LANES)
        at += count


def pack_faces(pieces):
    counts = [piece.shape[0] for piece in pieces]
    planes, rows = sum(counts), pieces[0].shape[1]
    groups = rows // ROWS
    return pl.pallas_call(
        functools.partial(pack_kernel, counts),
        out_shape=(
            jax.ShapeDtypeStruct((planes, 16, LANES), jnp.float32),
            jax.ShapeDtypeStruct((planes, ROWS, LANES), jnp.float32),
        ),
        in_specs=[pl.BlockSpec(memory_space=pltpu.VMEM)] * (len(pieces) + 1),
        out_specs=(pl.BlockSpec(memory_space=pltpu.VMEM),) * 2,
        compiler_params=pltpu.CompilerParams(vmem_limit_bytes=32 << 20),
        cost_estimate=pl.CostEstimate(
            flops=planes * rows * LANES * 4, bytes_accessed=planes * rows * LANES * 4, transcendentals=0
        ),
        name="pack_faces",
    )(*pieces, jnp.asarray(selection(groups)))


def stencil_kernel(counts, second, groups, band_ref, *refs):
    n = len(counts)
    current, before, after = refs[:n], refs[n : 2 * n], refs[2 * n : 3 * n]
    y_ref, z_ref, potential_ref, high_ref, low_ref, halo_ref = refs[3 * n : 3 * n + 6]
    rest = list(refs[3 * n + 6 :])
    planes = sum(counts)
    source_ref = rest.pop(0) if second else None
    extended, gathered = rest[-2:]
    outputs = rest[:-2]
    step = pl.program_id(0)
    group = step ^ (2 * band_ref[0]) if second else step
    at = 0
    for index, count in enumerate(counts):
        here = slice(at, at + count)
        extended[here, 8 : 8 + ROWS, :] = current[index][...]
        extended[here, 0:8, :] = jnp.where(group == 0, y_ref[here, 8:16, :], before[index][...])
        extended[here, 8 + ROWS : 16 + ROWS, :] = jnp.where(
            group == groups - 1, y_ref[here, 0:8, :], after[index][...]
        )
        at += count
    own_high, own_low = split(extended[:, 8 : 8 + ROWS, :].reshape(planes * ROWS, LANES))
    face_high, face_low = split(z_ref[...].reshape(planes * ROWS, LANES))
    both_high = jnp.concatenate([own_high, face_high], axis=1)
    both_low = jnp.concatenate([own_low, face_low], axis=1)
    weights_high, weights_low = high_ref[0], low_ref[0]
    along_z = jnp.dot(both_high, weights_high, preferred_element_type=jnp.float32)
    along_z += jnp.dot(both_low, weights_high, preferred_element_type=jnp.float32)
    along_z += jnp.dot(both_high, weights_low, preferred_element_type=jnp.float32)
    gathered[...] = along_z.reshape(planes, ROWS, LANES)
    for tile in range(ROWS // 8):
        top = 8 + 8 * tile
        within = slice(8 * tile, 8 * tile + 8)
        own = [extended[p, top : top + 8, :] for p in range(planes)]
        for p in range(planes):
            total = gathered[p, within, :] + (CENTER + potential_ref[p, within, :] * (1.0 / 7.0)) * own[p]
            for k in range(1, REACH + 1):
                beside = extended[p, top + k : top + k + 8, :] + extended[p, top - k : top - k + 8, :]
                if p - k >= 0:
                    beside = beside + own[p - k]
                elif not second:
                    beside = beside + halo_ref[REACH + p - k, within, :]
                if p + k < planes:
                    beside = beside + own[p + k]
                elif second:
                    beside = beside + halo_ref[p + k - planes, within, :]
                total = total + SIDE[k] * beside
            if not second:
                target, q = (outputs[0], p) if p < planes - REACH else (outputs[1], p - planes + REACH)
                target[q, within, :] = total
            else:
                outputs[0][p, within, :] = 2.0 * total - source_ref[p, within, :]
    if second:
        for slot in range(4):

            @pl.when(step // 2 == slot)
            def _(slot=slot):
                half = pl.ds(pl.multiple_of((step % 2) * ROWS, 8), ROWS)
                outputs[1 + slot][:, half, :] = outputs[0][REACH:planes, :, :]


def apply_stencil(pieces, faces, potential, halo, band, source=None):
    second = source is not None
    counts = [piece.shape[0] for piece in pieces]
    planes, rows = sum(counts), pieces[0].shape[1]
    groups = rows // ROWS
    per = ROWS // 8
    y_faces, z_faces = faces

    def group_of(step, s):
        return step ^ (2 * s[0]) if second else step

    def now(step, s):
        return (0, group_of(step, s), 0)

    def previous(step, s):
        return (0, jnp.maximum(per * group_of(step, s) - 1, 0), 0)

    def following(step, s):
        return (0, jnp.minimum(per * group_of(step, s) + per, per * groups - 1), 0)

    def fixed(step, s):
        return (0, 0, 0)

    def weights_at(step, s):
        return (group_of(step, s), 0, 0)

    in_specs = [pl.BlockSpec((count, ROWS, LANES), now) for count in counts]
    in_specs += [pl.BlockSpec((count, 8, LANES), previous) for count in counts]
    in_specs += [pl.BlockSpec((count, 8, LANES), following) for count in counts]
    in_specs += [
        pl.BlockSpec((planes, 16, LANES), fixed),
        pl.BlockSpec((planes, ROWS, LANES), fixed),
        pl.BlockSpec((planes, ROWS, LANES), now),
        pl.BlockSpec((1, 2 * LANES, LANES), weights_at),
        pl.BlockSpec((1, 2 * LANES, LANES), weights_at),
        pl.BlockSpec((REACH, ROWS, LANES), now),
    ]
    high, low = z_matrices(groups)
    operands = list(pieces) * 3 + [y_faces, z_faces, potential, jnp.asarray(high), jnp.asarray(low), halo]
    if second:
        in_specs.append(pl.BlockSpec((planes, ROWS, LANES), now))
        operands.append(source)
        out_shape = [jax.ShapeDtypeStruct((planes, rows, LANES), jnp.float32)]
        out_specs = [pl.BlockSpec((planes, ROWS, LANES), now)]
        for _ in range(4):
            out_shape.append(jax.ShapeDtypeStruct((planes - REACH, rows // 4, LANES), jnp.float32))
            out_specs.append(pl.BlockSpec((planes - REACH, rows // 4, LANES), fixed))
    else:
        out_shape = [
            jax.ShapeDtypeStruct((planes - REACH, rows, LANES), jnp.float32),
            jax.ShapeDtypeStruct((REACH, rows, LANES), jnp.float32),
        ]
        out_specs = [
            pl.BlockSpec((planes - REACH, ROWS, LANES), now),
            pl.BlockSpec((REACH, ROWS, LANES), now),
        ]
    cells = planes * rows * LANES
    return pl.pallas_call(
        functools.partial(stencil_kernel, counts, second, groups),
        out_shape=out_shape,
        grid_spec=pltpu.PrefetchScalarGridSpec(
            num_scalar_prefetch=1,
            grid=(groups,),
            in_specs=in_specs,
            out_specs=out_specs,
            scratch_shapes=[
                pltpu.VMEM((planes, ROWS + 16, LANES), jnp.float32),
                pltpu.VMEM((planes, ROWS, LANES), jnp.float32),
            ],
        ),
        compiler_params=pltpu.CompilerParams(
            vmem_limit_bytes=40 << 20, dimension_semantics=("arbitrary",)
        ),
        cost_estimate=pl.CostEstimate(flops=cells * 60, bytes_accessed=cells * 16, transcendentals=0),
        name="second_step" if second else "first_step",
    )(band, *operands)


def halo_terms(partial_ref, halo_ref, high_side, factor, planes):
    done = []
    for j in range(planes):
        total = partial_ref[j]
        for k in range(1, REACH + 1):
            m = j + k - REACH if high_side else REACH + j - k
            if 0 <= m < REACH:
                total = total + (factor * SIDE[k]) * halo_ref[m]
        done.append(total)
    return done


def high_side_kernel(partial_ref, halo_ref, out_ref):
    for j, total in enumerate(halo_terms(partial_ref, halo_ref, True, 1.0, REACH)):
        out_ref[j] = total


def finish_first(partial, halo):
    rows = partial.shape[1]
    block = pl.BlockSpec((REACH, rows // 4, LANES), lambda step: (0, step, 0))
    cells = REACH * rows * LANES
    return pl.pallas_call(
        high_side_kernel,
        out_shape=jax.ShapeDtypeStruct(partial.shape, jnp.float32),
        grid=(4,),
        in_specs=[block, block],
        out_specs=block,
        cost_estimate=pl.CostEstimate(flops=cells * 8, bytes_accessed=cells * 12, transcendentals=0),
        name="finish_first",
    )(partial, halo)


def low_side_kernel(band_ref, partial_ref, halo_ref, out_ref, *slots):
    step = pl.program_id(0)
    for j, total in enumerate(halo_terms(partial_ref, halo_ref, False, 2.0, REACH)):
        out_ref[j] = total
    for slot in range(4):

        @pl.when(step == slot)
        def _(slot=slot):
            slots[slot][...] = out_ref[...]


def finish_filtered(filtered, halo, band):
    rows = filtered.shape[1]
    part = (REACH, rows // 4, LANES)
    block = pl.BlockSpec(part, lambda step, s: (0, step ^ s[0], 0))
    whole = pl.BlockSpec(part, lambda step, s: (0, 0, 0))
    cells = REACH * rows * LANES
    return pl.pallas_call(
        low_side_kernel,
        out_shape=[jax.ShapeDtypeStruct(filtered.shape, jnp.float32)]
        + [jax.ShapeDtypeStruct(part, jnp.float32)] * 4,
        grid_spec=pltpu.PrefetchScalarGridSpec(
            num_scalar_prefetch=1,
            grid=(4,),
            in_specs=[block, block],
            out_specs=[block] + [whole] * 4,
        ),
        input_output_aliases={1: 0},
        cost_estimate=pl.CostEstimate(flops=cells * 8, bytes_accessed=cells * 16, transcendentals=0),
        name="finish_filtered",
    )(band, filtered, halo)


PAIRS = [(i, j) for i in range(4) for j in range(i, 4)]


def add_products(refs, totals):
    planes, rows = refs[0].shape[0], refs[0].shape[1]

    def body(p, carried):
        carried = list(carried)
        for tile in range(rows // 8):
            values = [ref[p, 8 * tile : 8 * tile + 8, :] for ref in refs]
            for n, (i, j) in enumerate(PAIRS):
                carried[n] = carried[n] + values[i] * values[j]
        return tuple(carried)

    return lax.fori_loop(0, planes, body, tuple(totals))


def early_gram_kernel(*refs):
    out_ref = refs[-1]
    totals = add_products(refs[:4], [jnp.zeros((8, LANES), jnp.float32)] * len(PAIRS))
    for n in range(len(PAIRS)):
        out_ref[n] = totals[n]


def early_gram(parts):
    cells = parts[0].size
    return pl.pallas_call(
        early_gram_kernel,
        out_shape=jax.ShapeDtypeStruct((len(PAIRS), 8, LANES), jnp.float32),
        in_specs=[pl.BlockSpec(memory_space=pltpu.VMEM)] * 4,
        out_specs=pl.BlockSpec(memory_space=pltpu.VMEM),
        compiler_params=pltpu.CompilerParams(vmem_limit_bytes=16 << 20),
        cost_estimate=pl.CostEstimate(flops=cells * 20, bytes_accessed=cells * 16, transcendentals=0),
        name="early_gram",
    )(*parts)


def late_gram_kernel(band_ref, before_ref, *refs):
    out_ref = refs[-1]
    totals = add_products(refs[:4], [before_ref[n] for n in range(len(PAIRS))])
    band = band_ref[0]
    lane = lax.broadcasted_iota(jnp.int32, (1, LANES), 1)
    row = jnp.zeros((1, LANES), jnp.float32)
    for n, (i, j) in enumerate(PAIRS):
        value = jnp.sum(totals[n])
        first, other = band ^ i, band ^ j
        hit = (lane == 4 * first + other) | (lane == 4 * other + first)
        row = row + jnp.where(hit, value, 0.0)
    out_ref[...] = jnp.broadcast_to(row, out_ref.shape)


def late_gram(before, parts, band, peers):
    cells = parts[0].size
    return pl.pallas_call(
        late_gram_kernel,
        out_shape=jax.ShapeDtypeStruct((peers, LANES), jnp.float32),
        in_specs=[pl.BlockSpec(memory_space=pltpu.SMEM)] + [pl.BlockSpec(memory_space=pltpu.VMEM)] * 5,
        out_specs=pl.BlockSpec(memory_space=pltpu.VMEM),
        compiler_params=pltpu.CompilerParams(vmem_limit_bytes=16 << 20),
        cost_estimate=pl.CostEstimate(flops=cells * 20, bytes_accessed=cells * 16, transcendentals=0),
        name="late_gram",
    )(band, before, *parts)


def shifted(array, by):
    peers = lax.axis_size("space")
    return lax.ppermute(array, "space", [(i, (i + by) % peers) for i in range(peers)])


def swapped(array, axis, bit):
    return lax.ppermute(array, axis, [(i, i ^ bit) for i in range(lax.axis_size(axis))])


def band_exchange(slots):
    return [slots[0]] + [swapped(slots[k], "band", k) for k in (1, 2, 3)]


def on_device(orbitals, potential):
    source, local_potential = orbitals[0, 0], potential[0]
    planes = source.shape[0]
    band = lax.axis_index("band").astype(jnp.int32).reshape(1)
    below = shifted(source[planes - REACH :], 4)
    above = shifted(source[:REACH], -4)
    y_faces, z_faces = pack_faces([source])
    faces = swapped(y_faces, "space", 2), swapped(z_faces, "space", 1)
    first_main, first_top = apply_stencil([source], faces, local_potential, below, band)
    above_first = shifted(first_main[:REACH], -4)
    first_top = finish_first(first_top, above)
    below_first = shifted(first_top, 4)
    y_faces, z_faces = pack_faces([first_main, first_top])
    faces = swapped(y_faces, "space", 2), swapped(z_faces, "space", 1)
    filtered, *slots = apply_stencil(
        [first_main, first_top], faces, local_potential, above_first, band, source
    )
    early = early_gram(band_exchange(slots))
    filtered, *slots = finish_filtered(filtered, below_first, band)
    both = ("band", "space")
    peers = lax.axis_size(both)
    rows = late_gram(early, band_exchange(slots), band, peers)
    everyone = lax.all_to_all(rows, both, 0, 0, tiled=True)
    summed = jnp.sum(everyone, axis=0)[:16].reshape(4, 4)
    cell_count = filtered.size * lax.axis_size("space")
    return filtered[None, None], summed / jnp.float32(cell_count)


def solution(mesh):
    placed = (P("band", "space", None, None, None), P("space", None, None, None))
    return jax.shard_map(
        on_device,
        mesh=mesh,
        in_specs=placed,
        out_specs=(P("band", "space", None, None, None), P()),
        check_vma=False,
    )
```

time: 373 us -> 118 us (0.32)
  other arithmetic: 84.2 us -> 0.16 us
  blocking collectives: 81.9 us -> 14.6 us
  matrix products: 58.2 us -> 0 us
  waiting for transfers between devices: 84.5 us -> 35.9 us
  Pallas kernels: 0 us -> 28.1 us
  local copies, waits for them, and re-layouts: 36.4 us -> 13.9 us
  between operations: 14.1 us -> 0.75 us
  starting transfers between devices: 13.2 us -> 22.4 us
    psum x1 -> x0, blocking collectives: 81.9 us -> none  [on_device(): summed_gram = lax.psum(partial_gram, 'space')]
    all_gather x1 -> x0, waiting for transfers between devices: 69.1 us -> none  [on_device(): gathered = lax.all_gather(filtered, 'band', axis=0, tiled=True)]
    sub x1 -> x0, other arithmetic: 60.9 us -> none  [on_device(): 2.0 * (kinetic(first_step) + local_potential * first_step - 9.0 * first_s...]
    dot_general x1 -> x0, matrix products: 58.2 us -> none  [on_device(): jnp.dot(flat_rows, flat_rows.T, precision=lax.Precision.HIGHEST, preferre...]
    slice x18 -> x2, local copies, waits for them, and re-layouts: 36.4 us -> 3.38 us  [the longest x1 2.48 us: on_device(): above = shifted(source[:REACH], -4)]
    pallas_call x0 -> x8, Pallas kernels: none -> 28.1 us  [the longest x2 17 us: apply_stencil(): pl.pallas_call(functools.partial(stencil_kernel, counts, second, groups),...]
    div x2 -> x1, other arithmetic: 21.5 us -> 0.01 us  [on_device(): return (filtered[None, None], summed / jnp.float32(cell_count))]
    ppermute x8 -> x14, waiting for transfers between devices: 15.4 us -> 35.9 us  [the longest x10 35.7 us: swapped(): lax.ppermute(array, axis, [(i, i ^ bit) for i in range(lax.axis_size(axis...]
  transfers between devices with their start and end apart: 9 -> 14, of which waited for: 4 -> 7; matrix products, arithmetic and copies ran while one was open for 9% -> 1% of each run, Pallas kernels for 0% -> 24%
where the time goes in v1:
time: 118 us; the launch traced here: 116 us
  waiting for transfers between devices  35.9 us (30%)
  Pallas kernels  28.1 us (24%)
  starting transfers between devices  22.4 us (19%)
  blocking collectives  14.6 us (12%)
  local copies, waits for them, and re-layouts  13.9 us (12%)
    ppermute x10, waiting for transfers between devices, swapped(): lax.ppermute(array, axis, [(i, i ^ bit) for i in range(lax.axis_size(axis...  35.7 us
    pallas_call x2, Pallas kernels, apply_stencil(): pl.pallas_call(functools.partial(stencil_kernel, counts, second, groups),...  17 us
    all_to_all x1, blocking collectives, on_device(): everyone = lax.all_to_all(rows, both, 0, 0, tiled=True)  14.6 us
    ppermute x10, starting transfers between devices, swapped(): lax.ppermute(array, axis, [(i, i ^ bit) for i in range(lax.axis_size(axis...  13.7 us
    unnamed x28, local copies, waits for them, and re-layouts  9.88 us
    ppermute x4, starting transfers between devices, shifted(): lax.ppermute(array, 'space', [(i, (i + by) % peers) for i in range(peers)])  8.71 us
    pallas_call x1, Pallas kernels, finish_filtered(): pl.pallas_call(low_side_kernel, out_shape=[jax.ShapeDtypeStruct(filtered....  3.65 us
    pallas_call x2, Pallas kernels, pack_faces(): pl.pallas_call(functools.partial(pack_kernel, counts), out_shape=(jax.Sha...  3.48 us
  transfers between devices with their start and end apart: 14, of which 7 were waited for; matrix products, arithmetic and copies ran while one was open for 1% of the time, Pallas kernels for 24%

profile of v1, /device:TPU:0, one launch (start us, length us, event | category | flops | bytes accessed | tf_op | source)
XLA Modules:
  0.0 115.9 jit_solution(9900448340170405882)
XLA Ops:
  0.6 0.0 copy-start
  0.6 0.0 copy-start.6
  0.7 0.0 copy-start.7
  0.7 2.5 %slice_bitcast_fusion = (f32[6,192,128]{2,1,0:T(8,128)}, f32[6,192,128]{2,1,0:T(8,128)}) fusion(f32[1,1,24,192,128]{4,3,2,1,0:T(8,128)} %param.8), kind=kLoop, calls=%fused_computation | loop fusion | bytes 2359296 | tf_op jit(solution)/shard_map/slice | solution.py:398
  3.1 1.7 %collective-permute-start.2 = (f32[6,192,128]{2,1,0:T(8,128)}, f32[6,192,128]{2,1,0:T(8,128)}, u32[]{:S(2)}, u32[]{:S(2)}) collective-permute-start(f32[6,192,128]{2,1,0:T(8,128)} %get-tuple-element.35), channel_id=1, source_target_pairs={{0,4},{1,5},{2,6},{3,7},{4,8},{5,9},{6,10},{7,11},{8,12},{9,13},{1... | collective-permute-start | bytes 1769480 | tf_op jit(solution)/shard_map/ppermute | solution.py:382
  4.8 0.0 copy-done
  4.8 0.0 copy-start.8
  4.8 1.0 copy-done.8
  5.8 1.5 %pack_faces.2 = (f32[24,16,128]{2,1,0:T(8,128)}, f32[24,24,128]{2,1,0:T(8,128)}) custom-call(f32[24,192,128]{2,1,0:T(8,128)S(1)} %bitcast.11, bf16[8,256,128]{2,1,0:T(8,128)(2,1)S(1)} %copy-done.8), custom_call_target="tpu_custom_call" | custom-call | flops 2359296 | bytes 2359296 | tf_op jit(solution)/shard_map/pack_faces/pallas_call | solution.py:97
  7.3 1.5 %collective-permute-start.1 = (f32[24,24,128]{2,1,0:T(8,128)}, f32[24,24,128]{2,1,0:T(8,128)}, u32[]{:S(2)}, u32[]{:S(2)}) collective-permute-start(f32[24,24,128]{2,1,0:T(8,128)} %get-tuple-element.19), channel_id=1, source_target_pairs={{0,1},{1,0},{2,3},{3,2},{4,5},{5,4},{6,7},{7,6},{8,9},{9,8},{10,11... | collective-permute-start | bytes 884744 | tf_op jit(solution)/shard_map/ppermute | solution.py:386
  8.8 3.5 %collective-permute-start.3 = (f32[6,192,128]{2,1,0:T(8,128)}, f32[6,192,128]{2,1,0:T(8,128)}, u32[]{:S(2)}, u32[]{:S(2)}) collective-permute-start(f32[6,192,128]{2,1,0:T(8,128)} %get-tuple-element.34), channel_id=1, source_target_pairs={{0,28},{1,29},{2,30},{3,31},{4,0},{5,1},{6,2},{7,3},{8,4},{9,5},{1... | collective-permute-start | bytes 1769480 | tf_op jit(solution)/shard_map/ppermute | solution.py:382
  12.3 2.7 %collective-permute-start = (f32[24,16,128]{2,1,0:T(8,128)}, f32[24,16,128]{2,1,0:T(8,128)}, u32[]{:S(2)}, u32[]{:S(2)}) collective-permute-start(f32[24,16,128]{2,1,0:T(8,128)} %get-tuple-element.18), channel_id=1, source_target_pairs={{0,2},{1,3},{2,0},{3,1},{4,6},{5,7},{6,4},{7,5},{8,10},{9,11},{10,... | collective-permute-start | bytes 589832 | tf_op jit(solution)/shard_map/ppermute | solution.py:386
  15.0 7.5 %collective-permute-done.refs_3_ = f32[24,16,128]{2,1,0:T(8,128)} collective-permute-done((f32[24,16,128]{2,1,0:T(8,128)}, f32[24,16,128]{2,1,0:T(8,128)}, u32[]{:S(2)}, u32[]{:S(2)}) %collective-permute-start) | collective-permute-done | bytes 196640 | tf_op jit(solution)/shard_map/ppermute | solution.py:386
  22.5 0.0 collective-permute-done.1.refs_4_
  22.5 0.2 collective-permute-done.2.refs_8_
  22.7 0.0 copy-done.6
  22.7 0.0 copy-done.7
  22.8 0.0 copy-start.4
  22.8 1.7 %copy-done.4 = f32[1,24,192,128]{3,2,1,0:T(8,128)S(1)} copy-done((f32[1,24,192,128]{3,2,1,0:T(8,128)S(1)}, f32[1,24,192,128]{3,2,1,0:T(8,128)}, u32[]{:S(2)}) %copy-start.4) | copy-done | bytes 2359320
  24.4 7.6 %first_step.1 = (f32[18,192,128]{2,1,0:T(8,128)S(1)}, f32[6,192,128]{2,1,0:T(8,128)S(1)}) custom-call(s32[1]{0:T(128)} %bitcast.band_ref, f32[24,192,128]{2,1,0:T(8,128)S(1)} %bitcast.12, f32[24,192,128]{2,1,0:T(8,128)S(1)} %bitcast.13, f32[24,192,128]{2,1,0:T(8,128)S(1)} %bitcast.14, f32[24,16,128]{2,1,0:T(8,128)} %collective-permute-done.refs_3_, ...), custom_call_target="tpu_custom_call" | custom-call | flops 35389440 | bytes 9437184 | tf_op jit(solution)/shard_map/first_step/pallas_call | solution.py:230
  32.0 0.0 copy-start.10
  32.0 0.9 slice.30
  32.9 0.1 copy-done.10
  33.0 0.0 copy-start.1
  33.0 1.2 %copy-done.1 = f32[18,192,128]{2,1,0:T(8,128)} copy-done((f32[18,192,128]{2,1,0:T(8,128)}, f32[18,192,128]{2,1,0:T(8,128)S(1)}, u32[]{:S(2)}) %copy-start.1) | copy-done | bytes 1769496
  34.2 3.6 %collective-permute-start.6 = (f32[6,192,128]{2,1,0:T(8,128)}, f32[6,192,128]{2,1,0:T(8,128)}, u32[]{:S(2)}, u32[]{:S(2)}) collective-permute-start(f32[6,192,128]{2,1,0:T(8,128)} %slice.30), channel_id=1, source_target_pairs={{0,28},{1,29},{2,30},{3,31},{4,0},{5,1},{6,2},{7,3},{8,4},{9,5},{1... | collective-permute-start | bytes 1769480 | tf_op jit(solution)/shard_map/ppermute | solution.py:382
  37.8 0.0 collective-permute-done.3.halo_ref
  37.8 3.4 %finish_first.1.refs_1_.refs_3_.refs_5_ = f32[6,192,128]{2,1,0:T(8,128)} custom-call(f32[6,192,128]{2,1,0:T(8,128)} %copy-done.10, f32[6,192,128]{2,1,0:T(8,128)} %collective-permute-done.3.halo_ref), custom_call_target="tpu_custom_call" | custom-call | flops 1179648 | bytes 1769472 | tf_op jit(solution)/shard_map/finish_first/pallas_call | solution.py:272
  41.2 0.0 copy-start.2
  41.2 1.5 %copy-done.2 = f32[18,192,128]{2,1,0:T(8,128)S(1)} copy-done((f32[18,192,128]{2,1,0:T(8,128)S(1)}, f32[18,192,128]{2,1,0:T(8,128)}, u32[]{:S(2)}) %copy-start.2) | copy-done | bytes 1769496
  42.7 1.0 copy-done.9
  43.7 2.0 %pack_faces.3 = (f32[24,16,128]{2,1,0:T(8,128)S(1)}, f32[24,24,128]{2,1,0:T(8,128)S(1)}) custom-call(f32[18,192,128]{2,1,0:T(8,128)S(1)} %copy-done.2, f32[6,192,128]{2,1,0:T(8,128)} %finish_first.1.refs_1_.refs_3_.refs_5_, bf16[8,256,128]{2,1,0:T(8,128)(2,1)S(1)} %copy-done.9), custom_call_target="tpu_custom_call" | custom-call | flops 2359296 | bytes 2359296 | tf_op jit(solution)/shard_map/pack_faces/pallas_call | solution.py:97
  45.7 0.3 collective-permute-start.5
  46.0 2.5 %collective-permute-start.4 = (f32[24,16,128]{2,1,0:T(8,128)S(1)}, f32[24,16,128]{2,1,0:T(8,128)S(1)}, u32[]{:S(2)}, u32[]{:S(2)}) collective-permute-start(f32[24,16,128]{2,1,0:T(8,128)S(1)} %get-tuple-element.22), channel_id=1, source_target_pairs={{0,2},{1,3},{2,0},{3,1},{4,6},{5,7},{6,4},{7,5},{8,10},{9,11},{10,... | collective-permute-start | bytes 589832 | tf_op jit(solution)/shard_map/ppermute | solution.py:386
  48.5 0.0 collective-permute-start.7
  48.5 9.0 %collective-permute-done.4.refs_6_ = f32[24,16,128]{2,1,0:T(8,128)S(1)} collective-permute-done((f32[24,16,128]{2,1,0:T(8,128)S(1)}, f32[24,16,128]{2,1,0:T(8,128)S(1)}, u32[]{:S(2)}, u32[]{:S(2)}) %collective-permute-start.4) | collective-permute-done | bytes 196640 | tf_op jit(solution)/shard_map/ppermute | solution.py:386
  57.5 0.0 collective-permute-done.5.refs_7_
  57.5 0.0 collective-permute-done.6.refs_11_
  57.5 0.0 copy-done.3
  57.5 0.0 copy-start.5
  57.5 1.7 %copy-done.5 = f32[1,24,192,128]{3,2,1,0:T(8,128)S(1)} copy-done((f32[1,24,192,128]{3,2,1,0:T(8,128)S(1)}, f32[1,24,192,128]{3,2,1,0:T(8,128)}, u32[]{:S(2)}) %copy-start.5) | copy-done | bytes 2359320
  59.2 9.4 %second_step.1 = (f32[24,192,128]{2,1,0:T(8,128)}, f32[18,48,128]{2,1,0:T(8,128)S(1)}, f32[18,48,128]{2,1,0:T(8,128)}, f32[18,48,128]{2,1,0:T(8,128)}, f32[18,48,128]{2,1,0:T(8,128)}) custom-call(s32[1]{0:T(128)} %bitcast.band_ref, f32[18,192,128]{2,1,0:T(8,128)S(1)} %copy-done.3, f32[6,192,128]{2,1,0:T(8,128)} %finish_first.1.refs_1_.refs_3_.refs_5_, ...), custom_call_target="tpu_custom_call" | custom-call | flops 35389440 | bytes 9437184 | tf_op jit(solution)/shard_map/second_step/pallas_call | solution.py:230
  68.6 0.8 copy-done.11
  69.3 0.0 collective-permute-start.10
  69.3 3.0 %collective-permute-start.8 = (f32[18,48,128]{2,1,0:T(8,128)}, f32[18,48,128]{2,1,0:T(8,128)S(1)}, u32[]{:S(2)}, u32[]{:S(2)}) collective-permute-start(f32[18,48,128]{2,1,0:T(8,128)} %get-tuple-element.27), channel_id=1, source_target_pairs={{0,32},{32,0},{64,96},{96,64},{1,33},{33,1},{65,97},{97,65},{2,34}... | collective-permute-start | bytes 1327112 | tf_op jit(solution)/shard_map/ppermute | solution.py:386
  72.4 0.6 collective-permute-start.9
  73.0 0.0 collective-permute-done.7.halo_ref
  73.0 3.7 %finish_filtered.1 = (f32[24,192,128]{2,1,0:T(8,128)}, f32[6,48,128]{2,1,0:T(8,128)}, f32[6,48,128]{2,1,0:T(8,128)}, f32[6,48,128]{2,1,0:T(8,128)}, f32[6,48,128]{2,1,0:T(8,128)}) custom-call(s32[1]{0:T(128)} %bitcast.band_ref, f32[24,192,128]{2,1,0:T(8,128)} %get-tuple-element.24.partial_ref, ...), custom_call_target="tpu_custom_call", output_to_operand_aliasing={{0}: (1, {})} | custom-call | flops 1179648 | bytes 2359296 | tf_op jit(solution)/shard_map/finish_filtered/pallas_call | solution.py:300
  76.6 0.0 collective-permute-start.11
  76.7 3.0 %collective-permute-start.12 = (f32[6,48,128]{2,1,0:T(8,128)}, f32[6,48,128]{2,1,0:T(8,128)S(1)}, u32[]{:S(2)}, u32[]{:S(2)}) collective-permute-start(f32[6,48,128]{2,1,0:T(8,128)} %get-tuple-element.32), channel_id=1, source_target_pairs={{0,64},{32,96},{64,0},{96,32},{1,65},{33,97},{65,1},{97,33},{2,66}... | collective-permute-start | bytes 442376 | tf_op jit(solution)/shard_map/ppermute | solution.py:386
  79.7 3.8 %collective-permute-done.10.refs_3_ = f32[18,48,128]{2,1,0:T(8,128)S(1)} collective-permute-done((f32[18,48,128]{2,1,0:T(8,128)}, f32[18,48,128]{2,1,0:T(8,128)S(1)}, u32[]{:S(2)}, u32[]{:S(2)}) %collective-permute-start.10) | collective-permute-done | bytes 442400 | tf_op jit(solution)/shard_map/ppermute | solution.py:386
  83.5 0.0 collective-permute-start.13
  83.5 0.0 collective-permute-done.8.refs_1_
  83.5 9.4 %collective-permute-done.9.refs_2_ = f32[18,48,128]{2,1,0:T(8,128)S(1)} collective-permute-done((f32[18,48,128]{2,1,0:T(8,128)}, f32[18,48,128]{2,1,0:T(8,128)S(1)}, u32[]{:S(2)}, u32[]{:S(2)}) %collective-permute-start.9) | collective-permute-done | bytes 442400 | tf_op jit(solution)/shard_map/ppermute | solution.py:386
  92.9 0.0 copy-done.12
  92.9 0.4 early_gram.1.before_ref
  93.3 0.0 collective-permute-done.11.refs_1_
  93.3 2.8 %collective-permute-done.12.refs_2_ = f32[6,48,128]{2,1,0:T(8,128)S(1)} collective-permute-done((f32[6,48,128]{2,1,0:T(8,128)}, f32[6,48,128]{2,1,0:T(8,128)S(1)}, u32[]{:S(2)}, u32[]{:S(2)}) %collective-permute-start.12) | collective-permute-done | bytes 147488 | tf_op jit(solution)/shard_map/ppermute | solution.py:386
  96.1 3.2 %collective-permute-done.13.refs_3_ = f32[6,48,128]{2,1,0:T(8,128)S(1)} collective-permute-done((f32[6,48,128]{2,1,0:T(8,128)}, f32[6,48,128]{2,1,0:T(8,128)S(1)}, u32[]{:S(2)}, u32[]{:S(2)}) %collective-permute-start.13) | collective-permute-done | bytes 147488 | tf_op jit(solution)/shard_map/ppermute | solution.py:386
  99.3 0.9 copy-done.13
  100.2 0.2 late_gram.1
  100.4 14.6 %all_to_all.9 = f32[128,1,128]{2,1,0:T(1,128)S(1)} all-to-all(f32[128,1,128]{2,1,0:T(1,128)S(1)} %bitcast.18), channel_id=1, replica_groups=mesh['band'=4,'space'=32] {'band','space'}, dimensions={0} | all-to-all | bytes 131072 | tf_op jit(solution)/shard_map/all_to_all | solution.py:415
  115.1 0.2 reduce_sum.9
  115.2 0.7 div.6
  (6 shorter events, 0.0 us)
Async XLA Ops:
  0.6 4.2 %copy-start = (f32[1,1,24,192,128]{4,3,2,1,0:T(8,128)S(1)}, f32[1,1,24,192,128]{4,3,2,1,0:T(8,128)}, u32[]{:S(2)}) copy-start(f32[1,1,24,192,128]{4,3,2,1,0:T(8,128)} %param.8) | copy-start | bytes 7077892
  0.6 22.1 %copy-start.6 = (bf16[8,256,128]{2,1,0:T(8,128)(2,1)S(1)}, bf16[8,256,128]{2,1,0:T(8,128)(2,1)}, u32[]{:S(2)}) copy-start(bf16[8,256,128]{2,1,0:T(8,128)(2,1)} %constant.18.clone.refs_6_.refs_9_) | copy-start | bytes 1572868
  0.7 22.1 %copy-start.7 = (bf16[8,256,128]{2,1,0:T(8,128)(2,1)S(1)}, bf16[8,256,128]{2,1,0:T(8,128)(2,1)}, u32[]{:S(2)}) copy-start(bf16[8,256,128]{2,1,0:T(8,128)(2,1)} %constant.19.clone.refs_7_.refs_10_) | copy-start | bytes 1572868
  3.1 19.6 %collective-permute-start.2 = (f32[6,192,128]{2,1,0:T(8,128)}, f32[6,192,128]{2,1,0:T(8,128)}, u32[]{:S(2)}, u32[]{:S(2)}) collective-permute-start(f32[6,192,128]{2,1,0:T(8,128)} %get-tuple-element.35), channel_id=1, source_target_pairs={{0,4},{1,5},{2,6},{3,7},{4,8},{5,9},{6,10},{7,11},{8,12},{9,13},{1... | collective-permute-start | bytes 1769480 | tf_op jit(solution)/shard_map/ppermute | solution.py:382
  4.8 1.0 copy-start.8
  7.3 15.2 %collective-permute-start.1 = (f32[24,24,128]{2,1,0:T(8,128)}, f32[24,24,128]{2,1,0:T(8,128)}, u32[]{:S(2)}, u32[]{:S(2)}) collective-permute-start(f32[24,24,128]{2,1,0:T(8,128)} %get-tuple-element.19), channel_id=1, source_target_pairs={{0,1},{1,0},{2,3},{3,2},{4,5},{5,4},{6,7},{7,6},{8,9},{9,8},{10,11... | collective-permute-start | bytes 884744 | tf_op jit(solution)/shard_map/ppermute | solution.py:386
  8.8 29.0 %collective-permute-start.3 = (f32[6,192,128]{2,1,0:T(8,128)}, f32[6,192,128]{2,1,0:T(8,128)}, u32[]{:S(2)}, u32[]{:S(2)}) collective-permute-start(f32[6,192,128]{2,1,0:T(8,128)} %get-tuple-element.34), channel_id=1, source_target_pairs={{0,28},{1,29},{2,30},{3,31},{4,0},{5,1},{6,2},{7,3},{8,4},{9,5},{1... | collective-permute-start | bytes 1769480 | tf_op jit(solution)/shard_map/ppermute | solution.py:382
  12.3 10.2 %collective-permute-start = (f32[24,16,128]{2,1,0:T(8,128)}, f32[24,16,128]{2,1,0:T(8,128)}, u32[]{:S(2)}, u32[]{:S(2)}) collective-permute-start(f32[24,16,128]{2,1,0:T(8,128)} %get-tuple-element.18), channel_id=1, source_target_pairs={{0,2},{1,3},{2,0},{3,1},{4,6},{5,7},{6,4},{7,5},{8,10},{9,11},{10,... | collective-permute-start | bytes 589832 | tf_op jit(solution)/shard_map/ppermute | solution.py:386
  22.8 1.7 %copy-start.4 = (f32[1,24,192,128]{3,2,1,0:T(8,128)S(1)}, f32[1,24,192,128]{3,2,1,0:T(8,128)}, u32[]{:S(2)}) copy-start(f32[1,24,192,128]{3,2,1,0:T(8,128)} %param.9) | copy-start | bytes 7077892
  32.0 1.0 copy-start.10
  33.0 1.2 %copy-start.1 = (f32[18,192,128]{2,1,0:T(8,128)}, f32[18,192,128]{2,1,0:T(8,128)S(1)}, u32[]{:S(2)}) copy-start(f32[18,192,128]{2,1,0:T(8,128)S(1)} %get-tuple-element.20.refs_0_.refs_2_.refs_4_) | copy-start | bytes 5308420
  34.2 23.3 %collective-permute-start.6 = (f32[6,192,128]{2,1,0:T(8,128)}, f32[6,192,128]{2,1,0:T(8,128)}, u32[]{:S(2)}, u32[]{:S(2)}) collective-permute-start(f32[6,192,128]{2,1,0:T(8,128)} %slice.30), channel_id=1, source_target_pairs={{0,28},{1,29},{2,30},{3,31},{4,0},{5,1},{6,2},{7,3},{8,4},{9,5},{1... | collective-permute-start | bytes 1769480 | tf_op jit(solution)/shard_map/ppermute | solution.py:382
  41.2 1.5 %copy-start.2 = (f32[18,192,128]{2,1,0:T(8,128)S(1)}, f32[18,192,128]{2,1,0:T(8,128)}, u32[]{:S(2)}) copy-start(f32[18,192,128]{2,1,0:T(8,128)} %copy-done.1) | copy-start | bytes 5308420
  42.7 1.0 copy-start.9
  43.7 13.8 %copy-start.3 = (f32[18,192,128]{2,1,0:T(8,128)S(1)}, f32[18,192,128]{2,1,0:T(8,128)}, u32[]{:S(2)}) copy-start(f32[18,192,128]{2,1,0:T(8,128)} %copy-done.1) | copy-start | bytes 5308420
  45.7 11.8 %collective-permute-start.5 = (f32[24,24,128]{2,1,0:T(8,128)S(1)}, f32[24,24,128]{2,1,0:T(8,128)S(1)}, u32[]{:S(2)}, u32[]{:S(2)}) collective-permute-start(f32[24,24,128]{2,1,0:T(8,128)S(1)} %get-tuple-element.23), channel_id=1, source_target_pairs={{0,1},{1,0},{2,3},{3,2},{4,5},{5,4},{6,7},{7,6},{8,9},{9,8},{10,11... | collective-permute-start | bytes 884744 | tf_op jit(solution)/shard_map/ppermute | solution.py:386
  46.0 11.5 %collective-permute-start.4 = (f32[24,16,128]{2,1,0:T(8,128)S(1)}, f32[24,16,128]{2,1,0:T(8,128)S(1)}, u32[]{:S(2)}, u32[]{:S(2)}) collective-permute-start(f32[24,16,128]{2,1,0:T(8,128)S(1)} %get-tuple-element.22), channel_id=1, source_target_pairs={{0,2},{1,3},{2,0},{3,1},{4,6},{5,7},{6,4},{7,5},{8,10},{9,11},{10,... | collective-permute-start | bytes 589832 | tf_op jit(solution)/shard_map/ppermute | solution.py:386
  48.5 24.5 %collective-permute-start.7 = (f32[6,192,128]{2,1,0:T(8,128)}, f32[6,192,128]{2,1,0:T(8,128)}, u32[]{:S(2)}, u32[]{:S(2)}) collective-permute-start(f32[6,192,128]{2,1,0:T(8,128)} %finish_first.1.refs_1_.refs_3_.refs_5_), channel_id=1, source_target_pairs={{0,4},{1,5},{2,6},{3,7},{4,8},{5,9},{6,10},{7,11},{8,12},{9,13},{1... | collective-permute-start | bytes 1769480 | tf_op jit(solution)/shard_map/ppermute | solution.py:382
  57.5 1.7 %copy-start.5 = (f32[1,24,192,128]{3,2,1,0:T(8,128)S(1)}, f32[1,24,192,128]{3,2,1,0:T(8,128)}, u32[]{:S(2)}) copy-start(f32[1,24,192,128]{3,2,1,0:T(8,128)} %param.9) | copy-start | bytes 7077892
  68.6 0.8 copy-start.11
  69.3 23.6 %copy-start.12 = (f32[18,48,128]{2,1,0:T(8,128)S(1)}, f32[18,48,128]{2,1,0:T(8,128)}, u32[]{:S(2)}) copy-start(f32[18,48,128]{2,1,0:T(8,128)} %copy-done.11) | copy-start | bytes 1327108
  69.3 14.2 %collective-permute-start.10 = (f32[18,48,128]{2,1,0:T(8,128)}, f32[18,48,128]{2,1,0:T(8,128)S(1)}, u32[]{:S(2)}, u32[]{:S(2)}) collective-permute-start(f32[18,48,128]{2,1,0:T(8,128)} %get-tuple-element.29), channel_id=1, source_target_pairs={{0,96},{32,64},{64,32},{96,0},{1,97},{33,65},{65,33},{97,1},{2,98}... | collective-permute-start | bytes 1327112 | tf_op jit(solution)/shard_map/ppermute | solution.py:386
  69.3 14.2 %collective-permute-start.8 = (f32[18,48,128]{2,1,0:T(8,128)}, f32[18,48,128]{2,1,0:T(8,128)S(1)}, u32[]{:S(2)}, u32[]{:S(2)}) collective-permute-start(f32[18,48,128]{2,1,0:T(8,128)} %get-tuple-element.27), channel_id=1, source_target_pairs={{0,32},{32,0},{64,96},{96,64},{1,33},{33,1},{65,97},{97,65},{2,34}... | collective-permute-start | bytes 1327112 | tf_op jit(solution)/shard_map/ppermute | solution.py:386
  72.4 20.5 %collective-permute-start.9 = (f32[18,48,128]{2,1,0:T(8,128)}, f32[18,48,128]{2,1,0:T(8,128)S(1)}, u32[]{:S(2)}, u32[]{:S(2)}) collective-permute-start(f32[18,48,128]{2,1,0:T(8,128)} %get-tuple-element.28), channel_id=1, source_target_pairs={{0,64},{32,96},{64,0},{96,32},{1,65},{33,97},{65,1},{97,33},{2,66}... | collective-permute-start | bytes 1327112 | tf_op jit(solution)/shard_map/ppermute | solution.py:386
  76.6 16.6 %collective-permute-start.11 = (f32[6,48,128]{2,1,0:T(8,128)}, f32[6,48,128]{2,1,0:T(8,128)S(1)}, u32[]{:S(2)}, u32[]{:S(2)}) collective-permute-start(f32[6,48,128]{2,1,0:T(8,128)} %get-tuple-element.31), channel_id=1, source_target_pairs={{0,32},{32,0},{64,96},{96,64},{1,33},{33,1},{65,97},{97,65},{2,34}... | collective-permute-start | bytes 442376 | tf_op jit(solution)/shard_map/ppermute | solution.py:386
  76.7 19.4 %collective-permute-start.12 = (f32[6,48,128]{2,1,0:T(8,128)}, f32[6,48,128]{2,1,0:T(8,128)S(1)}, u32[]{:S(2)}, u32[]{:S(2)}) collective-permute-start(f32[6,48,128]{2,1,0:T(8,128)} %get-tuple-element.32), channel_id=1, source_target_pairs={{0,64},{32,96},{64,0},{96,32},{1,65},{33,97},{65,1},{97,33},{2,66}... | collective-permute-start | bytes 442376 | tf_op jit(solution)/shard_map/ppermute | solution.py:386
  83.5 15.8 %collective-permute-start.13 = (f32[6,48,128]{2,1,0:T(8,128)}, f32[6,48,128]{2,1,0:T(8,128)S(1)}, u32[]{:S(2)}, u32[]{:S(2)}) collective-permute-start(f32[6,48,128]{2,1,0:T(8,128)} %get-tuple-element.33), channel_id=1, source_target_pairs={{0,96},{32,64},{64,32},{96,0},{1,97},{33,65},{65,33},{97,1},{2,98}... | collective-permute-start | bytes 442376 | tf_op jit(solution)/shard_map/ppermute | solution.py:386
  99.3 0.9 copy-start.13

commit v2 on v0

v2 whole, which is shorter than its diff:
```python
import functools
import math

import jax
import jax.numpy as jnp
import ml_dtypes
import numpy as np
from jax import lax
from jax.experimental import pallas as pl
from jax.experimental.pallas import tpu as pltpu
from jax.sharding import PartitionSpec as P

REACH = 6
ROWS = 24
LANES = 128
VMEM_LIMIT = 12 << 20
VMEM = pl.BlockSpec(memory_space=pltpu.VMEM)
SMEM = pl.BlockSpec(memory_space=pltpu.SMEM)
ANY = pl.BlockSpec(memory_space=pl.ANY)
HBM = pl.BlockSpec(memory_space=pltpu.HBM)
COST = pl.CostEstimate(flops=1, bytes_accessed=1, transcendentals=0)
SLOT = 16


def stencil_weights():
    weights = []
    for offset in range(1, 7):
        value = (
            2.0
            * (-1.0) ** (offset + 1)
            * math.factorial(6) ** 2
            / (offset * offset * math.factorial(6 - offset) * math.factorial(6 + offset))
        )
        weights.append(value)
    return [-2.0 * sum(weights)] + weights


WEIGHTS = stencil_weights()
CENTER = (-1.5 * WEIGHTS[0] - 9.0) / 7.0
SIDE = [0.0] + [-0.5 * w / 7.0 for w in WEIGHTS[1:]]


def side_weight(distance):
    distance = abs(distance)
    return SIDE[distance] if 1 <= distance <= REACH else 0.0


def z_matrix():
    whole = np.zeros((2 * LANES, LANES))
    for z in range(LANES):
        for other in range(max(0, z - REACH), min(LANES, z + REACH + 1)):
            whole[other, z] = side_weight(other - z)
        for c in range(2 * REACH):
            position = LANES + c if c < REACH else c - 2 * REACH
            whole[LANES + c, z] = side_weight(position - z)
    high = whole.astype(ml_dtypes.bfloat16)
    low = (whole - high.astype(np.float64)).astype(ml_dtypes.bfloat16)
    return np.concatenate([high, low], axis=1)


def selection(group):
    lane = lax.broadcasted_iota(jnp.int32, (LANES, LANES), 0)
    slot = lax.broadcasted_iota(jnp.int32, (LANES, LANES), 1) - SLOT * group
    low = (slot >= 0) & (slot < REACH) & (lane == slot)
    high = (slot >= REACH) & (slot < 2 * REACH) & (lane == slot + (LANES - 2 * REACH))
    chosen = jnp.where(low | high, 1.0, 0.0).astype(jnp.bfloat16)
    return jnp.concatenate([chosen, chosen], axis=0)


def split(values):
    high = values.astype(jnp.bfloat16)
    low = (values - high.astype(jnp.float32)).astype(jnp.bfloat16)
    return high, low


def pack_into(pieces, y_ref, z_ref):
    at = 0
    for piece in pieces:
        count, rows = piece.shape[0], piece.shape[1]
        for p in range(count):
            base = 2 * REACH * (at + p)
            y_ref[base : base + REACH, :] = piece[p, 0:REACH, :]
            y_ref[base + REACH : base + 2 * REACH, :] = piece[p, rows - REACH : rows, :]
        total = None
        for group in range(rows // ROWS):
            block = piece[:, group * ROWS : (group + 1) * ROWS, :].reshape(count * ROWS, LANES)
            high, low = split(block)
            part = jnp.dot(
                jnp.concatenate([high, low], axis=1),
                selection(group),
                preferred_element_type=jnp.float32,
            )
            total = part if total is None else total + part
        z_ref[at : at + count, :, :] = total.reshape(count, ROWS, LANES)
        at += count


def face_shapes(planes):
    return [
        jax.ShapeDtypeStruct((2 * REACH * planes, LANES), jnp.float32),
        jax.ShapeDtypeStruct((planes, ROWS, LANES), jnp.float32),
    ]


def pack_kernel(n, *refs):
    pack_into(refs[:n], refs[n], refs[n + 1])


def pack_faces(pieces):
    planes = sum(piece.shape[0] for piece in pieces)
    return pl.pallas_call(
        functools.partial(pack_kernel, len(pieces)),
        out_shape=face_shapes(planes),
        in_specs=[VMEM] * len(pieces),
        out_specs=[VMEM] * 2,
        compiler_params=pltpu.CompilerParams(vmem_limit_bytes=VMEM_LIMIT),
        cost_estimate=COST,
        name="pack_faces",
    )(*pieces)


def entry_kernel(source_ref, low_ref, y_ref, z_ref):
    low_ref[...] = source_ref[0:REACH]
    pack_into([source_ref], y_ref, z_ref)


def entry(source):
    outer = jax.ShapeDtypeStruct((REACH,) + source.shape[1:], jnp.float32)
    return pl.pallas_call(
        entry_kernel,
        out_shape=[outer] + face_shapes(source.shape[0]),
        in_specs=[VMEM],
        out_specs=[VMEM] * 3,
        compiler_params=pltpu.CompilerParams(vmem_limit_bytes=VMEM_LIMIT),
        cost_estimate=COST,
        name="entry",
    )(source)


def stencil_kernel(counts, sections, second, band_ref, *refs):
    n, m = len(counts), len(sections)
    pieces, y_refs, z_refs = refs[:n], refs[n : n + m], refs[n + m : n + 2 * m]
    potential_ref, weights_ref, halo_ref = refs[n + 2 * m : n + 2 * m + 3]
    rest = list(refs[n + 2 * m + 3 :])
    planes, rows = sum(counts), pieces[0].shape[1]
    source_ref = rest.pop(0) if second else None
    extended, gathered = rest[-2:]
    outputs = rest[:-2]
    face_of = [(y_refs[i], 2 * REACH * q) for i, size in enumerate(sections) for q in range(size)]

    def one_group(group, carry):
        start = pl.multiple_of(group * ROWS, 8)
        before = pl.ds(pl.multiple_of(jnp.maximum(start - 8, 0), 8), 8)
        after = pl.ds(pl.multiple_of(jnp.minimum(start + ROWS, rows - 8), 8), 8)
        at = 0
        for piece, count in zip(pieces, counts):
            here = slice(at, at + count)
            extended[here, 8 : 8 + ROWS, :] = piece[:, pl.ds(start, ROWS), :]
            extended[here, 0:8, :] = piece[:, before, :]
            extended[here, 8 + ROWS : 16 + ROWS, :] = piece[:, after, :]
            at += count

        @pl.when(group == 0)
        def _():
            for p, (face, base) in enumerate(face_of):
                extended[p, 8 - REACH : 8, :] = face[base + REACH : base + 2 * REACH, :]

        @pl.when(group == rows // ROWS - 1)
        def _():
            for p, (face, base) in enumerate(face_of):
                extended[p, 8 + ROWS : 8 + ROWS + REACH, :] = face[base : base + REACH, :]

        own_high, own_low = split(extended[:, 8 : 8 + ROWS, :].reshape(planes * ROWS, LANES))
        packed = jnp.concatenate([z[...] for z in z_refs], axis=0).reshape(planes * ROWS, LANES)
        face_high, face_low = split(pltpu.roll(packed, (LANES - SLOT * group) % LANES, 1))
        both_high = jnp.concatenate([own_high, face_high], axis=1)
        both_low = jnp.concatenate([own_low, face_low], axis=1)
        weights = weights_ref[...]
        along_z = jnp.dot(both_high, weights, preferred_element_type=jnp.float32)
        along_z = along_z[:, :LANES] + along_z[:, LANES:]
        along_z += jnp.dot(both_low, weights[:, :LANES], preferred_element_type=jnp.float32)
        gathered[...] = along_z.reshape(planes, ROWS, LANES)
        for tile in range(ROWS // 8):
            top = 8 + 8 * tile
            within = slice(8 * tile, 8 * tile + 8)
            there = pl.ds(pl.multiple_of(start + 8 * tile, 8), 8)
            own = [extended[p, top : top + 8, :] for p in range(planes)]
            for p in range(planes):
                total = gathered[p, within, :]
                total += (CENTER + potential_ref[p, there, :] * (1.0 / 7.0)) * own[p]
                for k in range(1, REACH + 1):
                    beside = extended[p, top + k : top + k + 8, :] + extended[p, top - k : top - k + 8, :]
                    if p - k >= 0:
                        beside = beside + own[p - k]
                    elif not second:
                        beside = beside + halo_ref[REACH + p - k, there, :]
                    if p + k < planes:
                        beside = beside + own[p + k]
                    elif second:
                        beside = beside + halo_ref[p + k - planes, there, :]
                    total = total + SIDE[k] * beside
                if second:
                    total = 2.0 * total - source_ref[p, there, :]
                    if p < REACH:
                        outputs[5][p, there, :] = total
                    else:
                        outputs[0][p, there, :] = total
                else:
                    at = 0
                    for target in outputs:
                        if at <= p < at + target.shape[0]:
                            target[p - at, there, :] = total
                        at += target.shape[0]
        return carry

    lax.fori_loop(0, rows // ROWS, one_group, 0)
    if second:
        part = rows // 4
        for slot in range(4):
            there = pl.ds(pl.multiple_of((band_ref[0] ^ slot) * part, 8), part)
            outputs[1 + slot][...] = outputs[0][REACH:planes, there, :]


def apply_stencil(pieces, faces, potential, halo, band, source=None):
    second = source is not None
    counts = [piece.shape[0] for piece in pieces]
    planes, rows = sum(counts), pieces[0].shape[1]
    sections = [z.shape[0] for _, z in faces]
    operands = list(pieces) + [y for y, _ in faces] + [z for _, z in faces]
    operands += [potential, jnp.asarray(z_matrix()), halo]
    if second:
        operands.append(source)
        shapes = [(planes, rows, LANES)] + [(planes - REACH, rows // 4, LANES)] * 4
        shapes.append((REACH, rows, LANES))
    else:
        shapes = [(REACH, rows, LANES), (planes - 2 * REACH, rows, LANES), (REACH, rows, LANES)]
    return pl.pallas_call(
        functools.partial(stencil_kernel, counts, sections, second),
        out_shape=[jax.ShapeDtypeStruct(shape, jnp.float32) for shape in shapes],
        in_specs=[SMEM] + [VMEM] * len(operands),
        out_specs=[VMEM] * len(shapes),
        scratch_shapes=[
            pltpu.VMEM((planes, ROWS + 16, LANES), jnp.float32),
            pltpu.VMEM((planes, ROWS, LANES), jnp.float32),
        ],
        compiler_params=pltpu.CompilerParams(vmem_limit_bytes=VMEM_LIMIT),
        cost_estimate=COST,
        name="second_step" if second else "first_step",
    )(band, *operands)


def add_halo(out_ref, partial_ref, halo_ref, high_side, factor):
    rows = halo_ref.shape[1]

    def body(tile, carry):
        there = pl.ds(pl.multiple_of(tile * 8, 8), 8)
        halo = [halo_ref[m, there, :] for m in range(REACH)]
        for j in range(REACH):
            total = partial_ref[j, there, :]
            for k in range(1, REACH + 1):
                m = j + k - REACH if high_side else REACH + j - k
                if 0 <= m < REACH:
                    total = total + (factor * SIDE[k]) * halo[m]
            out_ref[j, there, :] = total
        return carry

    lax.fori_loop(0, rows // 8, body, 0)


def finish_first_kernel(partial_ref, halo_ref, out_ref, y_ref, z_ref):
    add_halo(out_ref, partial_ref, halo_ref, True, 1.0)
    pack_into([out_ref], y_ref, z_ref)


def finish_first(partial, halo):
    planes = partial.shape[0]
    return pl.pallas_call(
        finish_first_kernel,
        out_shape=[jax.ShapeDtypeStruct(partial.shape, jnp.float32)] + face_shapes(planes),
        in_specs=[VMEM] * 2,
        out_specs=[VMEM] * 3,
        compiler_params=pltpu.CompilerParams(vmem_limit_bytes=VMEM_LIMIT),
        cost_estimate=COST,
        name="finish_first",
    )(partial, halo)


def finish_filtered_kernel(band_ref, partial_ref, halo_ref, whole_ref, out_ref, *rest):
    slots, done, semaphore = rest[:4], rest[4], rest[5]
    add_halo(done, partial_ref, halo_ref, False, 2.0)
    copy = pltpu.make_async_copy(done, out_ref.at[0:REACH], semaphore)
    copy.start()
    part = slots[0].shape[1]
    for slot in range(4):
        there = pl.ds(pl.multiple_of((band_ref[0] ^ slot) * part, 8), part)
        slots[slot][...] = done[:, there, :]
    copy.wait()


def finish_filtered(partial, halo, whole, band):
    part = jax.ShapeDtypeStruct((REACH, partial.shape[1] // 4, LANES), jnp.float32)
    return pl.pallas_call(
        finish_filtered_kernel,
        out_shape=[jax.ShapeDtypeStruct(whole.shape, jnp.float32)] + [part] * 4,
        in_specs=[SMEM, VMEM, VMEM, ANY],
        out_specs=[ANY] + [VMEM] * 4,
        input_output_aliases={3: 0},
        scratch_shapes=[pltpu.VMEM(partial.shape, jnp.float32), pltpu.SemaphoreType.DMA(())],
        compiler_params=pltpu.CompilerParams(vmem_limit_bytes=VMEM_LIMIT),
        cost_estimate=COST,
        name="finish_filtered",
    )(band, partial, halo, whole)


PAIRS = [(i, j) for i in range(4) for j in range(i, 4)]


def add_products(refs, totals):
    planes, rows = refs[0].shape[0], refs[0].shape[1]

    def body(p, carried):
        carried = list(carried)
        for tile in range(rows // 8):
            values = [ref[p, 8 * tile : 8 * tile + 8, :] for ref in refs]
            for n, (i, j) in enumerate(PAIRS):
                carried[n] = carried[n] + values[i] * values[j]
        return tuple(carried)

    return lax.fori_loop(0, planes, body, tuple(totals))


def early_gram_kernel(*refs):
    out_ref = refs[-1]
    totals = add_products(refs[:4], [jnp.zeros((8, LANES), jnp.float32)] * len(PAIRS))
    for n in range(len(PAIRS)):
        out_ref[n] = totals[n]


def early_gram(parts):
    return pl.pallas_call(
        early_gram_kernel,
        out_shape=jax.ShapeDtypeStruct((len(PAIRS), 8, LANES), jnp.float32),
        in_specs=[VMEM] * 4,
        out_specs=VMEM,
        compiler_params=pltpu.CompilerParams(vmem_limit_bytes=VMEM_LIMIT),
        cost_estimate=COST,
        name="early_gram",
    )(*parts)


def late_gram_kernel(band_ref, before_ref, *refs):
    out_ref = refs[-1]
    totals = add_products(refs[:4], [before_ref[n] for n in range(len(PAIRS))])
    band = band_ref[0]
    lane = lax.broadcasted_iota(jnp.int32, (1, LANES), 1)
    row = jnp.zeros((1, LANES), jnp.float32)
    for n, (i, j) in enumerate(PAIRS):
        value = jnp.sum(totals[n])
        first, other = band ^ i, band ^ j
        hit = (lane == 4 * first + other) | (lane == 4 * other + first)
        row = row + jnp.where(hit, value, 0.0)
    out_ref[...] = jnp.broadcast_to(row, out_ref.shape)


def late_gram(before, parts, band, peers):
    return pl.pallas_call(
        late_gram_kernel,
        out_shape=jax.ShapeDtypeStruct((peers, LANES), jnp.float32),
        in_specs=[SMEM] + [VMEM] * 5,
        out_specs=VMEM,
        compiler_params=pltpu.CompilerParams(vmem_limit_bytes=VMEM_LIMIT),
        cost_estimate=COST,
        name="late_gram",
    )(band, before, *parts)


def total_kernel(scale, rows_ref, out_ref):
    row = jnp.sum(rows_ref[...], axis=0, keepdims=True) * scale
    for i in range(4):
        out_ref[i : i + 1, :] = row[:, 4 * i : 4 * i + 4]


def total_gram(rows, cell_count):
    return pl.pallas_call(
        functools.partial(total_kernel, 1.0 / cell_count),
        out_shape=jax.ShapeDtypeStruct((4, 4), jnp.float32),
        in_specs=[VMEM],
        out_specs=VMEM,
        cost_estimate=COST,
        name="total_gram",
    )(rows)


def shifted(array, by):
    peers = lax.axis_size("space")
    return lax.ppermute(array, "space", [(i, (i + by) % peers) for i in range(peers)])


def swapped(array, axis, bit):
    return lax.ppermute(array, axis, [(i, i ^ bit) for i in range(lax.axis_size(axis))])


def swapped_faces(faces):
    y_faces, z_faces = faces
    return swapped(y_faces, "space", 2), swapped(z_faces, "space", 1)


def band_exchange(slots):
    moved = {k: swapped(slots[k], "band", k) for k in (3, 2, 1)}
    return [slots[0], moved[1], moved[2], moved[3]]


def on_device(orbitals, potential):
    source, local_potential = orbitals[0, 0], potential[0]
    band = lax.axis_index("band").astype(jnp.int32).reshape(1)
    below = shifted(source[source.shape[0] - REACH :], 4)
    low_planes, *faces = entry(source)
    faces = swapped_faces(faces)
    above = shifted(low_planes, -4)
    low, middle, top = apply_stencil([source], [faces], local_potential, below, band)
    above_first = shifted(low, -4)
    main_faces = swapped_faces(pack_faces([low, middle]))
    top, *top_faces = finish_first(top, above)
    below_first = shifted(top, 4)
    top_faces = swapped_faces(top_faces)
    filtered, *slots, low_filtered = apply_stencil(
        [low, middle, top], [main_faces, top_faces], local_potential, above_first, band, source
    )
    early = early_gram(band_exchange(slots))
    filtered, *slots = finish_filtered(low_filtered, below_first, filtered, band)
    both = ("band", "space")
    rows = late_gram(early, band_exchange(slots), band, lax.axis_size(both))
    everyone = lax.all_to_all(rows, both, 0, 0, tiled=True)
    correlation = total_gram(everyone, filtered.size * lax.axis_size("space"))
    return filtered[None, None], correlation


def solution(mesh):
    placed = (P("band", "space", None, None, None), P("space", None, None, None))
    return jax.shard_map(
        on_device,
        mesh=mesh,
        in_specs=placed,
        out_specs=(P("band", "space", None, None, None), P()),
        check_vma=False,
    )
```

time: 373 us -> 106 us (0.28)
  other arithmetic: 84.2 us -> 0 us
  blocking collectives: 81.9 us -> 17.4 us
  matrix products: 58.2 us -> 0 us
  waiting for transfers between devices: 84.5 us -> 36.8 us
  local copies, waits for them, and re-layouts: 36.4 us -> 6.2 us
  Pallas kernels: 0 us -> 19.3 us
  between operations: 14.1 us -> 0.73 us
  starting transfers between devices: 13.2 us -> 24.5 us
    psum x1 -> x0, blocking collectives: 81.9 us -> none  [on_device(): summed_gram = lax.psum(partial_gram, 'space')]
    all_gather x1 -> x0, waiting for transfers between devices: 69.1 us -> none  [on_device(): gathered = lax.all_gather(filtered, 'band', axis=0, tiled=True)]
    sub x1 -> x0, other arithmetic: 60.9 us -> none  [on_device(): 2.0 * (kinetic(first_step) + local_potential * first_step - 9.0 * first_s...]
    dot_general x1 -> x0, matrix products: 58.2 us -> none  [on_device(): jnp.dot(flat_rows, flat_rows.T, precision=lax.Precision.HIGHEST, preferre...]
    slice x18 -> x1, local copies, waits for them, and re-layouts: 36.4 us -> 1.95 us  [on_device(): below = shifted(source[source.shape[0] - REACH:], 4)]
    div x2 -> x0, other arithmetic: 21.5 us -> none  [the longest x1 20.9 us: on_device(): (kinetic(source) + local_potential * source - 9.0 * source) / 7.0]
    ppermute x8 -> x16, waiting for transfers between devices: 15.4 us -> 36.8 us  [the longest x12 34 us: swapped(): lax.ppermute(array, axis, [(i, i ^ bit) for i in range(lax.axis_size(axis...]
    pallas_call x0 -> x9, Pallas kernels: none -> 19.3 us  [the longest x2 13.1 us: apply_stencil(): pl.pallas_call(functools.partial(stencil_kernel, counts, sections, second...]
  transfers between devices with their start and end apart: 9 -> 16, of which waited for: 4 -> 9; matrix products, arithmetic and copies ran while one was open for 9% -> 0% of each run, Pallas kernels for 0% -> 17%
where the time goes in v2:
time: 106 us; the launch traced here: 105 us
  waiting for transfers between devices  36.8 us (35%)
  starting transfers between devices  24.5 us (23%)
  Pallas kernels  19.3 us (18%)
  blocking collectives  17.4 us (16%)
  local copies, waits for them, and re-layouts  6.2 us (6%)
    ppermute x12, waiting for transfers between devices, swapped(): lax.ppermute(array, axis, [(i, i ^ bit) for i in range(lax.axis_size(axis...  34 us
    all_to_all x1, blocking collectives, on_device(): everyone = lax.all_to_all(rows, both, 0, 0, tiled=True)  17.4 us
    ppermute x12, starting transfers between devices, swapped(): lax.ppermute(array, axis, [(i, i ^ bit) for i in range(lax.axis_size(axis...  15.8 us
    pallas_call x2, Pallas kernels, apply_stencil(): pl.pallas_call(functools.partial(stencil_kernel, counts, sections, second...  13.1 us
    ppermute x4, starting transfers between devices, shifted(): lax.ppermute(array, 'space', [(i, (i + by) % peers) for i in range(peers)])  8.71 us
    unnamed x12, local copies, waits for them, and re-layouts  4.25 us
    ppermute x4, waiting for transfers between devices, shifted(): lax.ppermute(array, 'space', [(i, (i + by) % peers) for i in range(peers)])  2.8 us
  transfers between devices with their start and end apart: 16, of which 9 were waited for; matrix products, arithmetic and copies ran while one was open for 0% of the time, Pallas kernels for 17%

profile of v2, /device:TPU:0, one launch (start us, length us, event | category | flops | bytes accessed | tf_op | source)
XLA Modules:
  0.0 104.9 jit_solution(7784675899394408580)
XLA Ops:
  0.6 2.0 %slice_bitcast_fusion = f32[6,192,128]{2,1,0:T(8,128)} fusion(f32[1,1,24,192,128]{4,3,2,1,0:T(8,128)} %param.4), kind=kLoop, calls=%fused_computation | loop fusion | bytes 1179648 | tf_op jit(solution)/shard_map/slice | solution.py:416
  2.6 1.7 %collective-permute-start.2 = (f32[6,192,128]{2,1,0:T(8,128)}, f32[6,192,128]{2,1,0:T(8,128)S(1)}, u32[]{:S(2)}, u32[]{:S(2)}) collective-permute-start(f32[6,192,128]{2,1,0:T(8,128)} %slice_bitcast_fusion), channel_id=1, source_target_pairs={{0,4},{1,5},{2,6},{3,7},{4,8},{5,9},{6,10},{7,11},{8,12},{9,13},{1... | collective-permute-start | bytes 1769480 | tf_op jit(solution)/shard_map/ppermute | solution.py:396
  4.2 0.0 copy-start
  4.2 1.7 %copy-done = f32[1,1,24,192,128]{4,3,2,1,0:T(8,128)S(1)} copy-done((f32[1,1,24,192,128]{4,3,2,1,0:T(8,128)S(1)}, f32[1,1,24,192,128]{4,3,2,1,0:T(8,128)}, u32[]{:S(2)}) %copy-start) | copy-done | bytes 2359320
  5.9 0.0 copy-start.1
  5.9 1.7 %entry.1 = (f32[6,192,128]{2,1,0:T(8,128)}, f32[288,128]{1,0:T(8,128)}, f32[24,24,128]{2,1,0:T(8,128)}) custom-call(f32[24,192,128]{2,1,0:T(8,128)S(1)} %bitcast.10), custom_call_target="tpu_custom_call" | custom-call | flops 1 | bytes 1 | tf_op jit(solution)/shard_map/entry/pallas_call | solution.py:129
  7.6 1.5 %collective-permute-start.1 = (f32[24,24,128]{2,1,0:T(8,128)}, f32[24,24,128]{2,1,0:T(8,128)}, u32[]{:S(2)}, u32[]{:S(2)}) collective-permute-start(f32[24,24,128]{2,1,0:T(8,128)} %get-tuple-element.25), channel_id=1, source_target_pairs={{0,1},{1,0},{2,3},{3,2},{4,5},{5,4},{6,7},{7,6},{8,9},{9,8},{10,11... | collective-permute-start | bytes 884744 | tf_op jit(solution)/shard_map/ppermute | solution.py:400
  9.1 2.7 %collective-permute-start = (f32[288,128]{1,0:T(8,128)}, f32[288,128]{1,0:T(8,128)}, u32[]{:S(2)}, u32[]{:S(2)}) collective-permute-start(f32[288,128]{1,0:T(8,128)} %get-tuple-element.24), channel_id=1, source_target_pairs={{0,2},{1,3},{2,0},{3,1},{4,6},{5,7},{6,4},{7,5},{8,10},{9,11},{10,... | collective-permute-start | bytes 442376 | tf_op jit(solution)/shard_map/ppermute | solution.py:400
  11.8 3.5 %collective-permute-start.3 = (f32[6,192,128]{2,1,0:T(8,128)}, f32[6,192,128]{2,1,0:T(8,128)S(1)}, u32[]{:S(2)}, u32[]{:S(2)}) collective-permute-start(f32[6,192,128]{2,1,0:T(8,128)} %get-tuple-element.29), channel_id=1, source_target_pairs={{0,28},{1,29},{2,30},{3,31},{4,0},{5,1},{6,2},{7,3},{8,4},{9,5},{1... | collective-permute-start | bytes 1769480 | tf_op jit(solution)/shard_map/ppermute | solution.py:396
  15.3 6.4 %collective-permute-done.refs_1_ = f32[288,128]{1,0:T(8,128)} collective-permute-done((f32[288,128]{1,0:T(8,128)}, f32[288,128]{1,0:T(8,128)}, u32[]{:S(2)}, u32[]{:S(2)}) %collective-permute-start) | collective-permute-done | bytes 147488 | tf_op jit(solution)/shard_map/ppermute | solution.py:400
  21.7 0.0 collective-permute-done.1.refs_2_
  21.7 0.3 collective-permute-done.2.refs_5_
  22.1 0.0 copy-done.1
  22.1 0.0 copy-start.2
  22.1 1.7 %copy-done.2 = f32[1,24,192,128]{3,2,1,0:T(8,128)S(1)} copy-done((f32[1,24,192,128]{3,2,1,0:T(8,128)S(1)}, f32[1,24,192,128]{3,2,1,0:T(8,128)}, u32[]{:S(2)}) %copy-start.2) | copy-done | bytes 2359320
  23.7 0.0 copy-start.4
  23.8 0.9 copy-done.4
  24.7 6.1 %first_step.1 = (f32[6,192,128]{2,1,0:T(8,128)S(1)}, f32[12,192,128]{2,1,0:T(8,128)S(1)}, f32[6,192,128]{2,1,0:T(8,128)S(1)}) custom-call(s32[1]{0:T(128)} %bitcast.band_ref, f32[24,192,128]{2,1,0:T(8,128)S(1)} %bitcast.11, f32[288,128]{1,0:T(8,128)} %collective-permute-done.refs_1_, f32[24,24,128]{2,1,0:T(8,128)} %collective-permute-done.1.refs_2_, ...), custom_call_target="tpu_custom_call" | custom-call | flops 1 | bytes 1 | tf_op jit(solution)/shard_map/first_step/pallas_call | solution.py:237
  30.8 0.0 copy-start.3
  30.8 0.0 copy-start.5
  30.8 3.5 %collective-permute-start.8 = (f32[6,192,128]{2,1,0:T(8,128)S(1)}, f32[6,192,128]{2,1,0:T(8,128)S(1)}, u32[]{:S(2)}, u32[]{:S(2)}) collective-permute-start(f32[6,192,128]{2,1,0:T(8,128)S(1)} %get-tuple-element.26.refs_0_), channel_id=1, source_target_pairs={{0,28},{1,29},{2,30},{3,31},{4,0},{5,1},{6,2},{7,3},{8,4},{9,5},{1... | collective-permute-start | bytes 1769480 | tf_op jit(solution)/shard_map/ppermute | solution.py:396
  34.3 0.6 pack_faces.1
  34.9 0.3 collective-permute-start.6
  35.2 0.0 collective-permute-done.3.halo_ref
  35.2 0.6 finish_first.1
  35.8 0.1 collective-permute-start.9
  35.9 2.7 %collective-permute-start.5 = (f32[72,128]{1,0:T(8,128)S(1)}, f32[72,128]{1,0:T(8,128)S(1)}, u32[]{:S(2)}, u32[]{:S(2)}) collective-permute-start(f32[72,128]{1,0:T(8,128)S(1)} %get-tuple-element.32), channel_id=1, source_target_pairs={{0,2},{1,3},{2,0},{3,1},{4,6},{5,7},{6,4},{7,5},{8,10},{9,11},{10,... | collective-permute-start | bytes 110600 | tf_op jit(solution)/shard_map/ppermute | solution.py:400
  38.6 0.9 collective-permute-start.4
  39.5 3.8 %collective-permute-done.5.refs_4_ = f32[72,128]{1,0:T(8,128)S(1)} collective-permute-done((f32[72,128]{1,0:T(8,128)S(1)}, f32[72,128]{1,0:T(8,128)S(1)}, u32[]{:S(2)}, u32[]{:S(2)}) %collective-permute-start.5) | collective-permute-done | bytes 36896 | tf_op jit(solution)/shard_map/ppermute | solution.py:400
  43.3 0.8 collective-permute-start.7
  44.2 3.5 %collective-permute-done.7.refs_6_ = f32[6,24,128]{2,1,0:T(8,128)S(1)} collective-permute-done((f32[6,24,128]{2,1,0:T(8,128)S(1)}, f32[6,24,128]{2,1,0:T(8,128)S(1)}, u32[]{:S(2)}, u32[]{:S(2)}) %collective-permute-start.7) | collective-permute-done | bytes 73760 | tf_op jit(solution)/shard_map/ppermute | solution.py:400
  47.7 0.0 collective-permute-done.4.refs_3_
  47.7 0.0 collective-permute-done.6.refs_5_
  47.7 0.4 collective-permute-done.8.refs_9_
  48.1 0.0 copy-done.3
  48.1 0.0 copy-done.5
  48.1 7.0 %second_step.1 = (f32[24,192,128]{2,1,0:T(8,128)}, f32[18,48,128]{2,1,0:T(8,128)S(1)}, f32[18,48,128]{2,1,0:T(8,128)S(1)}, f32[18,48,128]{2,1,0:T(8,128)S(1)}, f...) custom-call(s32[1]{0:T(128)} %bitcast.band_ref, f32[6,192,128]{2,1,0:T(8,128)S(1)} %get-tuple-element.26.refs_0_, ...), custom_call_target="tpu_custom_call" | custom-call | flops 1 | bytes 1 | tf_op jit(solution)/shard_map/second_step/pallas_call | solution.py:237
  55.1 0.0 collective-permute-start.10
  55.1 2.9 %collective-permute-start.11 = (f32[18,48,128]{2,1,0:T(8,128)S(1)}, f32[18,48,128]{2,1,0:T(8,128)S(1)}, u32[]{:S(2)}, u32[]{:S(2)}) collective-permute-start(f32[18,48,128]{2,1,0:T(8,128)S(1)} %get-tuple-element.40), channel_id=1, source_target_pairs={{0,64},{32,96},{64,0},{96,32},{1,65},{33,97},{65,1},{97,33},{2,66}... | collective-permute-start | bytes 1327112 | tf_op jit(solution)/shard_map/ppermute | solution.py:400
  58.0 0.5 collective-permute-start.12
  58.5 2.1 %collective-permute-done.9.halo_ref = f32[6,192,128]{2,1,0:T(8,128)S(1)} collective-permute-done((f32[6,192,128]{2,1,0:T(8,128)S(1)}, f32[6,192,128]{2,1,0:T(8,128)S(1)}, u32[]{:S(2)}, u32[]{:S(2)}) %collective-permute-start.9) | collective-permute-done | bytes 589856 | tf_op jit(solution)/shard_map/ppermute | solution.py:396
  60.5 1.1 %finish_filtered.1 = (f32[24,192,128]{2,1,0:T(8,128)}, f32[6,48,128]{2,1,0:T(8,128)S(1)}, f32[6,48,128]{2,1,0:T(8,128)S(1)}, f32[6,48,128]{2,1,0:T(8,128)S(1)}, f32[6,48,128]{2,1,0:T(8,128)S(1)}) custom-call(s32[1]{0:T(128)} %bitcast.band_ref, f32[6,192,128]{2,1,0:T(8,128)S(1)} %get-tuple-element.35.partial_ref, ...), custom_call_target="tpu_custom_call", output_to_operand_aliasing={{0}: (3, {})} | custom-call | flops 1 | bytes 1 | tf_op jit(solution)/shard_map/finish_filtered/pallas_call | solution.py:302
  61.7 0.1 collective-permute-start.13
  61.8 3.2 %collective-permute-start.14 = (f32[6,48,128]{2,1,0:T(8,128)S(1)}, f32[6,48,128]{2,1,0:T(8,128)S(1)}, u32[]{:S(2)}, u32[]{:S(2)}) collective-permute-start(f32[6,48,128]{2,1,0:T(8,128)S(1)} %get-tuple-element.44), channel_id=1, source_target_pairs={{0,64},{32,96},{64,0},{96,32},{1,65},{33,97},{65,1},{97,33},{2,66}... | collective-permute-start | bytes 442376 | tf_op jit(solution)/shard_map/ppermute | solution.py:400
  64.9 0.0 collective-permute-done.10.refs_1_
  64.9 0.2 collective-permute-start.15
  65.1 8.4 %collective-permute-done.11.refs_2_ = f32[18,48,128]{2,1,0:T(8,128)S(1)} collective-permute-done((f32[18,48,128]{2,1,0:T(8,128)S(1)}, f32[18,48,128]{2,1,0:T(8,128)S(1)}, u32[]{:S(2)}, u32[]{:S(2)}) %collective-permute-start.11) | collective-permute-done | bytes 442400 | tf_op jit(solution)/shard_map/ppermute | solution.py:400
  73.6 5.3 %collective-permute-done.12.refs_3_ = f32[18,48,128]{2,1,0:T(8,128)S(1)} collective-permute-done((f32[18,48,128]{2,1,0:T(8,128)S(1)}, f32[18,48,128]{2,1,0:T(8,128)S(1)}, u32[]{:S(2)}, u32[]{:S(2)}) %collective-permute-start.12) | collective-permute-done | bytes 442400 | tf_op jit(solution)/shard_map/ppermute | solution.py:400
  78.9 0.4 early_gram.1.before_ref
  79.3 0.0 collective-permute-done.13.refs_1_
  79.3 6.4 %collective-permute-done.14.refs_2_ = f32[6,48,128]{2,1,0:T(8,128)S(1)} collective-permute-done((f32[6,48,128]{2,1,0:T(8,128)S(1)}, f32[6,48,128]{2,1,0:T(8,128)S(1)}, u32[]{:S(2)}, u32[]{:S(2)}) %collective-permute-start.14) | collective-permute-done | bytes 147488 | tf_op jit(solution)/shard_map/ppermute | solution.py:400
  85.7 0.0 collective-permute-done.15.refs_3_
  85.7 0.2 late_gram.1
  86.0 17.4 %all_to_all.11 = f32[128,1,128]{2,1,0:T(1,128)} all-to-all(f32[128,1,128]{2,1,0:T(1,128)S(1)} %bitcast.15), channel_id=1, replica_groups=mesh['band'=4,'space'=32] {'band','space'}, dimensions={0} | all-to-all | bytes 131072 | tf_op jit(solution)/shard_map/all_to_all | solution.py:433
  103.4 1.5 %total_gram.1 = f32[4,4]{1,0:T(4,128)} custom-call(f32[128,128]{1,0:T(8,128)} %bitcast.17), custom_call_target="tpu_custom_call" | custom-call | flops 1 | bytes 1 | tf_op jit(solution)/shard_map/total_gram/pallas_call | solution.py:384
Async XLA Ops:
  2.6 19.5 %collective-permute-start.2 = (f32[6,192,128]{2,1,0:T(8,128)}, f32[6,192,128]{2,1,0:T(8,128)S(1)}, u32[]{:S(2)}, u32[]{:S(2)}) collective-permute-start(f32[6,192,128]{2,1,0:T(8,128)} %slice_bitcast_fusion), channel_id=1, source_target_pairs={{0,4},{1,5},{2,6},{3,7},{4,8},{5,9},{6,10},{7,11},{8,12},{9,13},{1... | collective-permute-start | bytes 1769480 | tf_op jit(solution)/shard_map/ppermute | solution.py:396
  4.2 1.7 %copy-start = (f32[1,1,24,192,128]{4,3,2,1,0:T(8,128)S(1)}, f32[1,1,24,192,128]{4,3,2,1,0:T(8,128)}, u32[]{:S(2)}) copy-start(f32[1,1,24,192,128]{4,3,2,1,0:T(8,128)} %param.4) | copy-start | bytes 7077892
  5.9 16.2 %copy-start.1 = (f32[1,1,24,192,128]{4,3,2,1,0:T(8,128)S(1)}, f32[1,1,24,192,128]{4,3,2,1,0:T(8,128)}, u32[]{:S(2)}) copy-start(f32[1,1,24,192,128]{4,3,2,1,0:T(8,128)} %param.4) | copy-start | bytes 7077892
  7.6 14.1 %collective-permute-start.1 = (f32[24,24,128]{2,1,0:T(8,128)}, f32[24,24,128]{2,1,0:T(8,128)}, u32[]{:S(2)}, u32[]{:S(2)}) collective-permute-start(f32[24,24,128]{2,1,0:T(8,128)} %get-tuple-element.25), channel_id=1, source_target_pairs={{0,1},{1,0},{2,3},{3,2},{4,5},{5,4},{6,7},{7,6},{8,9},{9,8},{10,11... | collective-permute-start | bytes 884744 | tf_op jit(solution)/shard_map/ppermute | solution.py:400
  9.1 12.6 %collective-permute-start = (f32[288,128]{1,0:T(8,128)}, f32[288,128]{1,0:T(8,128)}, u32[]{:S(2)}, u32[]{:S(2)}) collective-permute-start(f32[288,128]{1,0:T(8,128)} %get-tuple-element.24), channel_id=1, source_target_pairs={{0,2},{1,3},{2,0},{3,1},{4,6},{5,7},{6,4},{7,5},{8,10},{9,11},{10,... | collective-permute-start | bytes 442376 | tf_op jit(solution)/shard_map/ppermute | solution.py:400
  11.8 23.4 %collective-permute-start.3 = (f32[6,192,128]{2,1,0:T(8,128)}, f32[6,192,128]{2,1,0:T(8,128)S(1)}, u32[]{:S(2)}, u32[]{:S(2)}) collective-permute-start(f32[6,192,128]{2,1,0:T(8,128)} %get-tuple-element.29), channel_id=1, source_target_pairs={{0,28},{1,29},{2,30},{3,31},{4,0},{5,1},{6,2},{7,3},{8,4},{9,5},{1... | collective-permute-start | bytes 1769480 | tf_op jit(solution)/shard_map/ppermute | solution.py:396
  22.1 1.7 %copy-start.2 = (f32[1,24,192,128]{3,2,1,0:T(8,128)S(1)}, f32[1,24,192,128]{3,2,1,0:T(8,128)}, u32[]{:S(2)}) copy-start(f32[1,24,192,128]{3,2,1,0:T(8,128)} %param.5) | copy-start | bytes 7077892
  23.7 0.9 copy-start.4
  30.8 17.3 %copy-start.3 = (f32[1,24,192,128]{3,2,1,0:T(8,128)S(1)}, f32[1,24,192,128]{3,2,1,0:T(8,128)}, u32[]{:S(2)}) copy-start(f32[1,24,192,128]{3,2,1,0:T(8,128)} %param.5) | copy-start | bytes 7077892
  30.8 17.3 %copy-start.5 = (bf16[256,256]{1,0:T(8,128)(2,1)S(1)}, bf16[256,256]{1,0:T(8,128)(2,1)}, u32[]{:S(2)}) copy-start(bf16[256,256]{1,0:T(8,128)(2,1)} %constant.8.clone.refs_4_.refs_8_) | copy-start | bytes 393220
  30.8 17.3 %collective-permute-start.8 = (f32[6,192,128]{2,1,0:T(8,128)S(1)}, f32[6,192,128]{2,1,0:T(8,128)S(1)}, u32[]{:S(2)}, u32[]{:S(2)}) collective-permute-start(f32[6,192,128]{2,1,0:T(8,128)S(1)} %get-tuple-element.26.refs_0_), channel_id=1, source_target_pairs={{0,28},{1,29},{2,30},{3,31},{4,0},{5,1},{6,2},{7,3},{8,4},{9,5},{1... | collective-permute-start | bytes 1769480 | tf_op jit(solution)/shard_map/ppermute | solution.py:396
  34.9 12.8 %collective-permute-start.6 = (f32[18,24,128]{2,1,0:T(8,128)S(1)}, f32[18,24,128]{2,1,0:T(8,128)S(1)}, u32[]{:S(2)}, u32[]{:S(2)}) collective-permute-start(f32[18,24,128]{2,1,0:T(8,128)S(1)} %get-tuple-element.33), channel_id=1, source_target_pairs={{0,1},{1,0},{2,3},{3,2},{4,5},{5,4},{6,7},{7,6},{8,9},{9,8},{10,11... | collective-permute-start | bytes 663560 | tf_op jit(solution)/shard_map/ppermute | solution.py:400
  35.8 24.7 %collective-permute-start.9 = (f32[6,192,128]{2,1,0:T(8,128)S(1)}, f32[6,192,128]{2,1,0:T(8,128)S(1)}, u32[]{:S(2)}, u32[]{:S(2)}) collective-permute-start(f32[6,192,128]{2,1,0:T(8,128)S(1)} %get-tuple-element.30.refs_2_), channel_id=1, source_target_pairs={{0,4},{1,5},{2,6},{3,7},{4,8},{5,9},{6,10},{7,11},{8,12},{9,13},{1... | collective-permute-start | bytes 1769480 | tf_op jit(solution)/shard_map/ppermute | solution.py:396
  35.9 7.4 %collective-permute-start.5 = (f32[72,128]{1,0:T(8,128)S(1)}, f32[72,128]{1,0:T(8,128)S(1)}, u32[]{:S(2)}, u32[]{:S(2)}) collective-permute-start(f32[72,128]{1,0:T(8,128)S(1)} %get-tuple-element.32), channel_id=1, source_target_pairs={{0,2},{1,3},{2,0},{3,1},{4,6},{5,7},{6,4},{7,5},{8,10},{9,11},{10,... | collective-permute-start | bytes 110600 | tf_op jit(solution)/shard_map/ppermute | solution.py:400
  38.6 9.1 %collective-permute-start.4 = (f32[216,128]{1,0:T(8,128)S(1)}, f32[216,128]{1,0:T(8,128)S(1)}, u32[]{:S(2)}, u32[]{:S(2)}) collective-permute-start(f32[216,128]{1,0:T(8,128)S(1)} %get-tuple-element.31), channel_id=1, source_target_pairs={{0,2},{1,3},{2,0},{3,1},{4,6},{5,7},{6,4},{7,5},{8,10},{9,11},{10,... | collective-permute-start | bytes 331784 | tf_op jit(solution)/shard_map/ppermute | solution.py:400
  43.3 4.4 %collective-permute-start.7 = (f32[6,24,128]{2,1,0:T(8,128)S(1)}, f32[6,24,128]{2,1,0:T(8,128)S(1)}, u32[]{:S(2)}, u32[]{:S(2)}) collective-permute-start(f32[6,24,128]{2,1,0:T(8,128)S(1)} %get-tuple-element.34), channel_id=1, source_target_pairs={{0,1},{1,0},{2,3},{3,2},{4,5},{5,4},{6,7},{7,6},{8,9},{9,8},{10,11... | collective-permute-start | bytes 221192 | tf_op jit(solution)/shard_map/ppermute | solution.py:400
  55.1 9.8 %collective-permute-start.10 = (f32[18,48,128]{2,1,0:T(8,128)S(1)}, f32[18,48,128]{2,1,0:T(8,128)S(1)}, u32[]{:S(2)}, u32[]{:S(2)}) collective-permute-start(f32[18,48,128]{2,1,0:T(8,128)S(1)} %get-tuple-element.39), channel_id=1, source_target_pairs={{0,32},{32,0},{64,96},{96,64},{1,33},{33,1},{65,97},{97,65},{2,34}... | collective-permute-start | bytes 1327112 | tf_op jit(solution)/shard_map/ppermute | solution.py:400
  55.1 18.5 %collective-permute-start.11 = (f32[18,48,128]{2,1,0:T(8,128)S(1)}, f32[18,48,128]{2,1,0:T(8,128)S(1)}, u32[]{:S(2)}, u32[]{:S(2)}) collective-permute-start(f32[18,48,128]{2,1,0:T(8,128)S(1)} %get-tuple-element.40), channel_id=1, source_target_pairs={{0,64},{32,96},{64,0},{96,32},{1,65},{33,97},{65,1},{97,33},{2,66}... | collective-permute-start | bytes 1327112 | tf_op jit(solution)/shard_map/ppermute | solution.py:400
  58.0 20.9 %collective-permute-start.12 = (f32[18,48,128]{2,1,0:T(8,128)S(1)}, f32[18,48,128]{2,1,0:T(8,128)S(1)}, u32[]{:S(2)}, u32[]{:S(2)}) collective-permute-start(f32[18,48,128]{2,1,0:T(8,128)S(1)} %get-tuple-element.41), channel_id=1, source_target_pairs={{0,96},{32,64},{64,32},{96,0},{1,97},{33,65},{65,33},{97,1},{2,98}... | collective-permute-start | bytes 1327112 | tf_op jit(solution)/shard_map/ppermute | solution.py:400
  61.7 17.6 %collective-permute-start.13 = (f32[6,48,128]{2,1,0:T(8,128)S(1)}, f32[6,48,128]{2,1,0:T(8,128)S(1)}, u32[]{:S(2)}, u32[]{:S(2)}) collective-permute-start(f32[6,48,128]{2,1,0:T(8,128)S(1)} %get-tuple-element.43), channel_id=1, source_target_pairs={{0,32},{32,0},{64,96},{96,64},{1,33},{33,1},{65,97},{97,65},{2,34}... | collective-permute-start | bytes 442376 | tf_op jit(solution)/shard_map/ppermute | solution.py:400
  61.8 24.0 %collective-permute-start.14 = (f32[6,48,128]{2,1,0:T(8,128)S(1)}, f32[6,48,128]{2,1,0:T(8,128)S(1)}, u32[]{:S(2)}, u32[]{:S(2)}) collective-permute-start(f32[6,48,128]{2,1,0:T(8,128)S(1)} %get-tuple-element.44), channel_id=1, source_target_pairs={{0,64},{32,96},{64,0},{96,32},{1,65},{33,97},{65,1},{97,33},{2,66}... | collective-permute-start | bytes 442376 | tf_op jit(solution)/shard_map/ppermute | solution.py:400
  64.9 20.8 %collective-permute-start.15 = (f32[6,48,128]{2,1,0:T(8,128)S(1)}, f32[6,48,128]{2,1,0:T(8,128)S(1)}, u32[]{:S(2)}, u32[]{:S(2)}) collective-permute-start(f32[6,48,128]{2,1,0:T(8,128)S(1)} %get-tuple-element.45), channel_id=1, source_target_pairs={{0,96},{32,64},{64,32},{96,0},{1,97},{33,65},{65,33},{97,1},{2,98}... | collective-permute-start | bytes 442376 | tf_op jit(solution)/shard_map/ppermute | solution.py:400

commit v3 on v2

--- a/solution.py
+++ b/solution.py
@@ -3,8 +3,6 @@
 
 import jax
 import jax.numpy as jnp
-import ml_dtypes
-import numpy as np
 from jax import lax
 from jax.experimental import pallas as pl
 from jax.experimental.pallas import tpu as pltpu
@@ -40,22 +38,16 @@
 SIDE = [0.0] + [-0.5 * w / 7.0 for w in WEIGHTS[1:]]
 
 
-def side_weight(distance):
-    distance = abs(distance)
-    return SIDE[distance] if 1 <= distance <= REACH else 0.0
-
-
 def z_matrix():
-    whole = np.zeros((2 * LANES, LANES))
-    for z in range(LANES):
-        for other in range(max(0, z - REACH), min(LANES, z + REACH + 1)):
-            whole[other, z] = side_weight(other - z)
-        for c in range(2 * REACH):
-            position = LANES + c if c < REACH else c - 2 * REACH
-            whole[LANES + c, z] = side_weight(position - z)
-    high = whole.astype(ml_dtypes.bfloat16)
-    low = (whole - high.astype(np.float64)).astype(ml_dtypes.bfloat16)
-    return np.concatenate([high, low], axis=1)
+    row = lax.broadcasted_iota(jnp.int32, (LANES, LANES), 0)
+    column = lax.broadcasted_iota(jnp.int32, (LANES, LANES), 1)
+    position = jnp.where(row < REACH, LANES + row, row - 2 * REACH)
+    own = jnp.zeros((LANES, LANES), jnp.float32)
+    face = own
+    for k in range(1, REACH + 1):
+        own = jnp.where(jnp.abs(row - column) == k, SIDE[k], own)
+        face = jnp.where((row < 2 * REACH) & (jnp.abs(position - column) == k), SIDE[k], face)
+    return jnp.concatenate(split(jnp.concatenate([own, face], axis=0)), axis=1)
 
 
 def selection(group):
@@ -102,23 +94,6 @@
     ]
 
 
-def pack_kernel(n, *refs):
-    pack_into(refs[:n], refs[n], refs[n + 1])
-
-
-def pack_faces(pieces):
-    planes = sum(piece.shape[0] for piece in pieces)
-    return pl.pallas_call(
-        functools.partial(pack_kernel, len(pieces)),
-        out_shape=face_shapes(planes),
-        in_specs=[VMEM] * len(pieces),
-        out_specs=[VMEM] * 2,
-        compiler_params=pltpu.CompilerParams(vmem_limit_bytes=VMEM_LIMIT),
-        cost_estimate=COST,
-        name="pack_faces",
-    )(*pieces)
-
-
 def entry_kernel(source_ref, low_ref, y_ref, z_ref):
     low_ref[...] = source_ref[0:REACH]
     pack_into([source_ref], y_ref, z_ref)
@@ -140,12 +115,13 @@
 def stencil_kernel(counts, sections, second, band_ref, *refs):
     n, m = len(counts), len(sections)
     pieces, y_refs, z_refs = refs[:n], refs[n : n + m], refs[n + m : n + 2 * m]
-    potential_ref, weights_ref, halo_ref = refs[n + 2 * m : n + 2 * m + 3]
-    rest = list(refs[n + 2 * m + 3 :])
+    potential_ref, halo_ref = refs[n + 2 * m : n + 2 * m + 2]
+    rest = list(refs[n + 2 * m + 2 :])
     planes, rows = sum(counts), pieces[0].shape[1]
     source_ref = rest.pop(0) if second else None
-    extended, gathered = rest[-2:]
-    outputs = rest[:-2]
+    extended, gathered, weights_ref = rest[-3:]
+    outputs = rest[:-3]
+    weights_ref[...] = z_matrix()
     face_of = [(y_refs[i], 2 * REACH * q) for i, size in enumerate(sections) for q in range(size)]
 
     def one_group(group, carry):
@@ -227,7 +203,7 @@
     planes, rows = sum(counts), pieces[0].shape[1]
     sections = [z.shape[0] for _, z in faces]
     operands = list(pieces) + [y for y, _ in faces] + [z for _, z in faces]
-    operands += [potential, jnp.asarray(z_matrix()), halo]
+    operands += [potential, halo]
     if second:
         operands.append(source)
         shapes = [(planes, rows, LANES)] + [(planes - REACH, rows // 4, LANES)] * 4
@@ -242,6 +218,7 @@
         scratch_shapes=[
             pltpu.VMEM((planes, ROWS + 16, LANES), jnp.float32),
             pltpu.VMEM((planes, ROWS, LANES), jnp.float32),
+            pltpu.VMEM((2 * LANES, 2 * LANES), jnp.bfloat16),
         ],
         compiler_params=pltpu.CompilerParams(vmem_limit_bytes=VMEM_LIMIT),
         cost_estimate=COST,
@@ -267,22 +244,22 @@
     lax.fori_loop(0, rows // 8, body, 0)
 
 
-def finish_first_kernel(partial_ref, halo_ref, out_ref, y_ref, z_ref):
-    add_halo(out_ref, partial_ref, halo_ref, True, 1.0)
-    pack_into([out_ref], y_ref, z_ref)
-
-
-def finish_first(partial, halo):
-    planes = partial.shape[0]
+def finish_first_kernel(low_ref, middle_ref, partial_ref, halo_ref, top_ref, y_ref, z_ref):
+    add_halo(top_ref, partial_ref, halo_ref, True, 1.0)
+    pack_into([low_ref, middle_ref, top_ref], y_ref, z_ref)
+
+
+def finish_first(low, middle, partial, halo):
+    planes = low.shape[0] + middle.shape[0] + partial.shape[0]
     return pl.pallas_call(
         finish_first_kernel,
         out_shape=[jax.ShapeDtypeStruct(partial.shape, jnp.float32)] + face_shapes(planes),
-        in_specs=[VMEM] * 2,
+        in_specs=[VMEM] * 4,
         out_specs=[VMEM] * 3,
         compiler_params=pltpu.CompilerParams(vmem_limit_bytes=VMEM_LIMIT),
         cost_estimate=COST,
         name="finish_first",
-    )(partial, halo)
+    )(low, middle, partial, halo)
 
 
 def finish_filtered_kernel(band_ref, partial_ref, halo_ref, whole_ref, out_ref, *rest):
@@ -374,23 +351,6 @@
     )(band, before, *parts)
 
 
-def total_kernel(scale, rows_ref, out_ref):
-    row = jnp.sum(rows_ref[...], axis=0, keepdims=True) * scale
-    for i in range(4):
-        out_ref[i : i + 1, :] = row[:, 4 * i : 4 * i + 4]
-
-
-def total_gram(rows, cell_count):
-    return pl.pallas_call(
-        functools.partial(total_kernel, 1.0 / cell_count),
-        out_shape=jax.ShapeDtypeStruct((4, 4), jnp.float32),
-        in_specs=[VMEM],
-        out_specs=VMEM,
-        cost_estimate=COST,
-        name="total_gram",
-    )(rows)
-
-
 def shifted(array, by):
     peers = lax.axis_size("space")
     return lax.ppermute(array, "space", [(i, (i + by) % peers) for i in range(peers)])
@@ -419,19 +379,19 @@
     above = shifted(low_planes, -4)
     low, middle, top = apply_stencil([source], [faces], local_potential, below, band)
     above_first = shifted(low, -4)
-    main_faces = swapped_faces(pack_faces([low, middle]))
-    top, *top_faces = finish_first(top, above)
+    top, *faces = finish_first(low, middle, top, above)
     below_first = shifted(top, 4)
-    top_faces = swapped_faces(top_faces)
+    faces = swapped_faces(faces)
     filtered, *slots, low_filtered = apply_stencil(
-        [low, middle, top], [main_faces, top_faces], local_potential, above_first, band, source
+        [low, middle, top], [faces], local_potential, above_first, band, source
     )
     early = early_gram(band_exchange(slots))
     filtered, *slots = finish_filtered(low_filtered, below_first, filtered, band)
     both = ("band", "space")
     rows = late_gram(early, band_exchange(slots), band, lax.axis_size(both))
     everyone = lax.all_to_all(rows, both, 0, 0, tiled=True)
-    correlation = total_gram(everyone, filtered.size * lax.axis_size("space"))
+    summed = jnp.sum(everyone, axis=0)[:16].reshape(4, 4)
+    correlation = summed / jnp.float32(filtered.size * lax.axis_size("space"))
     return filtered[None, None], correlation
 
 

time: 106 us -> 104 us (0.981)
  starting transfers between devices: 24.5 us -> 27.7 us
  waiting for transfers between devices: 36.8 us -> 33.7 us
  Pallas kernels: 19.3 us -> 17.7 us
    ppermute x12 -> x10, waiting for transfers between devices: 34 us -> 30.7 us  [swapped(): lax.ppermute(array, axis, [(i, i ^ bit) for i in range(lax.axis_size(axis...]
    pallas_call x2 -> x0, Pallas kernels: 2.13 us -> none  [the longest x1 1.51 us: total_gram(): pl.pallas_call(functools.partial(total_kernel, 1.0 / cell_count), out_sha...]
    ppermute x4, starting transfers between devices: 8.71 us -> 10.5 us  [shifted(): lax.ppermute(array, 'space', [(i, (i + by) % peers) for i in range(peers)])]
    ppermute x12 -> x10, starting transfers between devices: 15.8 us -> 17.2 us  [swapped(): lax.ppermute(array, axis, [(i, i ^ bit) for i in range(lax.axis_size(axis...]
    unnamed x12 -> x8, local copies, waits for them, and re-layouts: 4.25 us -> 3.34 us
  transfers between devices with their start and end apart: 16 -> 14, of which waited for: 9 -> 8; matrix products, arithmetic and copies ran while one was open for 0% -> 0% of each run, Pallas kernels for 17% -> 17%
where the time goes in v3:
time: 104 us; the launch traced here: 103 us
  waiting for transfers between devices  33.7 us (32%)
  starting transfers between devices  27.7 us (27%)
  Pallas kernels  17.7 us (17%)
  blocking collectives  16.9 us (16%)
  local copies, waits for them, and re-layouts  5.94 us (6%)
    ppermute x10, waiting for transfers between devices, swapped(): lax.ppermute(array, axis, [(i, i ^ bit) for i in range(lax.axis_size(axis...  30.7 us
    ppermute x10, starting transfers between devices, swapped(): lax.ppermute(array, axis, [(i, i ^ bit) for i in range(lax.axis_size(axis...  17.2 us
    all_to_all x1, blocking collectives, on_device(): everyone = lax.all_to_all(rows, both, 0, 0, tiled=True)  16.9 us
    pallas_call x2, Pallas kernels, apply_stencil(): pl.pallas_call(functools.partial(stencil_kernel, counts, sections, second...  13.2 us
    ppermute x4, starting transfers between devices, shifted(): lax.ppermute(array, 'space', [(i, (i + by) % peers) for i in range(peers)])  10.5 us
    unnamed x8, local copies, waits for them, and re-layouts  3.34 us
    ppermute x4, waiting for transfers between devices, shifted(): lax.ppermute(array, 'space', [(i, (i + by) % peers) for i in range(peers)])  2.92 us
  transfers between devices with their start and end apart: 14, of which 8 were waited for; matrix products, arithmetic and copies ran while one was open for 0% of the time, Pallas kernels for 17%

profile of v3, /device:TPU:0, one launch (start us, length us, event | category | flops | bytes accessed | tf_op | source)
XLA Modules:
  0.0 102.8 jit_solution(6995654268640021042)
XLA Ops:
  0.6 1.9 %slice_bitcast_fusion = f32[6,192,128]{2,1,0:T(8,128)} fusion(f32[1,1,24,192,128]{4,3,2,1,0:T(8,128)} %param.2), kind=kLoop, calls=%fused_computation | loop fusion | bytes 1179648 | tf_op jit(solution)/shard_map/slice | solution.py:376
  2.6 1.7 %collective-permute-start.2 = (f32[6,192,128]{2,1,0:T(8,128)}, f32[6,192,128]{2,1,0:T(8,128)S(1)}, u32[]{:S(2)}, u32[]{:S(2)}) collective-permute-start(f32[6,192,128]{2,1,0:T(8,128)} %slice_bitcast_fusion), channel_id=1, source_target_pairs={{0,4},{1,5},{2,6},{3,7},{4,8},{5,9},{6,10},{7,11},{8,12},{9,13},{1... | collective-permute-start | bytes 1769480 | tf_op jit(solution)/shard_map/ppermute | solution.py:356
  4.2 0.0 copy-start
  4.2 1.7 %copy-done = f32[1,1,24,192,128]{4,3,2,1,0:T(8,128)S(1)} copy-done((f32[1,1,24,192,128]{4,3,2,1,0:T(8,128)S(1)}, f32[1,1,24,192,128]{4,3,2,1,0:T(8,128)}, u32[]{:S(2)}) %copy-start) | copy-done | bytes 2359320
  5.9 0.0 copy-start.1
  5.9 1.7 %entry.1 = (f32[6,192,128]{2,1,0:T(8,128)}, f32[288,128]{1,0:T(8,128)}, f32[24,24,128]{2,1,0:T(8,128)}) custom-call(f32[24,192,128]{2,1,0:T(8,128)S(1)} %bitcast.9), custom_call_target="tpu_custom_call" | custom-call | flops 1 | bytes 1 | tf_op jit(solution)/shard_map/entry/pallas_call | solution.py:104
  7.6 1.5 %collective-permute-start.1 = (f32[24,24,128]{2,1,0:T(8,128)}, f32[24,24,128]{2,1,0:T(8,128)}, u32[]{:S(2)}, u32[]{:S(2)}) collective-permute-start(f32[24,24,128]{2,1,0:T(8,128)} %get-tuple-element.23), channel_id=1, source_target_pairs={{0,1},{1,0},{2,3},{3,2},{4,5},{5,4},{6,7},{7,6},{8,9},{9,8},{10,11... | collective-permute-start | bytes 884744 | tf_op jit(solution)/shard_map/ppermute | solution.py:360
  9.1 3.5 %collective-permute-start.3 = (f32[6,192,128]{2,1,0:T(8,128)}, f32[6,192,128]{2,1,0:T(8,128)S(1)}, u32[]{:S(2)}, u32[]{:S(2)}) collective-permute-start(f32[6,192,128]{2,1,0:T(8,128)} %get-tuple-element.27), channel_id=1, source_target_pairs={{0,28},{1,29},{2,30},{3,31},{4,0},{5,1},{6,2},{7,3},{8,4},{9,5},{1... | collective-permute-start | bytes 1769480 | tf_op jit(solution)/shard_map/ppermute | solution.py:356
  12.6 2.7 %collective-permute-start = (f32[288,128]{1,0:T(8,128)}, f32[288,128]{1,0:T(8,128)}, u32[]{:S(2)}, u32[]{:S(2)}) collective-permute-start(f32[288,128]{1,0:T(8,128)} %get-tuple-element.22), channel_id=1, source_target_pairs={{0,2},{1,3},{2,0},{3,1},{4,6},{5,7},{6,4},{7,5},{8,10},{9,11},{10,... | collective-permute-start | bytes 442376 | tf_op jit(solution)/shard_map/ppermute | solution.py:360
  15.3 6.4 %collective-permute-done.refs_1_ = f32[288,128]{1,0:T(8,128)} collective-permute-done((f32[288,128]{1,0:T(8,128)}, f32[288,128]{1,0:T(8,128)}, u32[]{:S(2)}, u32[]{:S(2)}) %collective-permute-start) | collective-permute-done | bytes 147488 | tf_op jit(solution)/shard_map/ppermute | solution.py:360
  21.7 0.0 collective-permute-done.1.refs_2_
  21.7 0.3 collective-permute-done.2.refs_4_
  22.1 0.0 copy-done.1
  22.1 0.0 copy-start.2
  22.1 1.7 %copy-done.2 = f32[1,24,192,128]{3,2,1,0:T(8,128)S(1)} copy-done((f32[1,24,192,128]{3,2,1,0:T(8,128)S(1)}, f32[1,24,192,128]{3,2,1,0:T(8,128)}, u32[]{:S(2)}) %copy-start.2) | copy-done | bytes 2359320
  23.7 6.1 %first_step.1 = (f32[6,192,128]{2,1,0:T(8,128)S(1)}, f32[12,192,128]{2,1,0:T(8,128)S(1)}, f32[6,192,128]{2,1,0:T(8,128)S(1)}) custom-call(s32[1]{0:T(128)} %bitcast.band_ref, f32[24,192,128]{2,1,0:T(8,128)S(1)} %bitcast.10, f32[288,128]{1,0:T(8,128)} %collective-permute-done.refs_1_, f32[24,24,128]{2,1,0:T(8,128)} %collective-permute-done.1.refs_2_, ...), custom_call_target="tpu_custom_call" | custom-call | flops 1 | bytes 1 | tf_op jit(solution)/shard_map/first_step/pallas_call | solution.py:213
  29.9 0.0 copy-start.3
  29.9 3.5 %collective-permute-start.6 = (f32[6,192,128]{2,1,0:T(8,128)S(1)}, f32[6,192,128]{2,1,0:T(8,128)S(1)}, u32[]{:S(2)}, u32[]{:S(2)}) collective-permute-start(f32[6,192,128]{2,1,0:T(8,128)S(1)} %get-tuple-element.24.low_ref.refs_0_), channel_id=1, source_target_pairs={{0,28},{1,29},{2,30},{3,31},{4,0},{5,1},{6,2},{7,3},{8,4},{9,5},{1... | collective-permute-start | bytes 1769480 | tf_op jit(solution)/shard_map/ppermute | solution.py:356
  33.4 0.0 collective-permute-done.3.halo_ref
  33.4 1.1 %finish_first.1 = (f32[6,192,128]{2,1,0:T(8,128)S(1)}, f32[288,128]{1,0:T(8,128)S(1)}, f32[24,24,128]{2,1,0:T(8,128)S(1)}) custom-call(f32[6,192,128]{2,1,0:T(8,128)S(1)} %get-tuple-element.24.low_ref.refs_0_, f32[12,192,128]{2,1,0:T(8,128)S(1)} %get-tuple-element.25.middle_ref.refs_1_, f32[6,192,128]{2,1,0:T(8,128)S(1)} %get-tuple-element.26.partial_ref, ...), custom_call_target="tpu_custom_call" | custom-call | flops 1 | bytes 1 | tf_op jit(solution)/shard_map/finish_first/pallas_call | solution.py:254
  34.5 0.9 collective-permute-start.5
  35.4 1.9 %collective-permute-start.7 = (f32[6,192,128]{2,1,0:T(8,128)S(1)}, f32[6,192,128]{2,1,0:T(8,128)S(1)}, u32[]{:S(2)}, u32[]{:S(2)}) collective-permute-start(f32[6,192,128]{2,1,0:T(8,128)S(1)} %get-tuple-element.28.refs_2_), channel_id=1, source_target_pairs={{0,4},{1,5},{2,6},{3,7},{4,8},{5,9},{6,10},{7,11},{8,12},{9,13},{1... | collective-permute-start | bytes 1769480 | tf_op jit(solution)/shard_map/ppermute | solution.py:356
  37.3 2.7 %collective-permute-start.4 = (f32[288,128]{1,0:T(8,128)S(1)}, f32[288,128]{1,0:T(8,128)S(1)}, u32[]{:S(2)}, u32[]{:S(2)}) collective-permute-start(f32[288,128]{1,0:T(8,128)S(1)} %get-tuple-element.29), channel_id=1, source_target_pairs={{0,2},{1,3},{2,0},{3,1},{4,6},{5,7},{6,4},{7,5},{8,10},{9,11},{10,... | collective-permute-start | bytes 442376 | tf_op jit(solution)/shard_map/ppermute | solution.py:360
  40.0 6.3 %collective-permute-done.4.refs_3_ = f32[288,128]{1,0:T(8,128)S(1)} collective-permute-done((f32[288,128]{1,0:T(8,128)S(1)}, f32[288,128]{1,0:T(8,128)S(1)}, u32[]{:S(2)}, u32[]{:S(2)}) %collective-permute-start.4) | collective-permute-done | bytes 147488 | tf_op jit(solution)/shard_map/ppermute | solution.py:360
  46.3 0.0 collective-permute-done.5.refs_4_
  46.3 0.9 collective-permute-done.6.refs_6_
  47.2 0.0 copy-done.3
  47.2 7.0 %second_step.1 = (f32[24,192,128]{2,1,0:T(8,128)}, f32[18,48,128]{2,1,0:T(8,128)S(1)}, f32[18,48,128]{2,1,0:T(8,128)S(1)}, f32[18,48,128]{2,1,0:T(8,128)S(1)}, f...) custom-call(s32[1]{0:T(128)} %bitcast.band_ref, f32[6,192,128]{2,1,0:T(8,128)S(1)} %get-tuple-element.24.low_ref.refs_0_, ...), custom_call_target="tpu_custom_call" | custom-call | flops 1 | bytes 1 | tf_op jit(solution)/shard_map/second_step/pallas_call | solution.py:213
  54.2 0.0 collective-permute-start.10
  54.2 3.0 %collective-permute-start.8 = (f32[18,48,128]{2,1,0:T(8,128)S(1)}, f32[18,48,128]{2,1,0:T(8,128)S(1)}, u32[]{:S(2)}, u32[]{:S(2)}) collective-permute-start(f32[18,48,128]{2,1,0:T(8,128)S(1)} %get-tuple-element.35), channel_id=1, source_target_pairs={{0,32},{32,0},{64,96},{96,64},{1,33},{33,1},{65,97},{97,65},{2,34}... | collective-permute-start | bytes 1327112 | tf_op jit(solution)/shard_map/ppermute | solution.py:360
  57.3 0.6 collective-permute-start.9
  57.9 1.7 %collective-permute-done.7.halo_ref = f32[6,192,128]{2,1,0:T(8,128)S(1)} collective-permute-done((f32[6,192,128]{2,1,0:T(8,128)S(1)}, f32[6,192,128]{2,1,0:T(8,128)S(1)}, u32[]{:S(2)}, u32[]{:S(2)}) %collective-permute-start.7) | collective-permute-done | bytes 589856 | tf_op jit(solution)/shard_map/ppermute | solution.py:356
  59.6 1.1 %finish_filtered.1 = (f32[24,192,128]{2,1,0:T(8,128)}, f32[6,48,128]{2,1,0:T(8,128)S(1)}, f32[6,48,128]{2,1,0:T(8,128)S(1)}, f32[6,48,128]{2,1,0:T(8,128)S(1)}, f32[6,48,128]{2,1,0:T(8,128)S(1)}) custom-call(s32[1]{0:T(128)} %bitcast.band_ref, f32[6,192,128]{2,1,0:T(8,128)S(1)} %get-tuple-element.31.partial_ref, ...), custom_call_target="tpu_custom_call", output_to_operand_aliasing={{0}: (3, {})} | custom-call | flops 1 | bytes 1 | tf_op jit(solution)/shard_map/finish_filtered/pallas_call | solution.py:279
  60.7 0.1 collective-permute-start.11
  60.8 3.2 %collective-permute-start.12 = (f32[6,48,128]{2,1,0:T(8,128)S(1)}, f32[6,48,128]{2,1,0:T(8,128)S(1)}, u32[]{:S(2)}, u32[]{:S(2)}) collective-permute-start(f32[6,48,128]{2,1,0:T(8,128)S(1)} %get-tuple-element.40), channel_id=1, source_target_pairs={{0,64},{32,96},{64,0},{96,32},{1,65},{33,97},{65,1},{97,33},{2,66}... | collective-permute-start | bytes 442376 | tf_op jit(solution)/shard_map/ppermute | solution.py:360
  64.0 4.5 %collective-permute-done.10.refs_3_ = f32[18,48,128]{2,1,0:T(8,128)S(1)} collective-permute-done((f32[18,48,128]{2,1,0:T(8,128)S(1)}, f32[18,48,128]{2,1,0:T(8,128)S(1)}, u32[]{:S(2)}, u32[]{:S(2)}) %collective-permute-start.10) | collective-permute-done | bytes 442400 | tf_op jit(solution)/shard_map/ppermute | solution.py:360
  68.5 2.4 %collective-permute-start.13 = (f32[6,48,128]{2,1,0:T(8,128)S(1)}, f32[6,48,128]{2,1,0:T(8,128)S(1)}, u32[]{:S(2)}, u32[]{:S(2)}) collective-permute-start(f32[6,48,128]{2,1,0:T(8,128)S(1)} %get-tuple-element.41), channel_id=1, source_target_pairs={{0,96},{32,64},{64,32},{96,0},{1,97},{33,65},{65,33},{97,1},{2,98}... | collective-permute-start | bytes 442376 | tf_op jit(solution)/shard_map/ppermute | solution.py:360
  70.9 0.0 collective-permute-done.8.refs_1_
  70.9 11.2 %collective-permute-done.9.refs_2_ = f32[18,48,128]{2,1,0:T(8,128)S(1)} collective-permute-done((f32[18,48,128]{2,1,0:T(8,128)S(1)}, f32[18,48,128]{2,1,0:T(8,128)S(1)}, u32[]{:S(2)}, u32[]{:S(2)}) %collective-permute-start.9) | collective-permute-done | bytes 442400 | tf_op jit(solution)/shard_map/ppermute | solution.py:360
  82.1 0.4 early_gram.1.before_ref
  82.5 0.0 collective-permute-done.11.refs_1_
  82.5 2.3 %collective-permute-done.12.refs_2_ = f32[6,48,128]{2,1,0:T(8,128)S(1)} collective-permute-done((f32[6,48,128]{2,1,0:T(8,128)S(1)}, f32[6,48,128]{2,1,0:T(8,128)S(1)}, u32[]{:S(2)}, u32[]{:S(2)}) %collective-permute-start.12) | collective-permute-done | bytes 147488 | tf_op jit(solution)/shard_map/ppermute | solution.py:360
  84.8 0.0 collective-permute-done.13.refs_3_
  84.8 0.2 late_gram.1
  85.1 16.9 %all_to_all.9 = f32[128,1,128]{2,1,0:T(1,128)S(1)} all-to-all(f32[128,1,128]{2,1,0:T(1,128)S(1)} %bitcast.14), channel_id=1, replica_groups=mesh['band'=4,'space'=32] {'band','space'}, dimensions={0} | all-to-all | bytes 131072 | tf_op jit(solution)/shard_map/all_to_all | solution.py:392
  101.9 0.2 reduce_sum.9
  102.1 0.7 div.6
  (1 shorter events, 0.0 us)
Async XLA Ops:
  2.6 19.5 %collective-permute-start.2 = (f32[6,192,128]{2,1,0:T(8,128)}, f32[6,192,128]{2,1,0:T(8,128)S(1)}, u32[]{:S(2)}, u32[]{:S(2)}) collective-permute-start(f32[6,192,128]{2,1,0:T(8,128)} %slice_bitcast_fusion), channel_id=1, source_target_pairs={{0,4},{1,5},{2,6},{3,7},{4,8},{5,9},{6,10},{7,11},{8,12},{9,13},{1... | collective-permute-start | bytes 1769480 | tf_op jit(solution)/shard_map/ppermute | solution.py:356
  4.2 1.7 %copy-start = (f32[1,1,24,192,128]{4,3,2,1,0:T(8,128)S(1)}, f32[1,1,24,192,128]{4,3,2,1,0:T(8,128)}, u32[]{:S(2)}) copy-start(f32[1,1,24,192,128]{4,3,2,1,0:T(8,128)} %param.2) | copy-start | bytes 7077892
  5.9 16.2 %copy-start.1 = (f32[1,1,24,192,128]{4,3,2,1,0:T(8,128)S(1)}, f32[1,1,24,192,128]{4,3,2,1,0:T(8,128)}, u32[]{:S(2)}) copy-start(f32[1,1,24,192,128]{4,3,2,1,0:T(8,128)} %param.2) | copy-start | bytes 7077892
  7.6 14.1 %collective-permute-start.1 = (f32[24,24,128]{2,1,0:T(8,128)}, f32[24,24,128]{2,1,0:T(8,128)}, u32[]{:S(2)}, u32[]{:S(2)}) collective-permute-start(f32[24,24,128]{2,1,0:T(8,128)} %get-tuple-element.23), channel_id=1, source_target_pairs={{0,1},{1,0},{2,3},{3,2},{4,5},{5,4},{6,7},{7,6},{8,9},{9,8},{10,11... | collective-permute-start | bytes 884744 | tf_op jit(solution)/shard_map/ppermute | solution.py:360
  9.1 24.3 %collective-permute-start.3 = (f32[6,192,128]{2,1,0:T(8,128)}, f32[6,192,128]{2,1,0:T(8,128)S(1)}, u32[]{:S(2)}, u32[]{:S(2)}) collective-permute-start(f32[6,192,128]{2,1,0:T(8,128)} %get-tuple-element.27), channel_id=1, source_target_pairs={{0,28},{1,29},{2,30},{3,31},{4,0},{5,1},{6,2},{7,3},{8,4},{9,5},{1... | collective-permute-start | bytes 1769480 | tf_op jit(solution)/shard_map/ppermute | solution.py:356
  12.6 9.2 %collective-permute-start = (f32[288,128]{1,0:T(8,128)}, f32[288,128]{1,0:T(8,128)}, u32[]{:S(2)}, u32[]{:S(2)}) collective-permute-start(f32[288,128]{1,0:T(8,128)} %get-tuple-element.22), channel_id=1, source_target_pairs={{0,2},{1,3},{2,0},{3,1},{4,6},{5,7},{6,4},{7,5},{8,10},{9,11},{10,... | collective-permute-start | bytes 442376 | tf_op jit(solution)/shard_map/ppermute | solution.py:360
  22.1 1.7 %copy-start.2 = (f32[1,24,192,128]{3,2,1,0:T(8,128)S(1)}, f32[1,24,192,128]{3,2,1,0:T(8,128)}, u32[]{:S(2)}) copy-start(f32[1,24,192,128]{3,2,1,0:T(8,128)} %param.3) | copy-start | bytes 7077892
  29.9 17.3 %copy-start.3 = (f32[1,24,192,128]{3,2,1,0:T(8,128)S(1)}, f32[1,24,192,128]{3,2,1,0:T(8,128)}, u32[]{:S(2)}) copy-start(f32[1,24,192,128]{3,2,1,0:T(8,128)} %param.3) | copy-start | bytes 7077892
  29.9 17.3 %collective-permute-start.6 = (f32[6,192,128]{2,1,0:T(8,128)S(1)}, f32[6,192,128]{2,1,0:T(8,128)S(1)}, u32[]{:S(2)}, u32[]{:S(2)}) collective-permute-start(f32[6,192,128]{2,1,0:T(8,128)S(1)} %get-tuple-element.24.low_ref.refs_0_), channel_id=1, source_target_pairs={{0,28},{1,29},{2,30},{3,31},{4,0},{5,1},{6,2},{7,3},{8,4},{9,5},{1... | collective-permute-start | bytes 1769480 | tf_op jit(solution)/shard_map/ppermute | solution.py:356
  34.5 11.8 %collective-permute-start.5 = (f32[24,24,128]{2,1,0:T(8,128)S(1)}, f32[24,24,128]{2,1,0:T(8,128)S(1)}, u32[]{:S(2)}, u32[]{:S(2)}) collective-permute-start(f32[24,24,128]{2,1,0:T(8,128)S(1)} %get-tuple-element.30), channel_id=1, source_target_pairs={{0,1},{1,0},{2,3},{3,2},{4,5},{5,4},{6,7},{7,6},{8,9},{9,8},{10,11... | collective-permute-start | bytes 884744 | tf_op jit(solution)/shard_map/ppermute | solution.py:360
  35.4 24.2 %collective-permute-start.7 = (f32[6,192,128]{2,1,0:T(8,128)S(1)}, f32[6,192,128]{2,1,0:T(8,128)S(1)}, u32[]{:S(2)}, u32[]{:S(2)}) collective-permute-start(f32[6,192,128]{2,1,0:T(8,128)S(1)} %get-tuple-element.28.refs_2_), channel_id=1, source_target_pairs={{0,4},{1,5},{2,6},{3,7},{4,8},{5,9},{6,10},{7,11},{8,12},{9,13},{1... | collective-permute-start | bytes 1769480 | tf_op jit(solution)/shard_map/ppermute | solution.py:356
  37.3 9.0 %collective-permute-start.4 = (f32[288,128]{1,0:T(8,128)S(1)}, f32[288,128]{1,0:T(8,128)S(1)}, u32[]{:S(2)}, u32[]{:S(2)}) collective-permute-start(f32[288,128]{1,0:T(8,128)S(1)} %get-tuple-element.29), channel_id=1, source_target_pairs={{0,2},{1,3},{2,0},{3,1},{4,6},{5,7},{6,4},{7,5},{8,10},{9,11},{10,... | collective-permute-start | bytes 442376 | tf_op jit(solution)/shard_map/ppermute | solution.py:360
  54.2 14.3 %collective-permute-start.10 = (f32[18,48,128]{2,1,0:T(8,128)S(1)}, f32[18,48,128]{2,1,0:T(8,128)S(1)}, u32[]{:S(2)}, u32[]{:S(2)}) collective-permute-start(f32[18,48,128]{2,1,0:T(8,128)S(1)} %get-tuple-element.37), channel_id=1, source_target_pairs={{0,96},{32,64},{64,32},{96,0},{1,97},{33,65},{65,33},{97,1},{2,98}... | collective-permute-start | bytes 1327112 | tf_op jit(solution)/shard_map/ppermute | solution.py:360
  54.2 16.7 %collective-permute-start.8 = (f32[18,48,128]{2,1,0:T(8,128)S(1)}, f32[18,48,128]{2,1,0:T(8,128)S(1)}, u32[]{:S(2)}, u32[]{:S(2)}) collective-permute-start(f32[18,48,128]{2,1,0:T(8,128)S(1)} %get-tuple-element.35), channel_id=1, source_target_pairs={{0,32},{32,0},{64,96},{96,64},{1,33},{33,1},{65,97},{97,65},{2,34}... | collective-permute-start | bytes 1327112 | tf_op jit(solution)/shard_map/ppermute | solution.py:360
  57.3 24.9 %collective-permute-start.9 = (f32[18,48,128]{2,1,0:T(8,128)S(1)}, f32[18,48,128]{2,1,0:T(8,128)S(1)}, u32[]{:S(2)}, u32[]{:S(2)}) collective-permute-start(f32[18,48,128]{2,1,0:T(8,128)S(1)} %get-tuple-element.36), channel_id=1, source_target_pairs={{0,64},{32,96},{64,0},{96,32},{1,65},{33,97},{65,1},{97,33},{2,66}... | collective-permute-start | bytes 1327112 | tf_op jit(solution)/shard_map/ppermute | solution.py:360
  60.7 21.8 %collective-permute-start.11 = (f32[6,48,128]{2,1,0:T(8,128)S(1)}, f32[6,48,128]{2,1,0:T(8,128)S(1)}, u32[]{:S(2)}, u32[]{:S(2)}) collective-permute-start(f32[6,48,128]{2,1,0:T(8,128)S(1)} %get-tuple-element.39), channel_id=1, source_target_pairs={{0,32},{32,0},{64,96},{96,64},{1,33},{33,1},{65,97},{97,65},{2,34}... | collective-permute-start | bytes 442376 | tf_op jit(solution)/shard_map/ppermute | solution.py:360
  60.8 24.0 %collective-permute-start.12 = (f32[6,48,128]{2,1,0:T(8,128)S(1)}, f32[6,48,128]{2,1,0:T(8,128)S(1)}, u32[]{:S(2)}, u32[]{:S(2)}) collective-permute-start(f32[6,48,128]{2,1,0:T(8,128)S(1)} %get-tuple-element.40), channel_id=1, source_target_pairs={{0,64},{32,96},{64,0},{96,32},{1,65},{33,97},{65,1},{97,33},{2,66}... | collective-permute-start | bytes 442376 | tf_op jit(solution)/shard_map/ppermute | solution.py:360
  68.5 16.3 %collective-permute-start.13 = (f32[6,48,128]{2,1,0:T(8,128)S(1)}, f32[6,48,128]{2,1,0:T(8,128)S(1)}, u32[]{:S(2)}, u32[]{:S(2)}) collective-permute-start(f32[6,48,128]{2,1,0:T(8,128)S(1)} %get-tuple-element.41), channel_id=1, source_target_pairs={{0,96},{32,64},{64,32},{96,0},{1,97},{33,65},{65,33},{97,1},{2,98}... | collective-permute-start | bytes 442376 | tf_op jit(solution)/shard_map/ppermute | solution.py:360

commit v4 on v3

--- a/solution.py
+++ b/solution.py
@@ -94,22 +94,22 @@
     ]
 
 
-def entry_kernel(source_ref, low_ref, y_ref, z_ref):
+def entry_kernel(band_ref, source_ref, low_ref, y_ref, z_ref):
     low_ref[...] = source_ref[0:REACH]
     pack_into([source_ref], y_ref, z_ref)
 
 
-def entry(source):
+def entry(band, source):
     outer = jax.ShapeDtypeStruct((REACH,) + source.shape[1:], jnp.float32)
     return pl.pallas_call(
         entry_kernel,
         out_shape=[outer] + face_shapes(source.shape[0]),
-        in_specs=[VMEM],
+        in_specs=[SMEM, VMEM],
         out_specs=[VMEM] * 3,
         compiler_params=pltpu.CompilerParams(vmem_limit_bytes=VMEM_LIMIT),
         cost_estimate=COST,
         name="entry",
-    )(source)
+    )(band, source)
 
 
 def stencil_kernel(counts, sections, second, band_ref, *refs):
@@ -374,7 +374,7 @@
     source, local_potential = orbitals[0, 0], potential[0]
     band = lax.axis_index("band").astype(jnp.int32).reshape(1)
     below = shifted(source[source.shape[0] - REACH :], 4)
-    low_planes, *faces = entry(source)
+    low_planes, *faces = entry(band, source)
     faces = swapped_faces(faces)
     above = shifted(low_planes, -4)
     low, middle, top = apply_stencil([source], [faces], local_potential, below, band)

time: 104 us -> 103 us (level)
  waiting for transfers between devices: 33.7 us -> 37.8 us
  local copies, waits for them, and re-layouts: 5.94 us -> 3.44 us
  starting transfers between devices: 27.7 us -> 25.4 us
  Pallas kernels: 17.7 us -> 15.7 us
  blocking collectives: 16.9 us -> 18.5 us
    ppermute x4, waiting for transfers between devices: 2.92 us -> 6.79 us  [shifted(): lax.ppermute(array, 'space', [(i, (i + by) % peers) for i in range(peers)])]
    unnamed x8 -> x6, local copies, waits for them, and re-layouts: 3.34 us -> 1.67 us
    all_to_all x1, blocking collectives: 16.9 us -> 18.5 us  [on_device(): everyone = lax.all_to_all(rows, both, 0, 0, tiled=True)]
    ppermute x10, starting transfers between devices: 17.2 us -> 16 us  [swapped(): lax.ppermute(array, axis, [(i, i ^ bit) for i in range(lax.axis_size(axis...]
    ppermute x4, starting transfers between devices: 10.5 us -> 9.42 us  [shifted(): lax.ppermute(array, 'space', [(i, (i + by) % peers) for i in range(peers)])]
    pallas_call x2, Pallas kernels: 13.2 us -> 12.1 us  [apply_stencil(): pl.pallas_call(functools.partial(stencil_kernel, counts, sections, second...]
  transfers between devices with their start and end apart: 14 -> 14, of which waited for: 8 -> 9; matrix products, arithmetic and copies ran while one was open for 0% -> 0% of each run, Pallas kernels for 17% -> 15%
where the time goes in v4:
time: 103 us; the launch traced here: 102 us
  waiting for transfers between devices  37.8 us (37%)
  starting transfers between devices  25.4 us (25%)
  blocking collectives  18.5 us (18%)
  Pallas kernels  15.7 us (15%)
  local copies, waits for them, and re-layouts  3.44 us (3%)
    ppermute x10, waiting for transfers between devices, swapped(): lax.ppermute(array, axis, [(i, i ^ bit) for i in range(lax.axis_size(axis...  31 us
    all_to_all x1, blocking collectives, on_device(): everyone = lax.all_to_all(rows, both, 0, 0, tiled=True)  18.5 us
    ppermute x10, starting transfers between devices, swapped(): lax.ppermute(array, axis, [(i, i ^ bit) for i in range(lax.axis_size(axis...  16 us
    pallas_call x2, Pallas kernels, apply_stencil(): pl.pallas_call(functools.partial(stencil_kernel, counts, sections, second...  12.1 us
    ppermute x4, starting transfers between devices, shifted(): lax.ppermute(array, 'space', [(i, (i + by) % peers) for i in range(peers)])  9.42 us
    ppermute x4, waiting for transfers between devices, shifted(): lax.ppermute(array, 'space', [(i, (i + by) % peers) for i in range(peers)])  6.79 us
  transfers between devices with their start and end apart: 14, of which 9 were waited for; matrix products, arithmetic and copies ran while one was open for 0% of the time, Pallas kernels for 15%

profile of v4, /device:TPU:0, one launch (start us, length us, event | category | flops | bytes accessed | tf_op | source)
XLA Modules:
  0.0 101.8 jit_solution(1896487744301189462)
XLA Ops:
  0.6 1.1 %slice_bitcast_fusion = f32[6,192,128]{2,1,0:T(8,128)S(1)} fusion(f32[1,1,24,192,128]{4,3,2,1,0:T(8,128)} %param.2), kind=kLoop, calls=%fused_computation | loop fusion | bytes 1179648 | tf_op jit(solution)/shard_map/slice | solution.py:376
  1.7 1.7 %collective-permute-start.2 = (f32[6,192,128]{2,1,0:T(8,128)S(1)}, f32[6,192,128]{2,1,0:T(8,128)S(1)}, u32[]{:S(2)}, u32[]{:S(2)}) collective-permute-start(f32[6,192,128]{2,1,0:T(8,128)S(1)} %slice_bitcast_fusion), channel_id=1, source_target_pairs={{0,4},{1,5},{2,6},{3,7},{4,8},{5,9},{6,10},{7,11},{8,12},{9,13},{1... | collective-permute-start | bytes 1769480 | tf_op jit(solution)/shard_map/ppermute | solution.py:356
  3.5 0.0 copy-start
  3.5 1.7 %copy-done = f32[1,1,24,192,128]{4,3,2,1,0:T(8,128)S(1)} copy-done((f32[1,1,24,192,128]{4,3,2,1,0:T(8,128)S(1)}, f32[1,1,24,192,128]{4,3,2,1,0:T(8,128)}, u32[]{:S(2)}) %copy-start) | copy-done | bytes 2359320
  5.1 0.0 copy-start.2
  5.1 0.8 entry.1
  6.0 1.6 %collective-permute-start.1 = (f32[24,24,128]{2,1,0:T(8,128)S(1)}, f32[24,24,128]{2,1,0:T(8,128)S(1)}, u32[]{:S(2)}, u32[]{:S(2)}) collective-permute-start(f32[24,24,128]{2,1,0:T(8,128)S(1)} %get-tuple-element.23), channel_id=1, source_target_pairs={{0,1},{1,0},{2,3},{3,2},{4,5},{5,4},{6,7},{7,6},{8,9},{9,8},{10,11... | collective-permute-start | bytes 884744 | tf_op jit(solution)/shard_map/ppermute | solution.py:360
  7.5 3.5 %collective-permute-start.3 = (f32[6,192,128]{2,1,0:T(8,128)S(1)}, f32[6,192,128]{2,1,0:T(8,128)S(1)}, u32[]{:S(2)}, u32[]{:S(2)}) collective-permute-start(f32[6,192,128]{2,1,0:T(8,128)S(1)} %get-tuple-element.27), channel_id=1, source_target_pairs={{0,28},{1,29},{2,30},{3,31},{4,0},{5,1},{6,2},{7,3},{8,4},{9,5},{1... | collective-permute-start | bytes 1769480 | tf_op jit(solution)/shard_map/ppermute | solution.py:356
  11.0 2.7 %collective-permute-start = (f32[288,128]{1,0:T(8,128)S(1)}, f32[288,128]{1,0:T(8,128)S(1)}, u32[]{:S(2)}, u32[]{:S(2)}) collective-permute-start(f32[288,128]{1,0:T(8,128)S(1)} %get-tuple-element.22), channel_id=1, source_target_pairs={{0,2},{1,3},{2,0},{3,1},{4,6},{5,7},{6,4},{7,5},{8,10},{9,11},{10,... | collective-permute-start | bytes 442376 | tf_op jit(solution)/shard_map/ppermute | solution.py:360
  13.7 6.1 %collective-permute-done.refs_1_ = f32[288,128]{1,0:T(8,128)S(1)} collective-permute-done((f32[288,128]{1,0:T(8,128)S(1)}, f32[288,128]{1,0:T(8,128)S(1)}, u32[]{:S(2)}, u32[]{:S(2)}) %collective-permute-start) | collective-permute-done | bytes 147488 | tf_op jit(solution)/shard_map/ppermute | solution.py:360
  19.9 0.0 collective-permute-done.1.refs_2_
  19.9 1.2 %collective-permute-done.2.refs_4_ = f32[6,192,128]{2,1,0:T(8,128)S(1)} collective-permute-done((f32[6,192,128]{2,1,0:T(8,128)S(1)}, f32[6,192,128]{2,1,0:T(8,128)S(1)}, u32[]{:S(2)}, u32[]{:S(2)}) %collective-permute-start.2) | collective-permute-done | bytes 589856 | tf_op jit(solution)/shard_map/ppermute | solution.py:356
  21.1 0.0 copy-done.2
  21.1 5.1 %first_step.1 = (f32[6,192,128]{2,1,0:T(8,128)S(1)}, f32[12,192,128]{2,1,0:T(8,128)S(1)}, f32[6,192,128]{2,1,0:T(8,128)S(1)}) custom-call(s32[1]{0:T(128)} %bitcast.band_ref, f32[24,192,128]{2,1,0:T(8,128)S(1)} %bitcast.10, f32[288,128]{1,0:T(8,128)S(1)} %collective-permute-done.refs_1_, f32[24,24,128]{2,1,0:T(8,128)S(1)} %collective-permute-done.1.refs_2_, ...), custom_call_target="tpu_custom_call" | custom-call | flops 1 | bytes 1 | tf_op jit(solution)/shard_map/first_step/pallas_call | solution.py:213
  26.2 0.0 copy-start.1
  26.2 2.6 %collective-permute-start.6 = (f32[6,192,128]{2,1,0:T(8,128)S(1)}, f32[6,192,128]{2,1,0:T(8,128)S(1)}, u32[]{:S(2)}, u32[]{:S(2)}) collective-permute-start(f32[6,192,128]{2,1,0:T(8,128)S(1)} %get-tuple-element.24.low_ref.refs_0_), channel_id=1, source_target_pairs={{0,28},{1,29},{2,30},{3,31},{4,0},{5,1},{6,2},{7,3},{8,4},{9,5},{1... | collective-permute-start | bytes 1769480 | tf_op jit(solution)/shard_map/ppermute | solution.py:356
  28.9 3.2 %collective-permute-done.3.halo_ref = f32[6,192,128]{2,1,0:T(8,128)S(1)} collective-permute-done((f32[6,192,128]{2,1,0:T(8,128)S(1)}, f32[6,192,128]{2,1,0:T(8,128)S(1)}, u32[]{:S(2)}, u32[]{:S(2)}) %collective-permute-start.3) | collective-permute-done | bytes 589856 | tf_op jit(solution)/shard_map/ppermute | solution.py:356
  32.1 1.1 %finish_first.1 = (f32[6,192,128]{2,1,0:T(8,128)S(1)}, f32[288,128]{1,0:T(8,128)S(1)}, f32[24,24,128]{2,1,0:T(8,128)S(1)}) custom-call(f32[6,192,128]{2,1,0:T(8,128)S(1)} %get-tuple-element.24.low_ref.refs_0_, f32[12,192,128]{2,1,0:T(8,128)S(1)} %get-tuple-element.25.middle_ref.refs_1_, f32[6,192,128]{2,1,0:T(8,128)S(1)} %get-tuple-element.26.partial_ref, ...), custom_call_target="tpu_custom_call" | custom-call | flops 1 | bytes 1 | tf_op jit(solution)/shard_map/finish_first/pallas_call | solution.py:254
  33.2 1.6 %collective-permute-start.5 = (f32[24,24,128]{2,1,0:T(8,128)S(1)}, f32[24,24,128]{2,1,0:T(8,128)S(1)}, u32[]{:S(2)}, u32[]{:S(2)}) collective-permute-start(f32[24,24,128]{2,1,0:T(8,128)S(1)} %get-tuple-element.30), channel_id=1, source_target_pairs={{0,1},{1,0},{2,3},{3,2},{4,5},{5,4},{6,7},{7,6},{8,9},{9,8},{10,11... | collective-permute-start | bytes 884744 | tf_op jit(solution)/shard_map/ppermute | solution.py:360
  34.8 1.6 %collective-permute-start.7 = (f32[6,192,128]{2,1,0:T(8,128)S(1)}, f32[6,192,128]{2,1,0:T(8,128)S(1)}, u32[]{:S(2)}, u32[]{:S(2)}) collective-permute-start(f32[6,192,128]{2,1,0:T(8,128)S(1)} %get-tuple-element.28.refs_2_), channel_id=1, source_target_pairs={{0,4},{1,5},{2,6},{3,7},{4,8},{5,9},{6,10},{7,11},{8,12},{9,13},{1... | collective-permute-start | bytes 1769480 | tf_op jit(solution)/shard_map/ppermute | solution.py:356
  36.3 2.7 %collective-permute-start.4 = (f32[288,128]{1,0:T(8,128)S(1)}, f32[288,128]{1,0:T(8,128)S(1)}, u32[]{:S(2)}, u32[]{:S(2)}) collective-permute-start(f32[288,128]{1,0:T(8,128)S(1)} %get-tuple-element.29), channel_id=1, source_target_pairs={{0,2},{1,3},{2,0},{3,1},{4,6},{5,7},{6,4},{7,5},{8,10},{9,11},{10,... | collective-permute-start | bytes 442376 | tf_op jit(solution)/shard_map/ppermute | solution.py:360
  39.1 6.3 %collective-permute-done.4.refs_3_ = f32[288,128]{1,0:T(8,128)S(1)} collective-permute-done((f32[288,128]{1,0:T(8,128)S(1)}, f32[288,128]{1,0:T(8,128)S(1)}, u32[]{:S(2)}, u32[]{:S(2)}) %collective-permute-start.4) | collective-permute-done | bytes 147488 | tf_op jit(solution)/shard_map/ppermute | solution.py:360
  45.3 0.0 collective-permute-done.5.refs_4_
  45.4 0.0 collective-permute-done.6.refs_6_
  45.4 0.0 copy-done.1
  45.4 7.0 %second_step.1 = (f32[24,192,128]{2,1,0:T(8,128)}, f32[18,48,128]{2,1,0:T(8,128)S(1)}, f32[18,48,128]{2,1,0:T(8,128)S(1)}, f32[18,48,128]{2,1,0:T(8,128)S(1)}, f...) custom-call(s32[1]{0:T(128)} %bitcast.band_ref, f32[6,192,128]{2,1,0:T(8,128)S(1)} %get-tuple-element.24.low_ref.refs_0_, ...), custom_call_target="tpu_custom_call" | custom-call | flops 1 | bytes 1 | tf_op jit(solution)/shard_map/second_step/pallas_call | solution.py:213
  52.4 0.0 collective-permute-start.10
  52.4 3.3 %collective-permute-start.8 = (f32[18,48,128]{2,1,0:T(8,128)S(1)}, f32[18,48,128]{2,1,0:T(8,128)S(1)}, u32[]{:S(2)}, u32[]{:S(2)}) collective-permute-start(f32[18,48,128]{2,1,0:T(8,128)S(1)} %get-tuple-element.35), channel_id=1, source_target_pairs={{0,32},{32,0},{64,96},{96,64},{1,33},{33,1},{65,97},{97,65},{2,34}... | collective-permute-start | bytes 1327112 | tf_op jit(solution)/shard_map/ppermute | solution.py:360
  55.7 0.3 collective-permute-start.9
  56.0 2.3 %collective-permute-done.7.halo_ref = f32[6,192,128]{2,1,0:T(8,128)S(1)} collective-permute-done((f32[6,192,128]{2,1,0:T(8,128)S(1)}, f32[6,192,128]{2,1,0:T(8,128)S(1)}, u32[]{:S(2)}, u32[]{:S(2)}) %collective-permute-start.7) | collective-permute-done | bytes 589856 | tf_op jit(solution)/shard_map/ppermute | solution.py:356
  58.3 1.1 %finish_filtered.1 = (f32[24,192,128]{2,1,0:T(8,128)}, f32[6,48,128]{2,1,0:T(8,128)S(1)}, f32[6,48,128]{2,1,0:T(8,128)S(1)}, f32[6,48,128]{2,1,0:T(8,128)S(1)}, f32[6,48,128]{2,1,0:T(8,128)S(1)}) custom-call(s32[1]{0:T(128)} %bitcast.band_ref, f32[6,192,128]{2,1,0:T(8,128)S(1)} %get-tuple-element.31.partial_ref, ...), custom_call_target="tpu_custom_call", output_to_operand_aliasing={{0}: (3, {})} | custom-call | flops 1 | bytes 1 | tf_op jit(solution)/shard_map/finish_filtered/pallas_call | solution.py:279
  59.5 0.1 collective-permute-start.11
  59.6 3.7 %collective-permute-start.12 = (f32[6,48,128]{2,1,0:T(8,128)S(1)}, f32[6,48,128]{2,1,0:T(8,128)S(1)}, u32[]{:S(2)}, u32[]{:S(2)}) collective-permute-start(f32[6,48,128]{2,1,0:T(8,128)S(1)} %get-tuple-element.40), channel_id=1, source_target_pairs={{0,64},{32,96},{64,0},{96,32},{1,65},{33,97},{65,1},{97,33},{2,66}... | collective-permute-start | bytes 442376 | tf_op jit(solution)/shard_map/ppermute | solution.py:360
  63.2 3.2 %collective-permute-done.10.refs_3_ = f32[18,48,128]{2,1,0:T(8,128)S(1)} collective-permute-done((f32[18,48,128]{2,1,0:T(8,128)S(1)}, f32[18,48,128]{2,1,0:T(8,128)S(1)}, u32[]{:S(2)}, u32[]{:S(2)}) %collective-permute-start.10) | collective-permute-done | bytes 442400 | tf_op jit(solution)/shard_map/ppermute | solution.py:360
  66.4 0.0 collective-permute-start.13
  66.4 0.0 collective-permute-done.8.refs_1_
  66.4 10.3 %collective-permute-done.9.refs_2_ = f32[18,48,128]{2,1,0:T(8,128)S(1)} collective-permute-done((f32[18,48,128]{2,1,0:T(8,128)S(1)}, f32[18,48,128]{2,1,0:T(8,128)S(1)}, u32[]{:S(2)}, u32[]{:S(2)}) %collective-permute-start.9) | collective-permute-done | bytes 442400 | tf_op jit(solution)/shard_map/ppermute | solution.py:360
  76.7 0.4 early_gram.1.before_ref
  77.0 0.0 collective-permute-done.11.refs_1_
  77.1 2.8 %collective-permute-done.12.refs_2_ = f32[6,48,128]{2,1,0:T(8,128)S(1)} collective-permute-done((f32[6,48,128]{2,1,0:T(8,128)S(1)}, f32[6,48,128]{2,1,0:T(8,128)S(1)}, u32[]{:S(2)}, u32[]{:S(2)}) %collective-permute-start.12) | collective-permute-done | bytes 147488 | tf_op jit(solution)/shard_map/ppermute | solution.py:360
  79.8 2.4 %collective-permute-done.13.refs_3_ = f32[6,48,128]{2,1,0:T(8,128)S(1)} collective-permute-done((f32[6,48,128]{2,1,0:T(8,128)S(1)}, f32[6,48,128]{2,1,0:T(8,128)S(1)}, u32[]{:S(2)}, u32[]{:S(2)}) %collective-permute-start.13) | collective-permute-done | bytes 147488 | tf_op jit(solution)/shard_map/ppermute | solution.py:360
  82.2 0.2 late_gram.1
  82.5 18.5 %all_to_all.9 = f32[128,1,128]{2,1,0:T(1,128)S(1)} all-to-all(f32[128,1,128]{2,1,0:T(1,128)S(1)} %bitcast.14), channel_id=1, replica_groups=mesh['band'=4,'space'=32] {'band','space'}, dimensions={0} | all-to-all | bytes 131072 | tf_op jit(solution)/shard_map/all_to_all | solution.py:392
  101.0 0.2 reduce_sum.9
  101.1 0.7 div.6
  (1 shorter events, 0.0 us)
Async XLA Ops:
  1.7 19.4 %collective-permute-start.2 = (f32[6,192,128]{2,1,0:T(8,128)S(1)}, f32[6,192,128]{2,1,0:T(8,128)S(1)}, u32[]{:S(2)}, u32[]{:S(2)}) collective-permute-start(f32[6,192,128]{2,1,0:T(8,128)S(1)} %slice_bitcast_fusion), channel_id=1, source_target_pairs={{0,4},{1,5},{2,6},{3,7},{4,8},{5,9},{6,10},{7,11},{8,12},{9,13},{1... | collective-permute-start | bytes 1769480 | tf_op jit(solution)/shard_map/ppermute | solution.py:356
  3.5 1.7 %copy-start = (f32[1,1,24,192,128]{4,3,2,1,0:T(8,128)S(1)}, f32[1,1,24,192,128]{4,3,2,1,0:T(8,128)}, u32[]{:S(2)}) copy-start(f32[1,1,24,192,128]{4,3,2,1,0:T(8,128)} %param.2) | copy-start | bytes 7077892
  5.1 16.0 %copy-start.2 = (f32[1,24,192,128]{3,2,1,0:T(8,128)S(1)}, f32[1,24,192,128]{3,2,1,0:T(8,128)}, u32[]{:S(2)}) copy-start(f32[1,24,192,128]{3,2,1,0:T(8,128)} %param.3) | copy-start | bytes 7077892
  6.0 13.9 %collective-permute-start.1 = (f32[24,24,128]{2,1,0:T(8,128)S(1)}, f32[24,24,128]{2,1,0:T(8,128)S(1)}, u32[]{:S(2)}, u32[]{:S(2)}) collective-permute-start(f32[24,24,128]{2,1,0:T(8,128)S(1)} %get-tuple-element.23), channel_id=1, source_target_pairs={{0,1},{1,0},{2,3},{3,2},{4,5},{5,4},{6,7},{7,6},{8,9},{9,8},{10,11... | collective-permute-start | bytes 884744 | tf_op jit(solution)/shard_map/ppermute | solution.py:360
  7.5 24.6 %collective-permute-start.3 = (f32[6,192,128]{2,1,0:T(8,128)S(1)}, f32[6,192,128]{2,1,0:T(8,128)S(1)}, u32[]{:S(2)}, u32[]{:S(2)}) collective-permute-start(f32[6,192,128]{2,1,0:T(8,128)S(1)} %get-tuple-element.27), channel_id=1, source_target_pairs={{0,28},{1,29},{2,30},{3,31},{4,0},{5,1},{6,2},{7,3},{8,4},{9,5},{1... | collective-permute-start | bytes 1769480 | tf_op jit(solution)/shard_map/ppermute | solution.py:356
  11.0 8.8 %collective-permute-start = (f32[288,128]{1,0:T(8,128)S(1)}, f32[288,128]{1,0:T(8,128)S(1)}, u32[]{:S(2)}, u32[]{:S(2)}) collective-permute-start(f32[288,128]{1,0:T(8,128)S(1)} %get-tuple-element.22), channel_id=1, source_target_pairs={{0,2},{1,3},{2,0},{3,1},{4,6},{5,7},{6,4},{7,5},{8,10},{9,11},{10,... | collective-permute-start | bytes 442376 | tf_op jit(solution)/shard_map/ppermute | solution.py:360
  26.2 19.1 %copy-start.1 = (f32[1,1,24,192,128]{4,3,2,1,0:T(8,128)S(1)}, f32[1,1,24,192,128]{4,3,2,1,0:T(8,128)}, u32[]{:S(2)}) copy-start(f32[1,1,24,192,128]{4,3,2,1,0:T(8,128)} %param.2) | copy-start | bytes 7077892
  26.2 19.1 %collective-permute-start.6 = (f32[6,192,128]{2,1,0:T(8,128)S(1)}, f32[6,192,128]{2,1,0:T(8,128)S(1)}, u32[]{:S(2)}, u32[]{:S(2)}) collective-permute-start(f32[6,192,128]{2,1,0:T(8,128)S(1)} %get-tuple-element.24.low_ref.refs_0_), channel_id=1, source_target_pairs={{0,28},{1,29},{2,30},{3,31},{4,0},{5,1},{6,2},{7,3},{8,4},{9,5},{1... | collective-permute-start | bytes 1769480 | tf_op jit(solution)/shard_map/ppermute | solution.py:356
  33.2 12.2 %collective-permute-start.5 = (f32[24,24,128]{2,1,0:T(8,128)S(1)}, f32[24,24,128]{2,1,0:T(8,128)S(1)}, u32[]{:S(2)}, u32[]{:S(2)}) collective-permute-start(f32[24,24,128]{2,1,0:T(8,128)S(1)} %get-tuple-element.30), channel_id=1, source_target_pairs={{0,1},{1,0},{2,3},{3,2},{4,5},{5,4},{6,7},{7,6},{8,9},{9,8},{10,11... | collective-permute-start | bytes 884744 | tf_op jit(solution)/shard_map/ppermute | solution.py:360
  34.8 23.6 %collective-permute-start.7 = (f32[6,192,128]{2,1,0:T(8,128)S(1)}, f32[6,192,128]{2,1,0:T(8,128)S(1)}, u32[]{:S(2)}, u32[]{:S(2)}) collective-permute-start(f32[6,192,128]{2,1,0:T(8,128)S(1)} %get-tuple-element.28.refs_2_), channel_id=1, source_target_pairs={{0,4},{1,5},{2,6},{3,7},{4,8},{5,9},{6,10},{7,11},{8,12},{9,13},{1... | collective-permute-start | bytes 1769480 | tf_op jit(solution)/shard_map/ppermute | solution.py:356
  36.3 9.0 %collective-permute-start.4 = (f32[288,128]{1,0:T(8,128)S(1)}, f32[288,128]{1,0:T(8,128)S(1)}, u32[]{:S(2)}, u32[]{:S(2)}) collective-permute-start(f32[288,128]{1,0:T(8,128)S(1)} %get-tuple-element.29), channel_id=1, source_target_pairs={{0,2},{1,3},{2,0},{3,1},{4,6},{5,7},{6,4},{7,5},{8,10},{9,11},{10,... | collective-permute-start | bytes 442376 | tf_op jit(solution)/shard_map/ppermute | solution.py:360
  52.4 14.0 %collective-permute-start.10 = (f32[18,48,128]{2,1,0:T(8,128)S(1)}, f32[18,48,128]{2,1,0:T(8,128)S(1)}, u32[]{:S(2)}, u32[]{:S(2)}) collective-permute-start(f32[18,48,128]{2,1,0:T(8,128)S(1)} %get-tuple-element.37), channel_id=1, source_target_pairs={{0,96},{32,64},{64,32},{96,0},{1,97},{33,65},{65,33},{97,1},{2,98}... | collective-permute-start | bytes 1327112 | tf_op jit(solution)/shard_map/ppermute | solution.py:360
  52.4 14.0 %collective-permute-start.8 = (f32[18,48,128]{2,1,0:T(8,128)S(1)}, f32[18,48,128]{2,1,0:T(8,128)S(1)}, u32[]{:S(2)}, u32[]{:S(2)}) collective-permute-start(f32[18,48,128]{2,1,0:T(8,128)S(1)} %get-tuple-element.35), channel_id=1, source_target_pairs={{0,32},{32,0},{64,96},{96,64},{1,33},{33,1},{65,97},{97,65},{2,34}... | collective-permute-start | bytes 1327112 | tf_op jit(solution)/shard_map/ppermute | solution.py:360
  55.7 21.0 %collective-permute-start.9 = (f32[18,48,128]{2,1,0:T(8,128)S(1)}, f32[18,48,128]{2,1,0:T(8,128)S(1)}, u32[]{:S(2)}, u32[]{:S(2)}) collective-permute-start(f32[18,48,128]{2,1,0:T(8,128)S(1)} %get-tuple-element.36), channel_id=1, source_target_pairs={{0,64},{32,96},{64,0},{96,32},{1,65},{33,97},{65,1},{97,33},{2,66}... | collective-permute-start | bytes 1327112 | tf_op jit(solution)/shard_map/ppermute | solution.py:360
  59.5 17.6 %collective-permute-start.11 = (f32[6,48,128]{2,1,0:T(8,128)S(1)}, f32[6,48,128]{2,1,0:T(8,128)S(1)}, u32[]{:S(2)}, u32[]{:S(2)}) collective-permute-start(f32[6,48,128]{2,1,0:T(8,128)S(1)} %get-tuple-element.39), channel_id=1, source_target_pairs={{0,32},{32,0},{64,96},{96,64},{1,33},{33,1},{65,97},{97,65},{2,34}... | collective-permute-start | bytes 442376 | tf_op jit(solution)/shard_map/ppermute | solution.py:360
  59.6 20.3 %collective-permute-start.12 = (f32[6,48,128]{2,1,0:T(8,128)S(1)}, f32[6,48,128]{2,1,0:T(8,128)S(1)}, u32[]{:S(2)}, u32[]{:S(2)}) collective-permute-start(f32[6,48,128]{2,1,0:T(8,128)S(1)} %get-tuple-element.40), channel_id=1, source_target_pairs={{0,64},{32,96},{64,0},{96,32},{1,65},{33,97},{65,1},{97,33},{2,66}... | collective-permute-start | bytes 442376 | tf_op jit(solution)/shard_map/ppermute | solution.py:360
  66.4 15.8 %collective-permute-start.13 = (f32[6,48,128]{2,1,0:T(8,128)S(1)}, f32[6,48,128]{2,1,0:T(8,128)S(1)}, u32[]{:S(2)}, u32[]{:S(2)}) collective-permute-start(f32[6,48,128]{2,1,0:T(8,128)S(1)} %get-tuple-element.41), channel_id=1, source_target_pairs={{0,96},{32,64},{64,32},{96,0},{1,97},{33,65},{65,33},{97,1},{2,98}... | collective-permute-start | bytes 442376 | tf_op jit(solution)/shard_map/ppermute | solution.py:360

commit v5 on v4

--- a/solution.py
+++ b/solution.py
@@ -71,8 +71,8 @@
         count, rows = piece.shape[0], piece.shape[1]
         for p in range(count):
             base = 2 * REACH * (at + p)
-            y_ref[base : base + REACH, :] = piece[p, 0:REACH, :]
-            y_ref[base + REACH : base + 2 * REACH, :] = piece[p, rows - REACH : rows, :]
+            y_ref[base : base + REACH, :] = piece[p, 0:8, :][0:REACH]
+            y_ref[base + REACH : base + 2 * REACH, :] = piece[p, rows - 8 : rows, :][8 - REACH : 8]
         total = None
         for group in range(rows // ROWS):
             block = piece[:, group * ROWS : (group + 1) * ROWS, :].reshape(count * ROWS, LANES)
@@ -89,7 +89,7 @@
 
 def face_shapes(planes):
     return [
-        jax.ShapeDtypeStruct((2 * REACH * planes, LANES), jnp.float32),
+        jax.ShapeDtypeStruct((2 * REACH * planes + 8, LANES), jnp.float32),
         jax.ShapeDtypeStruct((planes, ROWS, LANES), jnp.float32),
     ]
 
@@ -139,12 +139,12 @@
         @pl.when(group == 0)
         def _():
             for p, (face, base) in enumerate(face_of):
-                extended[p, 8 - REACH : 8, :] = face[base + REACH : base + 2 * REACH, :]
+                extended[p, 0:8, :] = face[base + 2 * REACH - 8 : base + 2 * REACH, :]
 
         @pl.when(group == rows // ROWS - 1)
         def _():
             for p, (face, base) in enumerate(face_of):
-                extended[p, 8 + ROWS : 8 + ROWS + REACH, :] = face[base : base + REACH, :]
+                extended[p, 8 + ROWS : 16 + ROWS, :] = face[base : base + 8, :]
 
         own_high, own_low = split(extended[:, 8 : 8 + ROWS, :].reshape(planes * ROWS, LANES))
         packed = jnp.concatenate([z[...] for z in z_refs], axis=0).reshape(planes * ROWS, LANES)

time: 103 us -> 103 us (level)
  no operation moved by 1% of the time
where the time goes in v5:
time: 103 us; the launch traced here: 102 us
  waiting for transfers between devices  37.7 us (37%)
  starting transfers between devices  25.6 us (25%)
  blocking collectives  18.4 us (18%)
  Pallas kernels  15.8 us (15%)
  local copies, waits for them, and re-layouts  3.44 us (3%)
    ppermute x10, waiting for transfers between devices, swapped(): lax.ppermute(array, axis, [(i, i ^ bit) for i in range(lax.axis_size(axis...  31.4 us
    all_to_all x1, blocking collectives, on_device(): everyone = lax.all_to_all(rows, both, 0, 0, tiled=True)  18.4 us
    ppermute x10, starting transfers between devices, swapped(): lax.ppermute(array, axis, [(i, i ^ bit) for i in range(lax.axis_size(axis...  16.1 us
    pallas_call x2, Pallas kernels, apply_stencil(): pl.pallas_call(functools.partial(stencil_kernel, counts, sections, second...  12.2 us
    ppermute x4, starting transfers between devices, shifted(): lax.ppermute(array, 'space', [(i, (i + by) % peers) for i in range(peers)])  9.48 us
    ppermute x4, waiting for transfers between devices, shifted(): lax.ppermute(array, 'space', [(i, (i + by) % peers) for i in range(peers)])  6.34 us
  transfers between devices with their start and end apart: 14, of which 9 were waited for; matrix products, arithmetic and copies ran while one was open for 0% of the time, Pallas kernels for 15%

profile of v5, /device:TPU:0, one launch (start us, length us, event | category | flops | bytes accessed | tf_op | source)
XLA Modules:
  0.0 101.8 jit_solution(12124074126647602409)
XLA Ops:
  0.6 1.1 %slice_bitcast_fusion = f32[6,192,128]{2,1,0:T(8,128)S(1)} fusion(f32[1,1,24,192,128]{4,3,2,1,0:T(8,128)} %param.2), kind=kLoop, calls=%fused_computation | loop fusion | bytes 1179648 | tf_op jit(solution)/shard_map/slice | solution.py:376
  1.7 1.7 %collective-permute-start.2 = (f32[6,192,128]{2,1,0:T(8,128)S(1)}, f32[6,192,128]{2,1,0:T(8,128)S(1)}, u32[]{:S(2)}, u32[]{:S(2)}) collective-permute-start(f32[6,192,128]{2,1,0:T(8,128)S(1)} %slice_bitcast_fusion), channel_id=1, source_target_pairs={{0,4},{1,5},{2,6},{3,7},{4,8},{5,9},{6,10},{7,11},{8,12},{9,13},{1... | collective-permute-start | bytes 1769480 | tf_op jit(solution)/shard_map/ppermute | solution.py:356
  3.5 0.0 copy-start
  3.5 1.7 %copy-done = f32[1,1,24,192,128]{4,3,2,1,0:T(8,128)S(1)} copy-done((f32[1,1,24,192,128]{4,3,2,1,0:T(8,128)S(1)}, f32[1,1,24,192,128]{4,3,2,1,0:T(8,128)}, u32[]{:S(2)}) %copy-start) | copy-done | bytes 2359320
  5.1 0.0 copy-start.2
  5.1 0.8 entry.1
  5.9 1.6 %collective-permute-start.1 = (f32[24,24,128]{2,1,0:T(8,128)S(1)}, f32[24,24,128]{2,1,0:T(8,128)S(1)}, u32[]{:S(2)}, u32[]{:S(2)}) collective-permute-start(f32[24,24,128]{2,1,0:T(8,128)S(1)} %get-tuple-element.23), channel_id=1, source_target_pairs={{0,1},{1,0},{2,3},{3,2},{4,5},{5,4},{6,7},{7,6},{8,9},{9,8},{10,11... | collective-permute-start | bytes 884744 | tf_op jit(solution)/shard_map/ppermute | solution.py:360
  7.5 3.5 %collective-permute-start.3 = (f32[6,192,128]{2,1,0:T(8,128)S(1)}, f32[6,192,128]{2,1,0:T(8,128)S(1)}, u32[]{:S(2)}, u32[]{:S(2)}) collective-permute-start(f32[6,192,128]{2,1,0:T(8,128)S(1)} %get-tuple-element.27), channel_id=1, source_target_pairs={{0,28},{1,29},{2,30},{3,31},{4,0},{5,1},{6,2},{7,3},{8,4},{9,5},{1... | collective-permute-start | bytes 1769480 | tf_op jit(solution)/shard_map/ppermute | solution.py:356
  11.0 2.7 %collective-permute-start = (f32[296,128]{1,0:T(8,128)S(1)}, f32[296,128]{1,0:T(8,128)S(1)}, u32[]{:S(2)}, u32[]{:S(2)}) collective-permute-start(f32[296,128]{1,0:T(8,128)S(1)} %get-tuple-element.22), channel_id=1, source_target_pairs={{0,2},{1,3},{2,0},{3,1},{4,6},{5,7},{6,4},{7,5},{8,10},{9,11},{10,... | collective-permute-start | bytes 454664 | tf_op jit(solution)/shard_map/ppermute | solution.py:360
  13.7 6.2 %collective-permute-done.refs_1_ = f32[296,128]{1,0:T(8,128)S(1)} collective-permute-done((f32[296,128]{1,0:T(8,128)S(1)}, f32[296,128]{1,0:T(8,128)S(1)}, u32[]{:S(2)}, u32[]{:S(2)}) %collective-permute-start) | collective-permute-done | bytes 151584 | tf_op jit(solution)/shard_map/ppermute | solution.py:360
  19.9 0.0 collective-permute-done.1.refs_2_
  19.9 1.2 %collective-permute-done.2.refs_4_ = f32[6,192,128]{2,1,0:T(8,128)S(1)} collective-permute-done((f32[6,192,128]{2,1,0:T(8,128)S(1)}, f32[6,192,128]{2,1,0:T(8,128)S(1)}, u32[]{:S(2)}, u32[]{:S(2)}) %collective-permute-start.2) | collective-permute-done | bytes 589856 | tf_op jit(solution)/shard_map/ppermute | solution.py:356
  21.1 0.0 copy-done.2
  21.1 5.1 %first_step.1 = (f32[6,192,128]{2,1,0:T(8,128)S(1)}, f32[12,192,128]{2,1,0:T(8,128)S(1)}, f32[6,192,128]{2,1,0:T(8,128)S(1)}) custom-call(s32[1]{0:T(128)} %bitcast.band_ref, f32[24,192,128]{2,1,0:T(8,128)S(1)} %bitcast.10, f32[296,128]{1,0:T(8,128)S(1)} %collective-permute-done.refs_1_, f32[24,24,128]{2,1,0:T(8,128)S(1)} %collective-permute-done.1.refs_2_, ...), custom_call_target="tpu_custom_call" | custom-call | flops 1 | bytes 1 | tf_op jit(solution)/shard_map/first_step/pallas_call | solution.py:213
  26.2 0.0 copy-start.1
  26.3 2.7 %collective-permute-start.6 = (f32[6,192,128]{2,1,0:T(8,128)S(1)}, f32[6,192,128]{2,1,0:T(8,128)S(1)}, u32[]{:S(2)}, u32[]{:S(2)}) collective-permute-start(f32[6,192,128]{2,1,0:T(8,128)S(1)} %get-tuple-element.24.low_ref.refs_0_), channel_id=1, source_target_pairs={{0,28},{1,29},{2,30},{3,31},{4,0},{5,1},{6,2},{7,3},{8,4},{9,5},{1... | collective-permute-start | bytes 1769480 | tf_op jit(solution)/shard_map/ppermute | solution.py:356
  28.9 3.2 %collective-permute-done.3.halo_ref = f32[6,192,128]{2,1,0:T(8,128)S(1)} collective-permute-done((f32[6,192,128]{2,1,0:T(8,128)S(1)}, f32[6,192,128]{2,1,0:T(8,128)S(1)}, u32[]{:S(2)}, u32[]{:S(2)}) %collective-permute-start.3) | collective-permute-done | bytes 589856 | tf_op jit(solution)/shard_map/ppermute | solution.py:356
  32.1 1.1 %finish_first.1 = (f32[6,192,128]{2,1,0:T(8,128)S(1)}, f32[296,128]{1,0:T(8,128)S(1)}, f32[24,24,128]{2,1,0:T(8,128)S(1)}) custom-call(f32[6,192,128]{2,1,0:T(8,128)S(1)} %get-tuple-element.24.low_ref.refs_0_, f32[12,192,128]{2,1,0:T(8,128)S(1)} %get-tuple-element.25.middle_ref.refs_1_, f32[6,192,128]{2,1,0:T(8,128)S(1)} %get-tuple-element.26.partial_ref, ...), custom_call_target="tpu_custom_call" | custom-call | flops 1 | bytes 1 | tf_op jit(solution)/shard_map/finish_first/pallas_call | solution.py:254
  33.2 1.6 %collective-permute-start.5 = (f32[24,24,128]{2,1,0:T(8,128)S(1)}, f32[24,24,128]{2,1,0:T(8,128)S(1)}, u32[]{:S(2)}, u32[]{:S(2)}) collective-permute-start(f32[24,24,128]{2,1,0:T(8,128)S(1)} %get-tuple-element.30), channel_id=1, source_target_pairs={{0,1},{1,0},{2,3},{3,2},{4,5},{5,4},{6,7},{7,6},{8,9},{9,8},{10,11... | collective-permute-start | bytes 884744 | tf_op jit(solution)/shard_map/ppermute | solution.py:360
  34.8 2.7 %collective-permute-start.4 = (f32[296,128]{1,0:T(8,128)S(1)}, f32[296,128]{1,0:T(8,128)S(1)}, u32[]{:S(2)}, u32[]{:S(2)}) collective-permute-start(f32[296,128]{1,0:T(8,128)S(1)} %get-tuple-element.29), channel_id=1, source_target_pairs={{0,2},{1,3},{2,0},{3,1},{4,6},{5,7},{6,4},{7,5},{8,10},{9,11},{10,... | collective-permute-start | bytes 454664 | tf_op jit(solution)/shard_map/ppermute | solution.py:360
  37.5 1.6 %collective-permute-start.7 = (f32[6,192,128]{2,1,0:T(8,128)S(1)}, f32[6,192,128]{2,1,0:T(8,128)S(1)}, u32[]{:S(2)}, u32[]{:S(2)}) collective-permute-start(f32[6,192,128]{2,1,0:T(8,128)S(1)} %get-tuple-element.28.refs_2_), channel_id=1, source_target_pairs={{0,4},{1,5},{2,6},{3,7},{4,8},{5,9},{6,10},{7,11},{8,12},{9,13},{1... | collective-permute-start | bytes 1769480 | tf_op jit(solution)/shard_map/ppermute | solution.py:356
  39.1 6.4 %collective-permute-done.4.refs_3_ = f32[296,128]{1,0:T(8,128)S(1)} collective-permute-done((f32[296,128]{1,0:T(8,128)S(1)}, f32[296,128]{1,0:T(8,128)S(1)}, u32[]{:S(2)}, u32[]{:S(2)}) %collective-permute-start.4) | collective-permute-done | bytes 151584 | tf_op jit(solution)/shard_map/ppermute | solution.py:360
  45.5 0.0 collective-permute-done.5.refs_4_
  45.5 0.0 collective-permute-done.6.refs_6_
  45.5 0.0 copy-done.1
  45.5 7.1 %second_step.1 = (f32[24,192,128]{2,1,0:T(8,128)}, f32[18,48,128]{2,1,0:T(8,128)S(1)}, f32[18,48,128]{2,1,0:T(8,128)S(1)}, f32[18,48,128]{2,1,0:T(8,128)S(1)}, f...) custom-call(s32[1]{0:T(128)} %bitcast.band_ref, f32[6,192,128]{2,1,0:T(8,128)S(1)} %get-tuple-element.24.low_ref.refs_0_, ...), custom_call_target="tpu_custom_call" | custom-call | flops 1 | bytes 1 | tf_op jit(solution)/shard_map/second_step/pallas_call | solution.py:213
  52.5 0.0 collective-permute-start.10
  52.5 3.3 %collective-permute-start.8 = (f32[18,48,128]{2,1,0:T(8,128)S(1)}, f32[18,48,128]{2,1,0:T(8,128)S(1)}, u32[]{:S(2)}, u32[]{:S(2)}) collective-permute-start(f32[18,48,128]{2,1,0:T(8,128)S(1)} %get-tuple-element.35), channel_id=1, source_target_pairs={{0,32},{32,0},{64,96},{96,64},{1,33},{33,1},{65,97},{97,65},{2,34}... | collective-permute-start | bytes 1327112 | tf_op jit(solution)/shard_map/ppermute | solution.py:360
  55.8 0.3 collective-permute-start.9
  56.2 2.0 %collective-permute-done.7.halo_ref = f32[6,192,128]{2,1,0:T(8,128)S(1)} collective-permute-done((f32[6,192,128]{2,1,0:T(8,128)S(1)}, f32[6,192,128]{2,1,0:T(8,128)S(1)}, u32[]{:S(2)}, u32[]{:S(2)}) %collective-permute-start.7) | collective-permute-done | bytes 589856 | tf_op jit(solution)/shard_map/ppermute | solution.py:356
  58.2 1.1 %finish_filtered.1 = (f32[24,192,128]{2,1,0:T(8,128)}, f32[6,48,128]{2,1,0:T(8,128)S(1)}, f32[6,48,128]{2,1,0:T(8,128)S(1)}, f32[6,48,128]{2,1,0:T(8,128)S(1)}, f32[6,48,128]{2,1,0:T(8,128)S(1)}) custom-call(s32[1]{0:T(128)} %bitcast.band_ref, f32[6,192,128]{2,1,0:T(8,128)S(1)} %get-tuple-element.31.partial_ref, ...), custom_call_target="tpu_custom_call", output_to_operand_aliasing={{0}: (3, {})} | custom-call | flops 1 | bytes 1 | tf_op jit(solution)/shard_map/finish_filtered/pallas_call | solution.py:279
  59.3 0.1 collective-permute-start.11
  59.4 3.8 %collective-permute-start.12 = (f32[6,48,128]{2,1,0:T(8,128)S(1)}, f32[6,48,128]{2,1,0:T(8,128)S(1)}, u32[]{:S(2)}, u32[]{:S(2)}) collective-permute-start(f32[6,48,128]{2,1,0:T(8,128)S(1)} %get-tuple-element.40), channel_id=1, source_target_pairs={{0,64},{32,96},{64,0},{96,32},{1,65},{33,97},{65,1},{97,33},{2,66}... | collective-permute-start | bytes 442376 | tf_op jit(solution)/shard_map/ppermute | solution.py:360
  63.2 3.3 %collective-permute-done.10.refs_3_ = f32[18,48,128]{2,1,0:T(8,128)S(1)} collective-permute-done((f32[18,48,128]{2,1,0:T(8,128)S(1)}, f32[18,48,128]{2,1,0:T(8,128)S(1)}, u32[]{:S(2)}, u32[]{:S(2)}) %collective-permute-start.10) | collective-permute-done | bytes 442400 | tf_op jit(solution)/shard_map/ppermute | solution.py:360
  66.6 0.0 collective-permute-start.13
  66.6 0.0 collective-permute-done.8.refs_1_
  66.6 10.0 %collective-permute-done.9.refs_2_ = f32[18,48,128]{2,1,0:T(8,128)S(1)} collective-permute-done((f32[18,48,128]{2,1,0:T(8,128)S(1)}, f32[18,48,128]{2,1,0:T(8,128)S(1)}, u32[]{:S(2)}, u32[]{:S(2)}) %collective-permute-start.9) | collective-permute-done | bytes 442400 | tf_op jit(solution)/shard_map/ppermute | solution.py:360
  76.5 0.4 early_gram.1.before_ref
  76.9 0.0 collective-permute-done.11.refs_1_
  76.9 2.8 %collective-permute-done.12.refs_2_ = f32[6,48,128]{2,1,0:T(8,128)S(1)} collective-permute-done((f32[6,48,128]{2,1,0:T(8,128)S(1)}, f32[6,48,128]{2,1,0:T(8,128)S(1)}, u32[]{:S(2)}, u32[]{:S(2)}) %collective-permute-start.12) | collective-permute-done | bytes 147488 | tf_op jit(solution)/shard_map/ppermute | solution.py:360
  79.7 2.7 %collective-permute-done.13.refs_3_ = f32[6,48,128]{2,1,0:T(8,128)S(1)} collective-permute-done((f32[6,48,128]{2,1,0:T(8,128)S(1)}, f32[6,48,128]{2,1,0:T(8,128)S(1)}, u32[]{:S(2)}, u32[]{:S(2)}) %collective-permute-start.13) | collective-permute-done | bytes 147488 | tf_op jit(solution)/shard_map/ppermute | solution.py:360
  82.4 0.2 late_gram.1
  82.6 18.4 %all_to_all.9 = f32[128,1,128]{2,1,0:T(1,128)S(1)} all-to-all(f32[128,1,128]{2,1,0:T(1,128)S(1)} %bitcast.14), channel_id=1, replica_groups=mesh['band'=4,'space'=32] {'band','space'}, dimensions={0} | all-to-all | bytes 131072 | tf_op jit(solution)/shard_map/all_to_all | solution.py:392
  101.0 0.2 reduce_sum.9
  101.1 0.7 div.6
  (1 shorter events, 0.0 us)
Async XLA Ops:
  1.7 19.4 %collective-permute-start.2 = (f32[6,192,128]{2,1,0:T(8,128)S(1)}, f32[6,192,128]{2,1,0:T(8,128)S(1)}, u32[]{:S(2)}, u32[]{:S(2)}) collective-permute-start(f32[6,192,128]{2,1,0:T(8,128)S(1)} %slice_bitcast_fusion), channel_id=1, source_target_pairs={{0,4},{1,5},{2,6},{3,7},{4,8},{5,9},{6,10},{7,11},{8,12},{9,13},{1... | collective-permute-start | bytes 1769480 | tf_op jit(solution)/shard_map/ppermute | solution.py:356
  3.5 1.7 %copy-start = (f32[1,1,24,192,128]{4,3,2,1,0:T(8,128)S(1)}, f32[1,1,24,192,128]{4,3,2,1,0:T(8,128)}, u32[]{:S(2)}) copy-start(f32[1,1,24,192,128]{4,3,2,1,0:T(8,128)} %param.2) | copy-start | bytes 7077892
  5.1 16.0 %copy-start.2 = (f32[1,24,192,128]{3,2,1,0:T(8,128)S(1)}, f32[1,24,192,128]{3,2,1,0:T(8,128)}, u32[]{:S(2)}) copy-start(f32[1,24,192,128]{3,2,1,0:T(8,128)} %param.3) | copy-start | bytes 7077892
  5.9 14.0 %collective-permute-start.1 = (f32[24,24,128]{2,1,0:T(8,128)S(1)}, f32[24,24,128]{2,1,0:T(8,128)S(1)}, u32[]{:S(2)}, u32[]{:S(2)}) collective-permute-start(f32[24,24,128]{2,1,0:T(8,128)S(1)} %get-tuple-element.23), channel_id=1, source_target_pairs={{0,1},{1,0},{2,3},{3,2},{4,5},{5,4},{6,7},{7,6},{8,9},{9,8},{10,11... | collective-permute-start | bytes 884744 | tf_op jit(solution)/shard_map/ppermute | solution.py:360
  7.5 24.6 %collective-permute-start.3 = (f32[6,192,128]{2,1,0:T(8,128)S(1)}, f32[6,192,128]{2,1,0:T(8,128)S(1)}, u32[]{:S(2)}, u32[]{:S(2)}) collective-permute-start(f32[6,192,128]{2,1,0:T(8,128)S(1)} %get-tuple-element.27), channel_id=1, source_target_pairs={{0,28},{1,29},{2,30},{3,31},{4,0},{5,1},{6,2},{7,3},{8,4},{9,5},{1... | collective-permute-start | bytes 1769480 | tf_op jit(solution)/shard_map/ppermute | solution.py:356
  11.0 8.9 %collective-permute-start = (f32[296,128]{1,0:T(8,128)S(1)}, f32[296,128]{1,0:T(8,128)S(1)}, u32[]{:S(2)}, u32[]{:S(2)}) collective-permute-start(f32[296,128]{1,0:T(8,128)S(1)} %get-tuple-element.22), channel_id=1, source_target_pairs={{0,2},{1,3},{2,0},{3,1},{4,6},{5,7},{6,4},{7,5},{8,10},{9,11},{10,... | collective-permute-start | bytes 454664 | tf_op jit(solution)/shard_map/ppermute | solution.py:360
  26.2 19.2 %copy-start.1 = (f32[1,1,24,192,128]{4,3,2,1,0:T(8,128)S(1)}, f32[1,1,24,192,128]{4,3,2,1,0:T(8,128)}, u32[]{:S(2)}) copy-start(f32[1,1,24,192,128]{4,3,2,1,0:T(8,128)} %param.2) | copy-start | bytes 7077892
  26.3 19.2 %collective-permute-start.6 = (f32[6,192,128]{2,1,0:T(8,128)S(1)}, f32[6,192,128]{2,1,0:T(8,128)S(1)}, u32[]{:S(2)}, u32[]{:S(2)}) collective-permute-start(f32[6,192,128]{2,1,0:T(8,128)S(1)} %get-tuple-element.24.low_ref.refs_0_), channel_id=1, source_target_pairs={{0,28},{1,29},{2,30},{3,31},{4,0},{5,1},{6,2},{7,3},{8,4},{9,5},{1... | collective-permute-start | bytes 1769480 | tf_op jit(solution)/shard_map/ppermute | solution.py:356
  33.2 12.3 %collective-permute-start.5 = (f32[24,24,128]{2,1,0:T(8,128)S(1)}, f32[24,24,128]{2,1,0:T(8,128)S(1)}, u32[]{:S(2)}, u32[]{:S(2)}) collective-permute-start(f32[24,24,128]{2,1,0:T(8,128)S(1)} %get-tuple-element.30), channel_id=1, source_target_pairs={{0,1},{1,0},{2,3},{3,2},{4,5},{5,4},{6,7},{7,6},{8,9},{9,8},{10,11... | collective-permute-start | bytes 884744 | tf_op jit(solution)/shard_map/ppermute | solution.py:360
  34.8 10.7 %collective-permute-start.4 = (f32[296,128]{1,0:T(8,128)S(1)}, f32[296,128]{1,0:T(8,128)S(1)}, u32[]{:S(2)}, u32[]{:S(2)}) collective-permute-start(f32[296,128]{1,0:T(8,128)S(1)} %get-tuple-element.29), channel_id=1, source_target_pairs={{0,2},{1,3},{2,0},{3,1},{4,6},{5,7},{6,4},{7,5},{8,10},{9,11},{10,... | collective-permute-start | bytes 454664 | tf_op jit(solution)/shard_map/ppermute | solution.py:360
  37.5 20.7 %collective-permute-start.7 = (f32[6,192,128]{2,1,0:T(8,128)S(1)}, f32[6,192,128]{2,1,0:T(8,128)S(1)}, u32[]{:S(2)}, u32[]{:S(2)}) collective-permute-start(f32[6,192,128]{2,1,0:T(8,128)S(1)} %get-tuple-element.28.refs_2_), channel_id=1, source_target_pairs={{0,4},{1,5},{2,6},{3,7},{4,8},{5,9},{6,10},{7,11},{8,12},{9,13},{1... | collective-permute-start | bytes 1769480 | tf_op jit(solution)/shard_map/ppermute | solution.py:356
  52.5 14.0 %collective-permute-start.10 = (f32[18,48,128]{2,1,0:T(8,128)S(1)}, f32[18,48,128]{2,1,0:T(8,128)S(1)}, u32[]{:S(2)}, u32[]{:S(2)}) collective-permute-start(f32[18,48,128]{2,1,0:T(8,128)S(1)} %get-tuple-element.37), channel_id=1, source_target_pairs={{0,96},{32,64},{64,32},{96,0},{1,97},{33,65},{65,33},{97,1},{2,98}... | collective-permute-start | bytes 1327112 | tf_op jit(solution)/shard_map/ppermute | solution.py:360
  52.5 14.0 %collective-permute-start.8 = (f32[18,48,128]{2,1,0:T(8,128)S(1)}, f32[18,48,128]{2,1,0:T(8,128)S(1)}, u32[]{:S(2)}, u32[]{:S(2)}) collective-permute-start(f32[18,48,128]{2,1,0:T(8,128)S(1)} %get-tuple-element.35), channel_id=1, source_target_pairs={{0,32},{32,0},{64,96},{96,64},{1,33},{33,1},{65,97},{97,65},{2,34}... | collective-permute-start | bytes 1327112 | tf_op jit(solution)/shard_map/ppermute | solution.py:360
  55.8 20.7 %collective-permute-start.9 = (f32[18,48,128]{2,1,0:T(8,128)S(1)}, f32[18,48,128]{2,1,0:T(8,128)S(1)}, u32[]{:S(2)}, u32[]{:S(2)}) collective-permute-start(f32[18,48,128]{2,1,0:T(8,128)S(1)} %get-tuple-element.36), channel_id=1, source_target_pairs={{0,64},{32,96},{64,0},{96,32},{1,65},{33,97},{65,1},{97,33},{2,66}... | collective-permute-start | bytes 1327112 | tf_op jit(solution)/shard_map/ppermute | solution.py:360
  59.3 17.6 %collective-permute-start.11 = (f32[6,48,128]{2,1,0:T(8,128)S(1)}, f32[6,48,128]{2,1,0:T(8,128)S(1)}, u32[]{:S(2)}, u32[]{:S(2)}) collective-permute-start(f32[6,48,128]{2,1,0:T(8,128)S(1)} %get-tuple-element.39), channel_id=1, source_target_pairs={{0,32},{32,0},{64,96},{96,64},{1,33},{33,1},{65,97},{97,65},{2,34}... | collective-permute-start | bytes 442376 | tf_op jit(solution)/shard_map/ppermute | solution.py:360
  59.4 20.3 %collective-permute-start.12 = (f32[6,48,128]{2,1,0:T(8,128)S(1)}, f32[6,48,128]{2,1,0:T(8,128)S(1)}, u32[]{:S(2)}, u32[]{:S(2)}) collective-permute-start(f32[6,48,128]{2,1,0:T(8,128)S(1)} %get-tuple-element.40), channel_id=1, source_target_pairs={{0,64},{32,96},{64,0},{96,32},{1,65},{33,97},{65,1},{97,33},{2,66}... | collective-permute-start | bytes 442376 | tf_op jit(solution)/shard_map/ppermute | solution.py:360
  66.6 15.8 %collective-permute-start.13 = (f32[6,48,128]{2,1,0:T(8,128)S(1)}, f32[6,48,128]{2,1,0:T(8,128)S(1)}, u32[]{:S(2)}, u32[]{:S(2)}) collective-permute-start(f32[6,48,128]{2,1,0:T(8,128)S(1)} %get-tuple-element.41), channel_id=1, source_target_pairs={{0,96},{32,64},{64,32},{96,0},{1,97},{33,65},{65,33},{97,1},{2,98}... | collective-permute-start | bytes 442376 | tf_op jit(solution)/shard_map/ppermute | solution.py:360

commit v6 on v5

--- a/solution.py
+++ b/solution.py
@@ -13,7 +13,6 @@
 LANES = 128
 VMEM_LIMIT = 12 << 20
 VMEM = pl.BlockSpec(memory_space=pltpu.VMEM)
-SMEM = pl.BlockSpec(memory_space=pltpu.SMEM)
 ANY = pl.BlockSpec(memory_space=pl.ANY)
 HBM = pl.BlockSpec(memory_space=pltpu.HBM)
 COST = pl.CostEstimate(flops=1, bytes_accessed=1, transcendentals=0)
@@ -94,25 +93,25 @@
     ]
 
 
-def entry_kernel(band_ref, source_ref, low_ref, y_ref, z_ref):
+def entry_kernel(sent_ref, source_ref, low_ref, y_ref, z_ref):
     low_ref[...] = source_ref[0:REACH]
     pack_into([source_ref], y_ref, z_ref)
 
 
-def entry(band, source):
+def entry(sent, source):
     outer = jax.ShapeDtypeStruct((REACH,) + source.shape[1:], jnp.float32)
     return pl.pallas_call(
         entry_kernel,
         out_shape=[outer] + face_shapes(source.shape[0]),
-        in_specs=[SMEM, VMEM],
+        in_specs=[ANY, VMEM],
         out_specs=[VMEM] * 3,
         compiler_params=pltpu.CompilerParams(vmem_limit_bytes=VMEM_LIMIT),
         cost_estimate=COST,
         name="entry",
-    )(band, source)
-
-
-def stencil_kernel(counts, sections, second, band_ref, *refs):
+    )(sent, source)
+
+
+def stencil_kernel(counts, sections, second, *refs):
     n, m = len(counts), len(sections)
     pieces, y_refs, z_refs = refs[:n], refs[n : n + m], refs[n + m : n + 2 * m]
     potential_ref, halo_ref = refs[n + 2 * m : n + 2 * m + 2]
@@ -193,11 +192,11 @@
     if second:
         part = rows // 4
         for slot in range(4):
-            there = pl.ds(pl.multiple_of((band_ref[0] ^ slot) * part, 8), part)
+            there = pl.ds(pl.multiple_of((lax.axis_index("band") ^ slot) * part, 8), part)
             outputs[1 + slot][...] = outputs[0][REACH:planes, there, :]
 
 
-def apply_stencil(pieces, faces, potential, halo, band, source=None):
+def apply_stencil(pieces, faces, potential, halo, source=None):
     second = source is not None
     counts = [piece.shape[0] for piece in pieces]
     planes, rows = sum(counts), pieces[0].shape[1]
@@ -213,7 +212,7 @@
     return pl.pallas_call(
         functools.partial(stencil_kernel, counts, sections, second),
         out_shape=[jax.ShapeDtypeStruct(shape, jnp.float32) for shape in shapes],
-        in_specs=[SMEM] + [VMEM] * len(operands),
+        in_specs=[VMEM] * len(operands),
         out_specs=[VMEM] * len(shapes),
         scratch_shapes=[
             pltpu.VMEM((planes, ROWS + 16, LANES), jnp.float32),
@@ -223,7 +222,7 @@
         compiler_params=pltpu.CompilerParams(vmem_limit_bytes=VMEM_LIMIT),
         cost_estimate=COST,
         name="second_step" if second else "first_step",
-    )(band, *operands)
+    )(*operands)
 
 
 def add_halo(out_ref, partial_ref, halo_ref, high_side, factor):
@@ -262,31 +261,31 @@
     )(low, middle, partial, halo)
 
 
-def finish_filtered_kernel(band_ref, partial_ref, halo_ref, whole_ref, out_ref, *rest):
+def finish_filtered_kernel(partial_ref, halo_ref, whole_ref, out_ref, *rest):
     slots, done, semaphore = rest[:4], rest[4], rest[5]
     add_halo(done, partial_ref, halo_ref, False, 2.0)
     copy = pltpu.make_async_copy(done, out_ref.at[0:REACH], semaphore)
     copy.start()
     part = slots[0].shape[1]
     for slot in range(4):
-        there = pl.ds(pl.multiple_of((band_ref[0] ^ slot) * part, 8), part)
+        there = pl.ds(pl.multiple_of((lax.axis_index("band") ^ slot) * part, 8), part)
         slots[slot][...] = done[:, there, :]
     copy.wait()
 
 
-def finish_filtered(partial, halo, whole, band):
+def finish_filtered(partial, halo, whole):
     part = jax.ShapeDtypeStruct((REACH, partial.shape[1] // 4, LANES), jnp.float32)
     return pl.pallas_call(
         finish_filtered_kernel,
         out_shape=[jax.ShapeDtypeStruct(whole.shape, jnp.float32)] + [part] * 4,
-        in_specs=[SMEM, VMEM, VMEM, ANY],
+        in_specs=[VMEM, VMEM, ANY],
         out_specs=[ANY] + [VMEM] * 4,
-        input_output_aliases={3: 0},
+        input_output_aliases={2: 0},
         scratch_shapes=[pltpu.VMEM(partial.shape, jnp.float32), pltpu.SemaphoreType.DMA(())],
         compiler_params=pltpu.CompilerParams(vmem_limit_bytes=VMEM_LIMIT),
         cost_estimate=COST,
         name="finish_filtered",
-    )(band, partial, halo, whole)
+    )(partial, halo, whole)
 
 
 PAIRS = [(i, j) for i in range(4) for j in range(i, 4)]
@@ -325,10 +324,10 @@
     )(*parts)
 
 
-def late_gram_kernel(band_ref, before_ref, *refs):
+def late_gram_kernel(before_ref, *refs):
     out_ref = refs[-1]
     totals = add_products(refs[:4], [before_ref[n] for n in range(len(PAIRS))])
-    band = band_ref[0]
+    band = lax.axis_index("band")
     lane = lax.broadcasted_iota(jnp.int32, (1, LANES), 1)
     row = jnp.zeros((1, LANES), jnp.float32)
     for n, (i, j) in enumerate(PAIRS):
@@ -339,16 +338,16 @@
     out_ref[...] = jnp.broadcast_to(row, out_ref.shape)
 
 
-def late_gram(before, parts, band, peers):
+def late_gram(before, parts, peers):
     return pl.pallas_call(
         late_gram_kernel,
         out_shape=jax.ShapeDtypeStruct((peers, LANES), jnp.float32),
-        in_specs=[SMEM] + [VMEM] * 5,
+        in_specs=[VMEM] * 5,
         out_specs=VMEM,
         compiler_params=pltpu.CompilerParams(vmem_limit_bytes=VMEM_LIMIT),
         cost_estimate=COST,
         name="late_gram",
-    )(band, before, *parts)
+    )(before, *parts)
 
 
 def shifted(array, by):
@@ -372,23 +371,23 @@
 
 def on_device(orbitals, potential):
     source, local_potential = orbitals[0, 0], potential[0]
-    band = lax.axis_index("band").astype(jnp.int32).reshape(1)
-    below = shifted(source[source.shape[0] - REACH :], 4)
-    low_planes, *faces = entry(band, source)
+    high_planes = source[source.shape[0] - REACH :]
+    below = shifted(high_planes, 4)
+    low_planes, *faces = entry(high_planes, source)
     faces = swapped_faces(faces)
     above = shifted(low_planes, -4)
-    low, middle, top = apply_stencil([source], [faces], local_potential, below, band)
+    low, middle, top = apply_stencil([source], [faces], local_potential, below)
     above_first = shifted(low, -4)
     top, *faces = finish_first(low, middle, top, above)
     below_first = shifted(top, 4)
     faces = swapped_faces(faces)
     filtered, *slots, low_filtered = apply_stencil(
-        [low, middle, top], [faces], local_potential, above_first, band, source
+        [low, middle, top], [faces], local_potential, above_first, source
     )
     early = early_gram(band_exchange(slots))
-    filtered, *slots = finish_filtered(low_filtered, below_first, filtered, band)
+    filtered, *slots = finish_filtered(low_filtered, below_first, filtered)
     both = ("band", "space")
-    rows = late_gram(early, band_exchange(slots), band, lax.axis_size(both))
+    rows = late_gram(early, band_exchange(slots), lax.axis_size(both))
     everyone = lax.all_to_all(rows, both, 0, 0, tiled=True)
     summed = jnp.sum(everyone, axis=0)[:16].reshape(4, 4)
     correlation = summed / jnp.float32(filtered.size * lax.axis_size("space"))

time: 103 us -> 103 us (level)
  local copies, waits for them, and re-layouts: 3.44 us -> 5.11 us
  waiting for transfers between devices: 37.7 us -> 36.5 us
    unnamed x6 -> x8, local copies, waits for them, and re-layouts: 1.67 us -> 3.34 us
    ppermute x4, waiting for transfers between devices: 6.34 us -> 4.75 us  [shifted(): lax.ppermute(array, 'space', [(i, (i + by) % peers) for i in range(peers)])]
where the time goes in v6:
time: 103 us; the launch traced here: 102 us
  waiting for transfers between devices  36.5 us (35%)
  starting transfers between devices  25.1 us (24%)
  blocking collectives  18.4 us (18%)
  Pallas kernels  15.7 us (15%)
  local copies, waits for them, and re-layouts  5.11 us (5%)
    ppermute x10, waiting for transfers between devices, swapped(): lax.ppermute(array, axis, [(i, i ^ bit) for i in range(lax.axis_size(axis...  31.8 us
    all_to_all x1, blocking collectives, on_device(): everyone = lax.all_to_all(rows, both, 0, 0, tiled=True)  18.4 us
    ppermute x10, starting transfers between devices, swapped(): lax.ppermute(array, axis, [(i, i ^ bit) for i in range(lax.axis_size(axis...  15.6 us
    pallas_call x2, Pallas kernels, apply_stencil(): pl.pallas_call(functools.partial(stencil_kernel, counts, sections, second...  12.1 us
    ppermute x4, starting transfers between devices, shifted(): lax.ppermute(array, 'space', [(i, (i + by) % peers) for i in range(peers)])  9.47 us
    ppermute x4, waiting for transfers between devices, shifted(): lax.ppermute(array, 'space', [(i, (i + by) % peers) for i in range(peers)])  4.75 us
    unnamed x8, local copies, waits for them, and re-layouts  3.34 us
  transfers between devices with their start and end apart: 14, of which 9 were waited for; matrix products, arithmetic and copies ran while one was open for 0% of the time, Pallas kernels for 15%

profile of v6, /device:TPU:0, one launch (start us, length us, event | category | flops | bytes accessed | tf_op | source)
XLA Modules:
  0.0 101.8 jit_solution(16484797720324503183)
XLA Ops:
  0.6 1.1 %slice_bitcast_fusion.sent_ref = f32[6,192,128]{2,1,0:T(8,128)S(1)} fusion(f32[1,1,24,192,128]{4,3,2,1,0:T(8,128)} %param.2), kind=kLoop, calls=%fused_computation | loop fusion | bytes 1179648 | tf_op jit(solution)/shard_map/slice | solution.py:374
  1.7 1.7 %collective-permute-start.2 = (f32[6,192,128]{2,1,0:T(8,128)S(1)}, f32[6,192,128]{2,1,0:T(8,128)S(1)}, u32[]{:S(2)}, u32[]{:S(2)}) collective-permute-start(f32[6,192,128]{2,1,0:T(8,128)S(1)} %slice_bitcast_fusion.sent_ref), channel_id=1, source_target_pairs={{0,4},{1,5},{2,6},{3,7},{4,8},{5,9},{6,10},{7,11},{8,12},{9,13},{1... | collective-permute-start | bytes 1769480 | tf_op jit(solution)/shard_map/ppermute | solution.py:355
  3.5 0.0 copy-start
  3.5 1.7 %copy-done = f32[1,1,24,192,128]{4,3,2,1,0:T(8,128)S(1)} copy-done((f32[1,1,24,192,128]{4,3,2,1,0:T(8,128)S(1)}, f32[1,1,24,192,128]{4,3,2,1,0:T(8,128)}, u32[]{:S(2)}) %copy-start) | copy-done | bytes 2359320
  5.1 0.0 copy-start.1
  5.1 0.8 entry.1
  5.9 1.6 %collective-permute-start.1 = (f32[24,24,128]{2,1,0:T(8,128)S(1)}, f32[24,24,128]{2,1,0:T(8,128)S(1)}, u32[]{:S(2)}, u32[]{:S(2)}) collective-permute-start(f32[24,24,128]{2,1,0:T(8,128)S(1)} %get-tuple-element.23), channel_id=1, source_target_pairs={{0,1},{1,0},{2,3},{3,2},{4,5},{5,4},{6,7},{7,6},{8,9},{9,8},{10,11... | collective-permute-start | bytes 884744 | tf_op jit(solution)/shard_map/ppermute | solution.py:359
  7.5 3.5 %collective-permute-start.3 = (f32[6,192,128]{2,1,0:T(8,128)S(1)}, f32[6,192,128]{2,1,0:T(8,128)S(1)}, u32[]{:S(2)}, u32[]{:S(2)}) collective-permute-start(f32[6,192,128]{2,1,0:T(8,128)S(1)} %get-tuple-element.27), channel_id=1, source_target_pairs={{0,28},{1,29},{2,30},{3,31},{4,0},{5,1},{6,2},{7,3},{8,4},{9,5},{1... | collective-permute-start | bytes 1769480 | tf_op jit(solution)/shard_map/ppermute | solution.py:355
  11.0 2.7 %collective-permute-start = (f32[296,128]{1,0:T(8,128)S(1)}, f32[296,128]{1,0:T(8,128)S(1)}, u32[]{:S(2)}, u32[]{:S(2)}) collective-permute-start(f32[296,128]{1,0:T(8,128)S(1)} %get-tuple-element.22), channel_id=1, source_target_pairs={{0,2},{1,3},{2,0},{3,1},{4,6},{5,7},{6,4},{7,5},{8,10},{9,11},{10,... | collective-permute-start | bytes 454664 | tf_op jit(solution)/shard_map/ppermute | solution.py:359
  13.7 6.2 %collective-permute-done.refs_1_ = f32[296,128]{1,0:T(8,128)S(1)} collective-permute-done((f32[296,128]{1,0:T(8,128)S(1)}, f32[296,128]{1,0:T(8,128)S(1)}, u32[]{:S(2)}, u32[]{:S(2)}) %collective-permute-start) | collective-permute-done | bytes 151584 | tf_op jit(solution)/shard_map/ppermute | solution.py:359
  19.9 0.0 collective-permute-done.1.refs_2_
  19.9 1.2 %collective-permute-done.2.refs_4_ = f32[6,192,128]{2,1,0:T(8,128)S(1)} collective-permute-done((f32[6,192,128]{2,1,0:T(8,128)S(1)}, f32[6,192,128]{2,1,0:T(8,128)S(1)}, u32[]{:S(2)}, u32[]{:S(2)}) %collective-permute-start.2) | collective-permute-done | bytes 589856 | tf_op jit(solution)/shard_map/ppermute | solution.py:355
  21.1 0.0 copy-done.1
  21.1 0.0 copy-start.2
  21.1 1.7 %copy-done.2 = f32[1,24,192,128]{3,2,1,0:T(8,128)S(1)} copy-done((f32[1,24,192,128]{3,2,1,0:T(8,128)S(1)}, f32[1,24,192,128]{3,2,1,0:T(8,128)}, u32[]{:S(2)}) %copy-start.2) | copy-done | bytes 2359320
  22.8 5.1 %first_step.1 = (f32[6,192,128]{2,1,0:T(8,128)S(1)}, f32[12,192,128]{2,1,0:T(8,128)S(1)}, f32[6,192,128]{2,1,0:T(8,128)S(1)}) custom-call(f32[24,192,128]{2,1,0:T(8,128)S(1)} %bitcast.9, f32[296,128]{1,0:T(8,128)S(1)} %collective-permute-done.refs_1_, f32[24,24,128]{2,1,0:T(8,128)S(1)} %collective-permute-done.1.refs_2_, f32[24,192,128]{2,1,0:T(8,128)S(1)} %bitcast.11, ...), custom_call_target="tpu_custom_call" | custom-call | flops 1 | bytes 1 | tf_op jit(solution)/shard_map/first_step/pallas_call | solution.py:212
  27.9 0.0 copy-start.3
  27.9 2.7 %collective-permute-start.6 = (f32[6,192,128]{2,1,0:T(8,128)S(1)}, f32[6,192,128]{2,1,0:T(8,128)S(1)}, u32[]{:S(2)}, u32[]{:S(2)}) collective-permute-start(f32[6,192,128]{2,1,0:T(8,128)S(1)} %get-tuple-element.24.low_ref.refs_0_), channel_id=1, source_target_pairs={{0,28},{1,29},{2,30},{3,31},{4,0},{5,1},{6,2},{7,3},{8,4},{9,5},{1... | collective-permute-start | bytes 1769480 | tf_op jit(solution)/shard_map/ppermute | solution.py:355
  30.6 1.5 %collective-permute-done.3.halo_ref = f32[6,192,128]{2,1,0:T(8,128)S(1)} collective-permute-done((f32[6,192,128]{2,1,0:T(8,128)S(1)}, f32[6,192,128]{2,1,0:T(8,128)S(1)}, u32[]{:S(2)}, u32[]{:S(2)}) %collective-permute-start.3) | collective-permute-done | bytes 589856 | tf_op jit(solution)/shard_map/ppermute | solution.py:355
  32.1 1.1 %finish_first.1 = (f32[6,192,128]{2,1,0:T(8,128)S(1)}, f32[296,128]{1,0:T(8,128)S(1)}, f32[24,24,128]{2,1,0:T(8,128)S(1)}) custom-call(f32[6,192,128]{2,1,0:T(8,128)S(1)} %get-tuple-element.24.low_ref.refs_0_, f32[12,192,128]{2,1,0:T(8,128)S(1)} %get-tuple-element.25.middle_ref.refs_1_, f32[6,192,128]{2,1,0:T(8,128)S(1)} %get-tuple-element.26.partial_ref, ...), custom_call_target="tpu_custom_call" | custom-call | flops 1 | bytes 1 | tf_op jit(solution)/shard_map/finish_first/pallas_call | solution.py:253
  33.2 1.6 %collective-permute-start.5 = (f32[24,24,128]{2,1,0:T(8,128)S(1)}, f32[24,24,128]{2,1,0:T(8,128)S(1)}, u32[]{:S(2)}, u32[]{:S(2)}) collective-permute-start(f32[24,24,128]{2,1,0:T(8,128)S(1)} %get-tuple-element.30), channel_id=1, source_target_pairs={{0,1},{1,0},{2,3},{3,2},{4,5},{5,4},{6,7},{7,6},{8,9},{9,8},{10,11... | collective-permute-start | bytes 884744 | tf_op jit(solution)/shard_map/ppermute | solution.py:359
  34.8 2.7 %collective-permute-start.4 = (f32[296,128]{1,0:T(8,128)S(1)}, f32[296,128]{1,0:T(8,128)S(1)}, u32[]{:S(2)}, u32[]{:S(2)}) collective-permute-start(f32[296,128]{1,0:T(8,128)S(1)} %get-tuple-element.29), channel_id=1, source_target_pairs={{0,2},{1,3},{2,0},{3,1},{4,6},{5,7},{6,4},{7,5},{8,10},{9,11},{10,... | collective-permute-start | bytes 454664 | tf_op jit(solution)/shard_map/ppermute | solution.py:359
  37.5 1.6 %collective-permute-start.7 = (f32[6,192,128]{2,1,0:T(8,128)S(1)}, f32[6,192,128]{2,1,0:T(8,128)S(1)}, u32[]{:S(2)}, u32[]{:S(2)}) collective-permute-start(f32[6,192,128]{2,1,0:T(8,128)S(1)} %get-tuple-element.28.refs_2_), channel_id=1, source_target_pairs={{0,4},{1,5},{2,6},{3,7},{4,8},{5,9},{6,10},{7,11},{8,12},{9,13},{1... | collective-permute-start | bytes 1769480 | tf_op jit(solution)/shard_map/ppermute | solution.py:355
  39.1 6.4 %collective-permute-done.4.refs_3_ = f32[296,128]{1,0:T(8,128)S(1)} collective-permute-done((f32[296,128]{1,0:T(8,128)S(1)}, f32[296,128]{1,0:T(8,128)S(1)}, u32[]{:S(2)}, u32[]{:S(2)}) %collective-permute-start.4) | collective-permute-done | bytes 151584 | tf_op jit(solution)/shard_map/ppermute | solution.py:359
  45.4 0.0 collective-permute-done.5.refs_4_
  45.5 0.0 collective-permute-done.6.refs_6_
  45.5 0.0 copy-done.3
  45.5 7.0 %second_step.1 = (f32[24,192,128]{2,1,0:T(8,128)}, f32[18,48,128]{2,1,0:T(8,128)S(1)}, f32[18,48,128]{2,1,0:T(8,128)S(1)}, f32[18,48,128]{2,1,0:T(8,128)S(1)}, f...) custom-call(f32[6,192,128]{2,1,0:T(8,128)S(1)} %get-tuple-element.24.low_ref.refs_0_, ...), custom_call_target="tpu_custom_call" | custom-call | flops 1 | bytes 1 | tf_op jit(solution)/shard_map/second_step/pallas_call | solution.py:212
  52.5 0.0 collective-permute-start.10
  52.5 3.3 %collective-permute-start.8 = (f32[18,48,128]{2,1,0:T(8,128)S(1)}, f32[18,48,128]{2,1,0:T(8,128)S(1)}, u32[]{:S(2)}, u32[]{:S(2)}) collective-permute-start(f32[18,48,128]{2,1,0:T(8,128)S(1)} %get-tuple-element.35), channel_id=1, source_target_pairs={{0,32},{32,0},{64,96},{96,64},{1,33},{33,1},{65,97},{97,65},{2,34}... | collective-permute-start | bytes 1327112 | tf_op jit(solution)/shard_map/ppermute | solution.py:359
  55.8 0.3 collective-permute-start.9
  56.1 2.1 %collective-permute-done.7.halo_ref = f32[6,192,128]{2,1,0:T(8,128)S(1)} collective-permute-done((f32[6,192,128]{2,1,0:T(8,128)S(1)}, f32[6,192,128]{2,1,0:T(8,128)S(1)}, u32[]{:S(2)}, u32[]{:S(2)}) %collective-permute-start.7) | collective-permute-done | bytes 589856 | tf_op jit(solution)/shard_map/ppermute | solution.py:355
  58.2 1.1 %finish_filtered.1 = (f32[24,192,128]{2,1,0:T(8,128)}, f32[6,48,128]{2,1,0:T(8,128)S(1)}, f32[6,48,128]{2,1,0:T(8,128)S(1)}, f32[6,48,128]{2,1,0:T(8,128)S(1)}, f32[6,48,128]{2,1,0:T(8,128)S(1)}) custom-call(f32[6,192,128]{2,1,0:T(8,128)S(1)} %get-tuple-element.31.partial_ref, ...), custom_call_target="tpu_custom_call", output_to_operand_aliasing={{0}: (2, {})} | custom-call | flops 1 | bytes 1 | tf_op jit(solution)/shard_map/finish_filtered/pallas_call | solution.py:278
  59.3 0.1 collective-permute-start.11
  59.4 3.0 %collective-permute-start.12 = (f32[6,48,128]{2,1,0:T(8,128)S(1)}, f32[6,48,128]{2,1,0:T(8,128)S(1)}, u32[]{:S(2)}, u32[]{:S(2)}) collective-permute-start(f32[6,48,128]{2,1,0:T(8,128)S(1)} %get-tuple-element.40), channel_id=1, source_target_pairs={{0,64},{32,96},{64,0},{96,32},{1,65},{33,97},{65,1},{97,33},{2,66}... | collective-permute-start | bytes 442376 | tf_op jit(solution)/shard_map/ppermute | solution.py:359
  62.4 4.1 %collective-permute-done.10.refs_3_ = f32[18,48,128]{2,1,0:T(8,128)S(1)} collective-permute-done((f32[18,48,128]{2,1,0:T(8,128)S(1)}, f32[18,48,128]{2,1,0:T(8,128)S(1)}, u32[]{:S(2)}, u32[]{:S(2)}) %collective-permute-start.10) | collective-permute-done | bytes 442400 | tf_op jit(solution)/shard_map/ppermute | solution.py:359
  66.5 0.3 collective-permute-start.13
  66.8 0.0 collective-permute-done.8.refs_1_
  66.8 11.7 %collective-permute-done.9.refs_2_ = f32[18,48,128]{2,1,0:T(8,128)S(1)} collective-permute-done((f32[18,48,128]{2,1,0:T(8,128)S(1)}, f32[18,48,128]{2,1,0:T(8,128)S(1)}, u32[]{:S(2)}, u32[]{:S(2)}) %collective-permute-start.9) | collective-permute-done | bytes 442400 | tf_op jit(solution)/shard_map/ppermute | solution.py:359
  78.5 0.4 early_gram.1.before_ref
  78.9 0.0 collective-permute-done.11.refs_1_
  78.9 2.8 %collective-permute-done.12.refs_2_ = f32[6,48,128]{2,1,0:T(8,128)S(1)} collective-permute-done((f32[6,48,128]{2,1,0:T(8,128)S(1)}, f32[6,48,128]{2,1,0:T(8,128)S(1)}, u32[]{:S(2)}, u32[]{:S(2)}) %collective-permute-start.12) | collective-permute-done | bytes 147488 | tf_op jit(solution)/shard_map/ppermute | solution.py:359
  81.7 0.6 collective-permute-done.13.refs_3_
  82.3 0.2 late_gram.1
  82.6 18.4 %all_to_all.9 = f32[128,1,128]{2,1,0:T(1,128)S(1)} all-to-all(f32[128,1,128]{2,1,0:T(1,128)S(1)} %bitcast.13), channel_id=1, replica_groups=mesh['band'=4,'space'=32] {'band','space'}, dimensions={0} | all-to-all | bytes 131072 | tf_op jit(solution)/shard_map/all_to_all | solution.py:391
  101.0 0.2 reduce_sum.9
  101.1 0.7 div.6
  (1 shorter events, 0.0 us)
Async XLA Ops:
  1.7 19.4 %collective-permute-start.2 = (f32[6,192,128]{2,1,0:T(8,128)S(1)}, f32[6,192,128]{2,1,0:T(8,128)S(1)}, u32[]{:S(2)}, u32[]{:S(2)}) collective-permute-start(f32[6,192,128]{2,1,0:T(8,128)S(1)} %slice_bitcast_fusion.sent_ref), channel_id=1, source_target_pairs={{0,4},{1,5},{2,6},{3,7},{4,8},{5,9},{6,10},{7,11},{8,12},{9,13},{1... | collective-permute-start | bytes 1769480 | tf_op jit(solution)/shard_map/ppermute | solution.py:355
  3.5 1.7 %copy-start = (f32[1,1,24,192,128]{4,3,2,1,0:T(8,128)S(1)}, f32[1,1,24,192,128]{4,3,2,1,0:T(8,128)}, u32[]{:S(2)}) copy-start(f32[1,1,24,192,128]{4,3,2,1,0:T(8,128)} %param.2) | copy-start | bytes 7077892
  5.1 16.0 %copy-start.1 = (f32[1,1,24,192,128]{4,3,2,1,0:T(8,128)S(1)}, f32[1,1,24,192,128]{4,3,2,1,0:T(8,128)}, u32[]{:S(2)}) copy-start(f32[1,1,24,192,128]{4,3,2,1,0:T(8,128)} %param.2) | copy-start | bytes 7077892
  5.9 14.0 %collective-permute-start.1 = (f32[24,24,128]{2,1,0:T(8,128)S(1)}, f32[24,24,128]{2,1,0:T(8,128)S(1)}, u32[]{:S(2)}, u32[]{:S(2)}) collective-permute-start(f32[24,24,128]{2,1,0:T(8,128)S(1)} %get-tuple-element.23), channel_id=1, source_target_pairs={{0,1},{1,0},{2,3},{3,2},{4,5},{5,4},{6,7},{7,6},{8,9},{9,8},{10,11... | collective-permute-start | bytes 884744 | tf_op jit(solution)/shard_map/ppermute | solution.py:359
  7.5 24.6 %collective-permute-start.3 = (f32[6,192,128]{2,1,0:T(8,128)S(1)}, f32[6,192,128]{2,1,0:T(8,128)S(1)}, u32[]{:S(2)}, u32[]{:S(2)}) collective-permute-start(f32[6,192,128]{2,1,0:T(8,128)S(1)} %get-tuple-element.27), channel_id=1, source_target_pairs={{0,28},{1,29},{2,30},{3,31},{4,0},{5,1},{6,2},{7,3},{8,4},{9,5},{1... | collective-permute-start | bytes 1769480 | tf_op jit(solution)/shard_map/ppermute | solution.py:355
  11.0 8.9 %collective-permute-start = (f32[296,128]{1,0:T(8,128)S(1)}, f32[296,128]{1,0:T(8,128)S(1)}, u32[]{:S(2)}, u32[]{:S(2)}) collective-permute-start(f32[296,128]{1,0:T(8,128)S(1)} %get-tuple-element.22), channel_id=1, source_target_pairs={{0,2},{1,3},{2,0},{3,1},{4,6},{5,7},{6,4},{7,5},{8,10},{9,11},{10,... | collective-permute-start | bytes 454664 | tf_op jit(solution)/shard_map/ppermute | solution.py:359
  21.1 1.7 %copy-start.2 = (f32[1,24,192,128]{3,2,1,0:T(8,128)S(1)}, f32[1,24,192,128]{3,2,1,0:T(8,128)}, u32[]{:S(2)}) copy-start(f32[1,24,192,128]{3,2,1,0:T(8,128)} %param.3) | copy-start | bytes 7077892
  27.9 17.6 %copy-start.3 = (f32[1,24,192,128]{3,2,1,0:T(8,128)S(1)}, f32[1,24,192,128]{3,2,1,0:T(8,128)}, u32[]{:S(2)}) copy-start(f32[1,24,192,128]{3,2,1,0:T(8,128)} %param.3) | copy-start | bytes 7077892
  27.9 17.5 %collective-permute-start.6 = (f32[6,192,128]{2,1,0:T(8,128)S(1)}, f32[6,192,128]{2,1,0:T(8,128)S(1)}, u32[]{:S(2)}, u32[]{:S(2)}) collective-permute-start(f32[6,192,128]{2,1,0:T(8,128)S(1)} %get-tuple-element.24.low_ref.refs_0_), channel_id=1, source_target_pairs={{0,28},{1,29},{2,30},{3,31},{4,0},{5,1},{6,2},{7,3},{8,4},{9,5},{1... | collective-permute-start | bytes 1769480 | tf_op jit(solution)/shard_map/ppermute | solution.py:355
  33.2 12.3 %collective-permute-start.5 = (f32[24,24,128]{2,1,0:T(8,128)S(1)}, f32[24,24,128]{2,1,0:T(8,128)S(1)}, u32[]{:S(2)}, u32[]{:S(2)}) collective-permute-start(f32[24,24,128]{2,1,0:T(8,128)S(1)} %get-tuple-element.30), channel_id=1, source_target_pairs={{0,1},{1,0},{2,3},{3,2},{4,5},{5,4},{6,7},{7,6},{8,9},{9,8},{10,11... | collective-permute-start | bytes 884744 | tf_op jit(solution)/shard_map/ppermute | solution.py:359
  34.8 10.7 %collective-permute-start.4 = (f32[296,128]{1,0:T(8,128)S(1)}, f32[296,128]{1,0:T(8,128)S(1)}, u32[]{:S(2)}, u32[]{:S(2)}) collective-permute-start(f32[296,128]{1,0:T(8,128)S(1)} %get-tuple-element.29), channel_id=1, source_target_pairs={{0,2},{1,3},{2,0},{3,1},{4,6},{5,7},{6,4},{7,5},{8,10},{9,11},{10,... | collective-permute-start | bytes 454664 | tf_op jit(solution)/shard_map/ppermute | solution.py:359
  37.5 20.7 %collective-permute-start.7 = (f32[6,192,128]{2,1,0:T(8,128)S(1)}, f32[6,192,128]{2,1,0:T(8,128)S(1)}, u32[]{:S(2)}, u32[]{:S(2)}) collective-permute-start(f32[6,192,128]{2,1,0:T(8,128)S(1)} %get-tuple-element.28.refs_2_), channel_id=1, source_target_pairs={{0,4},{1,5},{2,6},{3,7},{4,8},{5,9},{6,10},{7,11},{8,12},{9,13},{1... | collective-permute-start | bytes 1769480 | tf_op jit(solution)/shard_map/ppermute | solution.py:355
  52.5 14.0 %collective-permute-start.10 = (f32[18,48,128]{2,1,0:T(8,128)S(1)}, f32[18,48,128]{2,1,0:T(8,128)S(1)}, u32[]{:S(2)}, u32[]{:S(2)}) collective-permute-start(f32[18,48,128]{2,1,0:T(8,128)S(1)} %get-tuple-element.37), channel_id=1, source_target_pairs={{0,96},{32,64},{64,32},{96,0},{1,97},{33,65},{65,33},{97,1},{2,98}... | collective-permute-start | bytes 1327112 | tf_op jit(solution)/shard_map/ppermute | solution.py:359
  52.5 14.4 %collective-permute-start.8 = (f32[18,48,128]{2,1,0:T(8,128)S(1)}, f32[18,48,128]{2,1,0:T(8,128)S(1)}, u32[]{:S(2)}, u32[]{:S(2)}) collective-permute-start(f32[18,48,128]{2,1,0:T(8,128)S(1)} %get-tuple-element.35), channel_id=1, source_target_pairs={{0,32},{32,0},{64,96},{96,64},{1,33},{33,1},{65,97},{97,65},{2,34}... | collective-permute-start | bytes 1327112 | tf_op jit(solution)/shard_map/ppermute | solution.py:359
  55.8 22.7 %collective-permute-start.9 = (f32[18,48,128]{2,1,0:T(8,128)S(1)}, f32[18,48,128]{2,1,0:T(8,128)S(1)}, u32[]{:S(2)}, u32[]{:S(2)}) collective-permute-start(f32[18,48,128]{2,1,0:T(8,128)S(1)} %get-tuple-element.36), channel_id=1, source_target_pairs={{0,64},{32,96},{64,0},{96,32},{1,65},{33,97},{65,1},{97,33},{2,66}... | collective-permute-start | bytes 1327112 | tf_op jit(solution)/shard_map/ppermute | solution.py:359
  59.3 19.6 %collective-permute-start.11 = (f32[6,48,128]{2,1,0:T(8,128)S(1)}, f32[6,48,128]{2,1,0:T(8,128)S(1)}, u32[]{:S(2)}, u32[]{:S(2)}) collective-permute-start(f32[6,48,128]{2,1,0:T(8,128)S(1)} %get-tuple-element.39), channel_id=1, source_target_pairs={{0,32},{32,0},{64,96},{96,64},{1,33},{33,1},{65,97},{97,65},{2,34}... | collective-permute-start | bytes 442376 | tf_op jit(solution)/shard_map/ppermute | solution.py:359
  59.4 22.3 %collective-permute-start.12 = (f32[6,48,128]{2,1,0:T(8,128)S(1)}, f32[6,48,128]{2,1,0:T(8,128)S(1)}, u32[]{:S(2)}, u32[]{:S(2)}) collective-permute-start(f32[6,48,128]{2,1,0:T(8,128)S(1)} %get-tuple-element.40), channel_id=1, source_target_pairs={{0,64},{32,96},{64,0},{96,32},{1,65},{33,97},{65,1},{97,33},{2,66}... | collective-permute-start | bytes 442376 | tf_op jit(solution)/shard_map/ppermute | solution.py:359
  66.5 15.8 %collective-permute-start.13 = (f32[6,48,128]{2,1,0:T(8,128)S(1)}, f32[6,48,128]{2,1,0:T(8,128)S(1)}, u32[]{:S(2)}, u32[]{:S(2)}) collective-permute-start(f32[6,48,128]{2,1,0:T(8,128)S(1)} %get-tuple-element.41), channel_id=1, source_target_pairs={{0,96},{32,64},{64,32},{96,0},{1,97},{33,65},{65,33},{97,1},{2,98}... | collective-permute-start | bytes 442376 | tf_op jit(solution)/shard_map/ppermute | solution.py:359

commit v7 on v6

--- a/solution.py
+++ b/solution.py
@@ -389,7 +389,8 @@
     both = ("band", "space")
     rows = late_gram(early, band_exchange(slots), lax.axis_size(both))
     everyone = lax.all_to_all(rows, both, 0, 0, tiled=True)
-    summed = jnp.sum(everyone, axis=0)[:16].reshape(4, 4)
+    row = jnp.sum(everyone, axis=0)
+    summed = jnp.stack([row[4 * i : 4 * i + 4] for i in range(4)])
     correlation = summed / jnp.float32(filtered.size * lax.axis_size("space"))
     return filtered[None, None], correlation
 

time: 103 us -> 103 us (level)
  no operation moved by 1% of the time
where the time goes in v7:
time: 103 us; the launch traced here: 102 us
  waiting for transfers between devices  36.5 us (35%)
  starting transfers between devices  25.1 us (24%)
  blocking collectives  18.4 us (18%)
  Pallas kernels  15.7 us (15%)
  local copies, waits for them, and re-layouts  4.52 us (4%)
    ppermute x10, waiting for transfers between devices, swapped(): lax.ppermute(array, axis, [(i, i ^ bit) for i in range(lax.axis_size(axis...  31.8 us
    all_to_all x1, blocking collectives, on_device(): everyone = lax.all_to_all(rows, both, 0, 0, tiled=True)  18.4 us
    ppermute x10, starting transfers between devices, swapped(): lax.ppermute(array, axis, [(i, i ^ bit) for i in range(lax.axis_size(axis...  15.6 us
    pallas_call x2, Pallas kernels, apply_stencil(): pl.pallas_call(functools.partial(stencil_kernel, counts, sections, second...  12.1 us
    ppermute x4, starting transfers between devices, shifted(): lax.ppermute(array, 'space', [(i, (i + by) % peers) for i in range(peers)])  9.47 us
    ppermute x4, waiting for transfers between devices, shifted(): lax.ppermute(array, 'space', [(i, (i + by) % peers) for i in range(peers)])  4.75 us
    unnamed x8, local copies, waits for them, and re-layouts  3.34 us
  transfers between devices with their start and end apart: 14, of which 9 were waited for; matrix products, arithmetic and copies ran while one was open for 0% of the time, Pallas kernels for 15%

profile of v7, /device:TPU:0, one launch (start us, length us, event | category | flops | bytes accessed | tf_op | source)
XLA Modules:
  0.0 101.8 jit_solution(4415429035661704838)
XLA Ops:
  0.6 1.1 %slice_bitcast_fusion.sent_ref = f32[6,192,128]{2,1,0:T(8,128)S(1)} fusion(f32[1,1,24,192,128]{4,3,2,1,0:T(8,128)} %param.2), kind=kLoop, calls=%fused_computation | loop fusion | bytes 1179648 | tf_op jit(solution)/shard_map/slice | solution.py:374
  1.7 1.7 %collective-permute-start.2 = (f32[6,192,128]{2,1,0:T(8,128)S(1)}, f32[6,192,128]{2,1,0:T(8,128)S(1)}, u32[]{:S(2)}, u32[]{:S(2)}) collective-permute-start(f32[6,192,128]{2,1,0:T(8,128)S(1)} %slice_bitcast_fusion.sent_ref), channel_id=1, source_target_pairs={{0,4},{1,5},{2,6},{3,7},{4,8},{5,9},{6,10},{7,11},{8,12},{9,13},{1... | collective-permute-start | bytes 1769480 | tf_op jit(solution)/shard_map/ppermute | solution.py:355
  3.5 0.0 copy-start
  3.5 1.7 %copy-done = f32[1,1,24,192,128]{4,3,2,1,0:T(8,128)S(1)} copy-done((f32[1,1,24,192,128]{4,3,2,1,0:T(8,128)S(1)}, f32[1,1,24,192,128]{4,3,2,1,0:T(8,128)}, u32[]{:S(2)}) %copy-start) | copy-done | bytes 2359320
  5.1 0.0 copy-start.1
  5.1 0.8 entry.1
  5.9 1.6 %collective-permute-start.1 = (f32[24,24,128]{2,1,0:T(8,128)S(1)}, f32[24,24,128]{2,1,0:T(8,128)S(1)}, u32[]{:S(2)}, u32[]{:S(2)}) collective-permute-start(f32[24,24,128]{2,1,0:T(8,128)S(1)} %get-tuple-element.23), channel_id=1, source_target_pairs={{0,1},{1,0},{2,3},{3,2},{4,5},{5,4},{6,7},{7,6},{8,9},{9,8},{10,11... | collective-permute-start | bytes 884744 | tf_op jit(solution)/shard_map/ppermute | solution.py:359
  7.5 3.5 %collective-permute-start.3 = (f32[6,192,128]{2,1,0:T(8,128)S(1)}, f32[6,192,128]{2,1,0:T(8,128)S(1)}, u32[]{:S(2)}, u32[]{:S(2)}) collective-permute-start(f32[6,192,128]{2,1,0:T(8,128)S(1)} %get-tuple-element.27), channel_id=1, source_target_pairs={{0,28},{1,29},{2,30},{3,31},{4,0},{5,1},{6,2},{7,3},{8,4},{9,5},{1... | collective-permute-start | bytes 1769480 | tf_op jit(solution)/shard_map/ppermute | solution.py:355
  11.0 2.7 %collective-permute-start = (f32[296,128]{1,0:T(8,128)S(1)}, f32[296,128]{1,0:T(8,128)S(1)}, u32[]{:S(2)}, u32[]{:S(2)}) collective-permute-start(f32[296,128]{1,0:T(8,128)S(1)} %get-tuple-element.22), channel_id=1, source_target_pairs={{0,2},{1,3},{2,0},{3,1},{4,6},{5,7},{6,4},{7,5},{8,10},{9,11},{10,... | collective-permute-start | bytes 454664 | tf_op jit(solution)/shard_map/ppermute | solution.py:359
  13.7 6.2 %collective-permute-done.refs_1_ = f32[296,128]{1,0:T(8,128)S(1)} collective-permute-done((f32[296,128]{1,0:T(8,128)S(1)}, f32[296,128]{1,0:T(8,128)S(1)}, u32[]{:S(2)}, u32[]{:S(2)}) %collective-permute-start) | collective-permute-done | bytes 151584 | tf_op jit(solution)/shard_map/ppermute | solution.py:359
  19.9 0.0 collective-permute-done.1.refs_2_
  19.9 1.2 %collective-permute-done.2.refs_4_ = f32[6,192,128]{2,1,0:T(8,128)S(1)} collective-permute-done((f32[6,192,128]{2,1,0:T(8,128)S(1)}, f32[6,192,128]{2,1,0:T(8,128)S(1)}, u32[]{:S(2)}, u32[]{:S(2)}) %collective-permute-start.2) | collective-permute-done | bytes 589856 | tf_op jit(solution)/shard_map/ppermute | solution.py:355
  21.1 0.0 copy-done.1
  21.1 0.0 copy-start.2
  21.1 1.7 %copy-done.2 = f32[1,24,192,128]{3,2,1,0:T(8,128)S(1)} copy-done((f32[1,24,192,128]{3,2,1,0:T(8,128)S(1)}, f32[1,24,192,128]{3,2,1,0:T(8,128)}, u32[]{:S(2)}) %copy-start.2) | copy-done | bytes 2359320
  22.8 5.1 %first_step.1 = (f32[6,192,128]{2,1,0:T(8,128)S(1)}, f32[12,192,128]{2,1,0:T(8,128)S(1)}, f32[6,192,128]{2,1,0:T(8,128)S(1)}) custom-call(f32[24,192,128]{2,1,0:T(8,128)S(1)} %bitcast.17, f32[296,128]{1,0:T(8,128)S(1)} %collective-permute-done.refs_1_, f32[24,24,128]{2,1,0:T(8,128)S(1)} %collective-permute-done.1.refs_2_, f32[24,192,128]{2,1,0:T(8,128)S(1)} %bitcast.19, ...), custom_call_target="tpu_custom_call" | custom-call | flops 1 | bytes 1 | tf_op jit(solution)/shard_map/first_step/pallas_call | solution.py:212
  27.9 0.0 copy-start.3
  27.9 2.7 %collective-permute-start.6 = (f32[6,192,128]{2,1,0:T(8,128)S(1)}, f32[6,192,128]{2,1,0:T(8,128)S(1)}, u32[]{:S(2)}, u32[]{:S(2)}) collective-permute-start(f32[6,192,128]{2,1,0:T(8,128)S(1)} %get-tuple-element.24.low_ref.refs_0_), channel_id=1, source_target_pairs={{0,28},{1,29},{2,30},{3,31},{4,0},{5,1},{6,2},{7,3},{8,4},{9,5},{1... | collective-permute-start | bytes 1769480 | tf_op jit(solution)/shard_map/ppermute | solution.py:355
  30.6 1.5 %collective-permute-done.3.halo_ref = f32[6,192,128]{2,1,0:T(8,128)S(1)} collective-permute-done((f32[6,192,128]{2,1,0:T(8,128)S(1)}, f32[6,192,128]{2,1,0:T(8,128)S(1)}, u32[]{:S(2)}, u32[]{:S(2)}) %collective-permute-start.3) | collective-permute-done | bytes 589856 | tf_op jit(solution)/shard_map/ppermute | solution.py:355
  32.1 1.1 %finish_first.1 = (f32[6,192,128]{2,1,0:T(8,128)S(1)}, f32[296,128]{1,0:T(8,128)S(1)}, f32[24,24,128]{2,1,0:T(8,128)S(1)}) custom-call(f32[6,192,128]{2,1,0:T(8,128)S(1)} %get-tuple-element.24.low_ref.refs_0_, f32[12,192,128]{2,1,0:T(8,128)S(1)} %get-tuple-element.25.middle_ref.refs_1_, f32[6,192,128]{2,1,0:T(8,128)S(1)} %get-tuple-element.26.partial_ref, ...), custom_call_target="tpu_custom_call" | custom-call | flops 1 | bytes 1 | tf_op jit(solution)/shard_map/finish_first/pallas_call | solution.py:253
  33.2 1.6 %collective-permute-start.5 = (f32[24,24,128]{2,1,0:T(8,128)S(1)}, f32[24,24,128]{2,1,0:T(8,128)S(1)}, u32[]{:S(2)}, u32[]{:S(2)}) collective-permute-start(f32[24,24,128]{2,1,0:T(8,128)S(1)} %get-tuple-element.30), channel_id=1, source_target_pairs={{0,1},{1,0},{2,3},{3,2},{4,5},{5,4},{6,7},{7,6},{8,9},{9,8},{10,11... | collective-permute-start | bytes 884744 | tf_op jit(solution)/shard_map/ppermute | solution.py:359
  34.8 2.7 %collective-permute-start.4 = (f32[296,128]{1,0:T(8,128)S(1)}, f32[296,128]{1,0:T(8,128)S(1)}, u32[]{:S(2)}, u32[]{:S(2)}) collective-permute-start(f32[296,128]{1,0:T(8,128)S(1)} %get-tuple-element.29), channel_id=1, source_target_pairs={{0,2},{1,3},{2,0},{3,1},{4,6},{5,7},{6,4},{7,5},{8,10},{9,11},{10,... | collective-permute-start | bytes 454664 | tf_op jit(solution)/shard_map/ppermute | solution.py:359
  37.5 1.6 %collective-permute-start.7 = (f32[6,192,128]{2,1,0:T(8,128)S(1)}, f32[6,192,128]{2,1,0:T(8,128)S(1)}, u32[]{:S(2)}, u32[]{:S(2)}) collective-permute-start(f32[6,192,128]{2,1,0:T(8,128)S(1)} %get-tuple-element.28.refs_2_), channel_id=1, source_target_pairs={{0,4},{1,5},{2,6},{3,7},{4,8},{5,9},{6,10},{7,11},{8,12},{9,13},{1... | collective-permute-start | bytes 1769480 | tf_op jit(solution)/shard_map/ppermute | solution.py:355
  39.1 6.4 %collective-permute-done.4.refs_3_ = f32[296,128]{1,0:T(8,128)S(1)} collective-permute-done((f32[296,128]{1,0:T(8,128)S(1)}, f32[296,128]{1,0:T(8,128)S(1)}, u32[]{:S(2)}, u32[]{:S(2)}) %collective-permute-start.4) | collective-permute-done | bytes 151584 | tf_op jit(solution)/shard_map/ppermute | solution.py:359
  45.4 0.0 collective-permute-done.5.refs_4_
  45.5 0.0 collective-permute-done.6.refs_6_
  45.5 0.0 copy-done.3
  45.5 7.0 %second_step.1 = (f32[24,192,128]{2,1,0:T(8,128)}, f32[18,48,128]{2,1,0:T(8,128)S(1)}, f32[18,48,128]{2,1,0:T(8,128)S(1)}, f32[18,48,128]{2,1,0:T(8,128)S(1)}, f...) custom-call(f32[6,192,128]{2,1,0:T(8,128)S(1)} %get-tuple-element.24.low_ref.refs_0_, ...), custom_call_target="tpu_custom_call" | custom-call | flops 1 | bytes 1 | tf_op jit(solution)/shard_map/second_step/pallas_call | solution.py:212
  52.5 0.0 collective-permute-start.10
  52.5 3.3 %collective-permute-start.8 = (f32[18,48,128]{2,1,0:T(8,128)S(1)}, f32[18,48,128]{2,1,0:T(8,128)S(1)}, u32[]{:S(2)}, u32[]{:S(2)}) collective-permute-start(f32[18,48,128]{2,1,0:T(8,128)S(1)} %get-tuple-element.35), channel_id=1, source_target_pairs={{0,32},{32,0},{64,96},{96,64},{1,33},{33,1},{65,97},{97,65},{2,34}... | collective-permute-start | bytes 1327112 | tf_op jit(solution)/shard_map/ppermute | solution.py:359
  55.8 0.3 collective-permute-start.9
  56.1 2.1 %collective-permute-done.7.halo_ref = f32[6,192,128]{2,1,0:T(8,128)S(1)} collective-permute-done((f32[6,192,128]{2,1,0:T(8,128)S(1)}, f32[6,192,128]{2,1,0:T(8,128)S(1)}, u32[]{:S(2)}, u32[]{:S(2)}) %collective-permute-start.7) | collective-permute-done | bytes 589856 | tf_op jit(solution)/shard_map/ppermute | solution.py:355
  58.2 1.1 %finish_filtered.1 = (f32[24,192,128]{2,1,0:T(8,128)}, f32[6,48,128]{2,1,0:T(8,128)S(1)}, f32[6,48,128]{2,1,0:T(8,128)S(1)}, f32[6,48,128]{2,1,0:T(8,128)S(1)}, f32[6,48,128]{2,1,0:T(8,128)S(1)}) custom-call(f32[6,192,128]{2,1,0:T(8,128)S(1)} %get-tuple-element.31.partial_ref, ...), custom_call_target="tpu_custom_call", output_to_operand_aliasing={{0}: (2, {})} | custom-call | flops 1 | bytes 1 | tf_op jit(solution)/shard_map/finish_filtered/pallas_call | solution.py:278
  59.3 0.1 collective-permute-start.11
  59.4 3.0 %collective-permute-start.12 = (f32[6,48,128]{2,1,0:T(8,128)S(1)}, f32[6,48,128]{2,1,0:T(8,128)S(1)}, u32[]{:S(2)}, u32[]{:S(2)}) collective-permute-start(f32[6,48,128]{2,1,0:T(8,128)S(1)} %get-tuple-element.40), channel_id=1, source_target_pairs={{0,64},{32,96},{64,0},{96,32},{1,65},{33,97},{65,1},{97,33},{2,66}... | collective-permute-start | bytes 442376 | tf_op jit(solution)/shard_map/ppermute | solution.py:359
  62.4 4.1 %collective-permute-done.10.refs_3_ = f32[18,48,128]{2,1,0:T(8,128)S(1)} collective-permute-done((f32[18,48,128]{2,1,0:T(8,128)S(1)}, f32[18,48,128]{2,1,0:T(8,128)S(1)}, u32[]{:S(2)}, u32[]{:S(2)}) %collective-permute-start.10) | collective-permute-done | bytes 442400 | tf_op jit(solution)/shard_map/ppermute | solution.py:359
  66.5 0.3 collective-permute-start.13
  66.8 0.0 collective-permute-done.8.refs_1_
  66.8 11.7 %collective-permute-done.9.refs_2_ = f32[18,48,128]{2,1,0:T(8,128)S(1)} collective-permute-done((f32[18,48,128]{2,1,0:T(8,128)S(1)}, f32[18,48,128]{2,1,0:T(8,128)S(1)}, u32[]{:S(2)}, u32[]{:S(2)}) %collective-permute-start.9) | collective-permute-done | bytes 442400 | tf_op jit(solution)/shard_map/ppermute | solution.py:359
  78.5 0.4 early_gram.1.before_ref
  78.9 0.0 collective-permute-done.11.refs_1_
  78.9 2.8 %collective-permute-done.12.refs_2_ = f32[6,48,128]{2,1,0:T(8,128)S(1)} collective-permute-done((f32[6,48,128]{2,1,0:T(8,128)S(1)}, f32[6,48,128]{2,1,0:T(8,128)S(1)}, u32[]{:S(2)}, u32[]{:S(2)}) %collective-permute-start.12) | collective-permute-done | bytes 147488 | tf_op jit(solution)/shard_map/ppermute | solution.py:359
  81.7 0.6 collective-permute-done.13.refs_3_
  82.3 0.2 late_gram.1
  82.6 18.4 %all_to_all.9 = f32[128,1,128]{2,1,0:T(1,128)S(1)} all-to-all(f32[128,1,128]{2,1,0:T(1,128)S(1)} %bitcast.21), channel_id=1, replica_groups=mesh['band'=4,'space'=32] {'band','space'}, dimensions={0} | all-to-all | bytes 131072 | tf_op jit(solution)/shard_map/all_to_all | solution.py:391
  101.0 0.2 reduce_sum.9
  101.1 0.1 slice_bitcast_fusion.4
  101.2 0.6 maximum_multiply_fusion
Async XLA Ops:
  1.7 19.4 %collective-permute-start.2 = (f32[6,192,128]{2,1,0:T(8,128)S(1)}, f32[6,192,128]{2,1,0:T(8,128)S(1)}, u32[]{:S(2)}, u32[]{:S(2)}) collective-permute-start(f32[6,192,128]{2,1,0:T(8,128)S(1)} %slice_bitcast_fusion.sent_ref), channel_id=1, source_target_pairs={{0,4},{1,5},{2,6},{3,7},{4,8},{5,9},{6,10},{7,11},{8,12},{9,13},{1... | collective-permute-start | bytes 1769480 | tf_op jit(solution)/shard_map/ppermute | solution.py:355
  3.5 1.7 %copy-start = (f32[1,1,24,192,128]{4,3,2,1,0:T(8,128)S(1)}, f32[1,1,24,192,128]{4,3,2,1,0:T(8,128)}, u32[]{:S(2)}) copy-start(f32[1,1,24,192,128]{4,3,2,1,0:T(8,128)} %param.2) | copy-start | bytes 7077892
  5.1 16.0 %copy-start.1 = (f32[1,1,24,192,128]{4,3,2,1,0:T(8,128)S(1)}, f32[1,1,24,192,128]{4,3,2,1,0:T(8,128)}, u32[]{:S(2)}) copy-start(f32[1,1,24,192,128]{4,3,2,1,0:T(8,128)} %param.2) | copy-start | bytes 7077892
  5.9 14.0 %collective-permute-start.1 = (f32[24,24,128]{2,1,0:T(8,128)S(1)}, f32[24,24,128]{2,1,0:T(8,128)S(1)}, u32[]{:S(2)}, u32[]{:S(2)}) collective-permute-start(f32[24,24,128]{2,1,0:T(8,128)S(1)} %get-tuple-element.23), channel_id=1, source_target_pairs={{0,1},{1,0},{2,3},{3,2},{4,5},{5,4},{6,7},{7,6},{8,9},{9,8},{10,11... | collective-permute-start | bytes 884744 | tf_op jit(solution)/shard_map/ppermute | solution.py:359
  7.5 24.6 %collective-permute-start.3 = (f32[6,192,128]{2,1,0:T(8,128)S(1)}, f32[6,192,128]{2,1,0:T(8,128)S(1)}, u32[]{:S(2)}, u32[]{:S(2)}) collective-permute-start(f32[6,192,128]{2,1,0:T(8,128)S(1)} %get-tuple-element.27), channel_id=1, source_target_pairs={{0,28},{1,29},{2,30},{3,31},{4,0},{5,1},{6,2},{7,3},{8,4},{9,5},{1... | collective-permute-start | bytes 1769480 | tf_op jit(solution)/shard_map/ppermute | solution.py:355
  11.0 8.9 %collective-permute-start = (f32[296,128]{1,0:T(8,128)S(1)}, f32[296,128]{1,0:T(8,128)S(1)}, u32[]{:S(2)}, u32[]{:S(2)}) collective-permute-start(f32[296,128]{1,0:T(8,128)S(1)} %get-tuple-element.22), channel_id=1, source_target_pairs={{0,2},{1,3},{2,0},{3,1},{4,6},{5,7},{6,4},{7,5},{8,10},{9,11},{10,... | collective-permute-start | bytes 454664 | tf_op jit(solution)/shard_map/ppermute | solution.py:359
  21.1 1.7 %copy-start.2 = (f32[1,24,192,128]{3,2,1,0:T(8,128)S(1)}, f32[1,24,192,128]{3,2,1,0:T(8,128)}, u32[]{:S(2)}) copy-start(f32[1,24,192,128]{3,2,1,0:T(8,128)} %param.3) | copy-start | bytes 7077892
  27.9 17.6 %copy-start.3 = (f32[1,24,192,128]{3,2,1,0:T(8,128)S(1)}, f32[1,24,192,128]{3,2,1,0:T(8,128)}, u32[]{:S(2)}) copy-start(f32[1,24,192,128]{3,2,1,0:T(8,128)} %param.3) | copy-start | bytes 7077892
  27.9 17.5 %collective-permute-start.6 = (f32[6,192,128]{2,1,0:T(8,128)S(1)}, f32[6,192,128]{2,1,0:T(8,128)S(1)}, u32[]{:S(2)}, u32[]{:S(2)}) collective-permute-start(f32[6,192,128]{2,1,0:T(8,128)S(1)} %get-tuple-element.24.low_ref.refs_0_), channel_id=1, source_target_pairs={{0,28},{1,29},{2,30},{3,31},{4,0},{5,1},{6,2},{7,3},{8,4},{9,5},{1... | collective-permute-start | bytes 1769480 | tf_op jit(solution)/shard_map/ppermute | solution.py:355
  33.2 12.3 %collective-permute-start.5 = (f32[24,24,128]{2,1,0:T(8,128)S(1)}, f32[24,24,128]{2,1,0:T(8,128)S(1)}, u32[]{:S(2)}, u32[]{:S(2)}) collective-permute-start(f32[24,24,128]{2,1,0:T(8,128)S(1)} %get-tuple-element.30), channel_id=1, source_target_pairs={{0,1},{1,0},{2,3},{3,2},{4,5},{5,4},{6,7},{7,6},{8,9},{9,8},{10,11... | collective-permute-start | bytes 884744 | tf_op jit(solution)/shard_map/ppermute | solution.py:359
  34.8 10.7 %collective-permute-start.4 = (f32[296,128]{1,0:T(8,128)S(1)}, f32[296,128]{1,0:T(8,128)S(1)}, u32[]{:S(2)}, u32[]{:S(2)}) collective-permute-start(f32[296,128]{1,0:T(8,128)S(1)} %get-tuple-element.29), channel_id=1, source_target_pairs={{0,2},{1,3},{2,0},{3,1},{4,6},{5,7},{6,4},{7,5},{8,10},{9,11},{10,... | collective-permute-start | bytes 454664 | tf_op jit(solution)/shard_map/ppermute | solution.py:359
  37.5 20.7 %collective-permute-start.7 = (f32[6,192,128]{2,1,0:T(8,128)S(1)}, f32[6,192,128]{2,1,0:T(8,128)S(1)}, u32[]{:S(2)}, u32[]{:S(2)}) collective-permute-start(f32[6,192,128]{2,1,0:T(8,128)S(1)} %get-tuple-element.28.refs_2_), channel_id=1, source_target_pairs={{0,4},{1,5},{2,6},{3,7},{4,8},{5,9},{6,10},{7,11},{8,12},{9,13},{1... | collective-permute-start | bytes 1769480 | tf_op jit(solution)/shard_map/ppermute | solution.py:355
  52.5 14.0 %collective-permute-start.10 = (f32[18,48,128]{2,1,0:T(8,128)S(1)}, f32[18,48,128]{2,1,0:T(8,128)S(1)}, u32[]{:S(2)}, u32[]{:S(2)}) collective-permute-start(f32[18,48,128]{2,1,0:T(8,128)S(1)} %get-tuple-element.37), channel_id=1, source_target_pairs={{0,96},{32,64},{64,32},{96,0},{1,97},{33,65},{65,33},{97,1},{2,98}... | collective-permute-start | bytes 1327112 | tf_op jit(solution)/shard_map/ppermute | solution.py:359
  52.5 14.4 %collective-permute-start.8 = (f32[18,48,128]{2,1,0:T(8,128)S(1)}, f32[18,48,128]{2,1,0:T(8,128)S(1)}, u32[]{:S(2)}, u32[]{:S(2)}) collective-permute-start(f32[18,48,128]{2,1,0:T(8,128)S(1)} %get-tuple-element.35), channel_id=1, source_target_pairs={{0,32},{32,0},{64,96},{96,64},{1,33},{33,1},{65,97},{97,65},{2,34}... | collective-permute-start | bytes 1327112 | tf_op jit(solution)/shard_map/ppermute | solution.py:359
  55.8 22.7 %collective-permute-start.9 = (f32[18,48,128]{2,1,0:T(8,128)S(1)}, f32[18,48,128]{2,1,0:T(8,128)S(1)}, u32[]{:S(2)}, u32[]{:S(2)}) collective-permute-start(f32[18,48,128]{2,1,0:T(8,128)S(1)} %get-tuple-element.36), channel_id=1, source_target_pairs={{0,64},{32,96},{64,0},{96,32},{1,65},{33,97},{65,1},{97,33},{2,66}... | collective-permute-start | bytes 1327112 | tf_op jit(solution)/shard_map/ppermute | solution.py:359
  59.3 19.6 %collective-permute-start.11 = (f32[6,48,128]{2,1,0:T(8,128)S(1)}, f32[6,48,128]{2,1,0:T(8,128)S(1)}, u32[]{:S(2)}, u32[]{:S(2)}) collective-permute-start(f32[6,48,128]{2,1,0:T(8,128)S(1)} %get-tuple-element.39), channel_id=1, source_target_pairs={{0,32},{32,0},{64,96},{96,64},{1,33},{33,1},{65,97},{97,65},{2,34}... | collective-permute-start | bytes 442376 | tf_op jit(solution)/shard_map/ppermute | solution.py:359
  59.4 22.3 %collective-permute-start.12 = (f32[6,48,128]{2,1,0:T(8,128)S(1)}, f32[6,48,128]{2,1,0:T(8,128)S(1)}, u32[]{:S(2)}, u32[]{:S(2)}) collective-permute-start(f32[6,48,128]{2,1,0:T(8,128)S(1)} %get-tuple-element.40), channel_id=1, source_target_pairs={{0,64},{32,96},{64,0},{96,32},{1,65},{33,97},{65,1},{97,33},{2,66}... | collective-permute-start | bytes 442376 | tf_op jit(solution)/shard_map/ppermute | solution.py:359
  66.5 15.8 %collective-permute-start.13 = (f32[6,48,128]{2,1,0:T(8,128)S(1)}, f32[6,48,128]{2,1,0:T(8,128)S(1)}, u32[]{:S(2)}, u32[]{:S(2)}) collective-permute-start(f32[6,48,128]{2,1,0:T(8,128)S(1)} %get-tuple-element.41), channel_id=1, source_target_pairs={{0,96},{32,64},{64,32},{96,0},{1,97},{33,65},{65,33},{97,1},{2,98}... | collective-permute-start | bytes 442376 | tf_op jit(solution)/shard_map/ppermute | solution.py:359

commit v8 on v6

--- a/solution.py
+++ b/solution.py
@@ -371,8 +371,8 @@
 
 def on_device(orbitals, potential):
     source, local_potential = orbitals[0, 0], potential[0]
-    high_planes = source[source.shape[0] - REACH :]
-    below = shifted(high_planes, 4)
+    high_planes = orbitals[:, :, source.shape[0] - REACH :]
+    below = shifted(high_planes, 4)[0, 0]
     low_planes, *faces = entry(high_planes, source)
     faces = swapped_faces(faces)
     above = shifted(low_planes, -4)

time: 103 us -> 103 us (level)
  no operation moved by 1% of the time
where the time goes in v8:
time: 103 us; the launch traced here: 102 us
  waiting for transfers between devices  36.5 us (35%)
  starting transfers between devices  25.1 us (24%)
  blocking collectives  18.4 us (18%)
  Pallas kernels  15.7 us (15%)
  local copies, waits for them, and re-layouts  5.11 us (5%)
    ppermute x10, waiting for transfers between devices, swapped(): lax.ppermute(array, axis, [(i, i ^ bit) for i in range(lax.axis_size(axis...  31.8 us
    all_to_all x1, blocking collectives, on_device(): everyone = lax.all_to_all(rows, both, 0, 0, tiled=True)  18.4 us
    ppermute x10, starting transfers between devices, swapped(): lax.ppermute(array, axis, [(i, i ^ bit) for i in range(lax.axis_size(axis...  15.6 us
    pallas_call x2, Pallas kernels, apply_stencil(): pl.pallas_call(functools.partial(stencil_kernel, counts, sections, second...  12.1 us
    ppermute x4, starting transfers between devices, shifted(): lax.ppermute(array, 'space', [(i, (i + by) % peers) for i in range(peers)])  9.47 us
    ppermute x4, waiting for transfers between devices, shifted(): lax.ppermute(array, 'space', [(i, (i + by) % peers) for i in range(peers)])  4.75 us
    unnamed x8, local copies, waits for them, and re-layouts  3.34 us
  transfers between devices with their start and end apart: 14, of which 9 were waited for; matrix products, arithmetic and copies ran while one was open for 0% of the time, Pallas kernels for 15%

profile of v8, /device:TPU:0, one launch (start us, length us, event | category | flops | bytes accessed | tf_op | source)
XLA Modules:
  0.0 101.8 jit_solution(16484797720324503183)
XLA Ops:
  0.6 1.1 %slice.14.sent_ref = f32[1,1,6,192,128]{4,3,2,1,0:T(8,128)S(1)} slice(f32[1,1,24,192,128]{4,3,2,1,0:T(8,128)} %param.2), slice={[0:1], [0:1], [18:24], [0:192], [0:128]} | slice | bytes 1179648 | tf_op jit(solution)/shard_map/slice | solution.py:374
  1.7 1.7 %collective-permute-start.2 = (f32[1,1,6,192,128]{4,3,2,1,0:T(8,128)S(1)}, f32[1,1,6,192,128]{4,3,2,1,0:T(8,128)S(1)}, u32[]{:S(2)}, u32[]{:S(2)}) collective-permute-start(f32[1,1,6,192,128]{4,3,2,1,0:T(8,128)S(1)} %slice.14.sent_ref), channel_id=1, source_target_pairs={{0,4},{1,5},{2,6},{3,7},{4,8},{5,9},{6,10},{7,11},{8,12},{9,13},{1... | collective-permute-start | bytes 1769480 | tf_op jit(solution)/shard_map/ppermute | solution.py:355
  3.5 0.0 copy-start
  3.5 1.7 %copy-done = f32[1,1,24,192,128]{4,3,2,1,0:T(8,128)S(1)} copy-done((f32[1,1,24,192,128]{4,3,2,1,0:T(8,128)S(1)}, f32[1,1,24,192,128]{4,3,2,1,0:T(8,128)}, u32[]{:S(2)}) %copy-start) | copy-done | bytes 2359320
  5.1 0.0 copy-start.1
  5.1 0.8 entry.1
  5.9 1.6 %collective-permute-start.1 = (f32[24,24,128]{2,1,0:T(8,128)S(1)}, f32[24,24,128]{2,1,0:T(8,128)S(1)}, u32[]{:S(2)}, u32[]{:S(2)}) collective-permute-start(f32[24,24,128]{2,1,0:T(8,128)S(1)} %get-tuple-element.23), channel_id=1, source_target_pairs={{0,1},{1,0},{2,3},{3,2},{4,5},{5,4},{6,7},{7,6},{8,9},{9,8},{10,11... | collective-permute-start | bytes 884744 | tf_op jit(solution)/shard_map/ppermute | solution.py:359
  7.5 3.5 %collective-permute-start.3 = (f32[6,192,128]{2,1,0:T(8,128)S(1)}, f32[6,192,128]{2,1,0:T(8,128)S(1)}, u32[]{:S(2)}, u32[]{:S(2)}) collective-permute-start(f32[6,192,128]{2,1,0:T(8,128)S(1)} %get-tuple-element.27), channel_id=1, source_target_pairs={{0,28},{1,29},{2,30},{3,31},{4,0},{5,1},{6,2},{7,3},{8,4},{9,5},{1... | collective-permute-start | bytes 1769480 | tf_op jit(solution)/shard_map/ppermute | solution.py:355
  11.0 2.7 %collective-permute-start = (f32[296,128]{1,0:T(8,128)S(1)}, f32[296,128]{1,0:T(8,128)S(1)}, u32[]{:S(2)}, u32[]{:S(2)}) collective-permute-start(f32[296,128]{1,0:T(8,128)S(1)} %get-tuple-element.22), channel_id=1, source_target_pairs={{0,2},{1,3},{2,0},{3,1},{4,6},{5,7},{6,4},{7,5},{8,10},{9,11},{10,... | collective-permute-start | bytes 454664 | tf_op jit(solution)/shard_map/ppermute | solution.py:359
  13.7 6.2 %collective-permute-done.refs_1_ = f32[296,128]{1,0:T(8,128)S(1)} collective-permute-done((f32[296,128]{1,0:T(8,128)S(1)}, f32[296,128]{1,0:T(8,128)S(1)}, u32[]{:S(2)}, u32[]{:S(2)}) %collective-permute-start) | collective-permute-done | bytes 151584 | tf_op jit(solution)/shard_map/ppermute | solution.py:359
  19.9 0.0 collective-permute-done.1.refs_2_
  19.9 1.2 %collective-permute-done.2 = f32[1,1,6,192,128]{4,3,2,1,0:T(8,128)S(1)} collective-permute-done((f32[1,1,6,192,128]{4,3,2,1,0:T(8,128)S(1)}, f32[1,1,6,192,128]{4,3,2,1,0:T(8,128)S(1)}, u32[]{:S(2)}, u32[]{:S(2)}) %collective-permute-start.2) | collective-permute-done | bytes 589856 | tf_op jit(solution)/shard_map/ppermute | solution.py:355
  21.1 0.0 copy-done.1
  21.1 0.0 copy-start.2
  21.1 1.7 %copy-done.2 = f32[1,24,192,128]{3,2,1,0:T(8,128)S(1)} copy-done((f32[1,24,192,128]{3,2,1,0:T(8,128)S(1)}, f32[1,24,192,128]{3,2,1,0:T(8,128)}, u32[]{:S(2)}) %copy-start.2) | copy-done | bytes 2359320
  22.8 5.1 %first_step.1 = (f32[6,192,128]{2,1,0:T(8,128)S(1)}, f32[12,192,128]{2,1,0:T(8,128)S(1)}, f32[6,192,128]{2,1,0:T(8,128)S(1)}) custom-call(f32[24,192,128]{2,1,0:T(8,128)S(1)} %bitcast.8, f32[296,128]{1,0:T(8,128)S(1)} %collective-permute-done.refs_1_, f32[24,24,128]{2,1,0:T(8,128)S(1)} %collective-permute-done.1.refs_2_, f32[24,192,128]{2,1,0:T(8,128)S(1)} %bitcast.10, ...), custom_call_target="tpu_custom_call" | custom-call | flops 1 | bytes 1 | tf_op jit(solution)/shard_map/first_step/pallas_call | solution.py:212
  27.9 0.0 copy-start.3
  27.9 2.7 %collective-permute-start.6 = (f32[6,192,128]{2,1,0:T(8,128)S(1)}, f32[6,192,128]{2,1,0:T(8,128)S(1)}, u32[]{:S(2)}, u32[]{:S(2)}) collective-permute-start(f32[6,192,128]{2,1,0:T(8,128)S(1)} %get-tuple-element.24.low_ref.refs_0_), channel_id=1, source_target_pairs={{0,28},{1,29},{2,30},{3,31},{4,0},{5,1},{6,2},{7,3},{8,4},{9,5},{1... | collective-permute-start | bytes 1769480 | tf_op jit(solution)/shard_map/ppermute | solution.py:355
  30.6 1.5 %collective-permute-done.3.halo_ref = f32[6,192,128]{2,1,0:T(8,128)S(1)} collective-permute-done((f32[6,192,128]{2,1,0:T(8,128)S(1)}, f32[6,192,128]{2,1,0:T(8,128)S(1)}, u32[]{:S(2)}, u32[]{:S(2)}) %collective-permute-start.3) | collective-permute-done | bytes 589856 | tf_op jit(solution)/shard_map/ppermute | solution.py:355
  32.1 1.1 %finish_first.1 = (f32[6,192,128]{2,1,0:T(8,128)S(1)}, f32[296,128]{1,0:T(8,128)S(1)}, f32[24,24,128]{2,1,0:T(8,128)S(1)}) custom-call(f32[6,192,128]{2,1,0:T(8,128)S(1)} %get-tuple-element.24.low_ref.refs_0_, f32[12,192,128]{2,1,0:T(8,128)S(1)} %get-tuple-element.25.middle_ref.refs_1_, f32[6,192,128]{2,1,0:T(8,128)S(1)} %get-tuple-element.26.partial_ref, ...), custom_call_target="tpu_custom_call" | custom-call | flops 1 | bytes 1 | tf_op jit(solution)/shard_map/finish_first/pallas_call | solution.py:253
  33.2 1.6 %collective-permute-start.5 = (f32[24,24,128]{2,1,0:T(8,128)S(1)}, f32[24,24,128]{2,1,0:T(8,128)S(1)}, u32[]{:S(2)}, u32[]{:S(2)}) collective-permute-start(f32[24,24,128]{2,1,0:T(8,128)S(1)} %get-tuple-element.30), channel_id=1, source_target_pairs={{0,1},{1,0},{2,3},{3,2},{4,5},{5,4},{6,7},{7,6},{8,9},{9,8},{10,11... | collective-permute-start | bytes 884744 | tf_op jit(solution)/shard_map/ppermute | solution.py:359
  34.8 2.7 %collective-permute-start.4 = (f32[296,128]{1,0:T(8,128)S(1)}, f32[296,128]{1,0:T(8,128)S(1)}, u32[]{:S(2)}, u32[]{:S(2)}) collective-permute-start(f32[296,128]{1,0:T(8,128)S(1)} %get-tuple-element.29), channel_id=1, source_target_pairs={{0,2},{1,3},{2,0},{3,1},{4,6},{5,7},{6,4},{7,5},{8,10},{9,11},{10,... | collective-permute-start | bytes 454664 | tf_op jit(solution)/shard_map/ppermute | solution.py:359
  37.5 1.6 %collective-permute-start.7 = (f32[6,192,128]{2,1,0:T(8,128)S(1)}, f32[6,192,128]{2,1,0:T(8,128)S(1)}, u32[]{:S(2)}, u32[]{:S(2)}) collective-permute-start(f32[6,192,128]{2,1,0:T(8,128)S(1)} %get-tuple-element.28.refs_2_), channel_id=1, source_target_pairs={{0,4},{1,5},{2,6},{3,7},{4,8},{5,9},{6,10},{7,11},{8,12},{9,13},{1... | collective-permute-start | bytes 1769480 | tf_op jit(solution)/shard_map/ppermute | solution.py:355
  39.1 6.4 %collective-permute-done.4.refs_3_ = f32[296,128]{1,0:T(8,128)S(1)} collective-permute-done((f32[296,128]{1,0:T(8,128)S(1)}, f32[296,128]{1,0:T(8,128)S(1)}, u32[]{:S(2)}, u32[]{:S(2)}) %collective-permute-start.4) | collective-permute-done | bytes 151584 | tf_op jit(solution)/shard_map/ppermute | solution.py:359
  45.4 0.0 collective-permute-done.5.refs_4_
  45.5 0.0 collective-permute-done.6.refs_6_
  45.5 0.0 copy-done.3
  45.5 7.0 %second_step.1 = (f32[24,192,128]{2,1,0:T(8,128)}, f32[18,48,128]{2,1,0:T(8,128)S(1)}, f32[18,48,128]{2,1,0:T(8,128)S(1)}, f32[18,48,128]{2,1,0:T(8,128)S(1)}, f...) custom-call(f32[6,192,128]{2,1,0:T(8,128)S(1)} %get-tuple-element.24.low_ref.refs_0_, ...), custom_call_target="tpu_custom_call" | custom-call | flops 1 | bytes 1 | tf_op jit(solution)/shard_map/second_step/pallas_call | solution.py:212
  52.5 0.0 collective-permute-start.10
  52.5 3.3 %collective-permute-start.8 = (f32[18,48,128]{2,1,0:T(8,128)S(1)}, f32[18,48,128]{2,1,0:T(8,128)S(1)}, u32[]{:S(2)}, u32[]{:S(2)}) collective-permute-start(f32[18,48,128]{2,1,0:T(8,128)S(1)} %get-tuple-element.35), channel_id=1, source_target_pairs={{0,32},{32,0},{64,96},{96,64},{1,33},{33,1},{65,97},{97,65},{2,34}... | collective-permute-start | bytes 1327112 | tf_op jit(solution)/shard_map/ppermute | solution.py:359
  55.8 0.3 collective-permute-start.9
  56.1 2.1 %collective-permute-done.7.halo_ref = f32[6,192,128]{2,1,0:T(8,128)S(1)} collective-permute-done((f32[6,192,128]{2,1,0:T(8,128)S(1)}, f32[6,192,128]{2,1,0:T(8,128)S(1)}, u32[]{:S(2)}, u32[]{:S(2)}) %collective-permute-start.7) | collective-permute-done | bytes 589856 | tf_op jit(solution)/shard_map/ppermute | solution.py:355
  58.2 1.1 %finish_filtered.1 = (f32[24,192,128]{2,1,0:T(8,128)}, f32[6,48,128]{2,1,0:T(8,128)S(1)}, f32[6,48,128]{2,1,0:T(8,128)S(1)}, f32[6,48,128]{2,1,0:T(8,128)S(1)}, f32[6,48,128]{2,1,0:T(8,128)S(1)}) custom-call(f32[6,192,128]{2,1,0:T(8,128)S(1)} %get-tuple-element.31.partial_ref, ...), custom_call_target="tpu_custom_call", output_to_operand_aliasing={{0}: (2, {})} | custom-call | flops 1 | bytes 1 | tf_op jit(solution)/shard_map/finish_filtered/pallas_call | solution.py:278
  59.3 0.1 collective-permute-start.11
  59.4 3.0 %collective-permute-start.12 = (f32[6,48,128]{2,1,0:T(8,128)S(1)}, f32[6,48,128]{2,1,0:T(8,128)S(1)}, u32[]{:S(2)}, u32[]{:S(2)}) collective-permute-start(f32[6,48,128]{2,1,0:T(8,128)S(1)} %get-tuple-element.40), channel_id=1, source_target_pairs={{0,64},{32,96},{64,0},{96,32},{1,65},{33,97},{65,1},{97,33},{2,66}... | collective-permute-start | bytes 442376 | tf_op jit(solution)/shard_map/ppermute | solution.py:359
  62.4 4.1 %collective-permute-done.10.refs_3_ = f32[18,48,128]{2,1,0:T(8,128)S(1)} collective-permute-done((f32[18,48,128]{2,1,0:T(8,128)S(1)}, f32[18,48,128]{2,1,0:T(8,128)S(1)}, u32[]{:S(2)}, u32[]{:S(2)}) %collective-permute-start.10) | collective-permute-done | bytes 442400 | tf_op jit(solution)/shard_map/ppermute | solution.py:359
  66.5 0.3 collective-permute-start.13
  66.8 0.0 collective-permute-done.8.refs_1_
  66.8 11.7 %collective-permute-done.9.refs_2_ = f32[18,48,128]{2,1,0:T(8,128)S(1)} collective-permute-done((f32[18,48,128]{2,1,0:T(8,128)S(1)}, f32[18,48,128]{2,1,0:T(8,128)S(1)}, u32[]{:S(2)}, u32[]{:S(2)}) %collective-permute-start.9) | collective-permute-done | bytes 442400 | tf_op jit(solution)/shard_map/ppermute | solution.py:359
  78.5 0.4 early_gram.1.before_ref
  78.9 0.0 collective-permute-done.11.refs_1_
  78.9 2.8 %collective-permute-done.12.refs_2_ = f32[6,48,128]{2,1,0:T(8,128)S(1)} collective-permute-done((f32[6,48,128]{2,1,0:T(8,128)S(1)}, f32[6,48,128]{2,1,0:T(8,128)S(1)}, u32[]{:S(2)}, u32[]{:S(2)}) %collective-permute-start.12) | collective-permute-done | bytes 147488 | tf_op jit(solution)/shard_map/ppermute | solution.py:359
  81.7 0.6 collective-permute-done.13.refs_3_
  82.3 0.2 late_gram.1
  82.6 18.4 %all_to_all.9 = f32[128,1,128]{2,1,0:T(1,128)S(1)} all-to-all(f32[128,1,128]{2,1,0:T(1,128)S(1)} %bitcast.13), channel_id=1, replica_groups=mesh['band'=4,'space'=32] {'band','space'}, dimensions={0} | all-to-all | bytes 131072 | tf_op jit(solution)/shard_map/all_to_all | solution.py:391
  101.0 0.2 reduce_sum.9
  101.1 0.7 div.6
  (1 shorter events, 0.0 us)
Async XLA Ops:
  1.7 19.4 %collective-permute-start.2 = (f32[1,1,6,192,128]{4,3,2,1,0:T(8,128)S(1)}, f32[1,1,6,192,128]{4,3,2,1,0:T(8,128)S(1)}, u32[]{:S(2)}, u32[]{:S(2)}) collective-permute-start(f32[1,1,6,192,128]{4,3,2,1,0:T(8,128)S(1)} %slice.14.sent_ref), channel_id=1, source_target_pairs={{0,4},{1,5},{2,6},{3,7},{4,8},{5,9},{6,10},{7,11},{8,12},{9,13},{1... | collective-permute-start | bytes 1769480 | tf_op jit(solution)/shard_map/ppermute | solution.py:355
  3.5 1.7 %copy-start = (f32[1,1,24,192,128]{4,3,2,1,0:T(8,128)S(1)}, f32[1,1,24,192,128]{4,3,2,1,0:T(8,128)}, u32[]{:S(2)}) copy-start(f32[1,1,24,192,128]{4,3,2,1,0:T(8,128)} %param.2) | copy-start | bytes 7077892
  5.1 16.0 %copy-start.1 = (f32[1,1,24,192,128]{4,3,2,1,0:T(8,128)S(1)}, f32[1,1,24,192,128]{4,3,2,1,0:T(8,128)}, u32[]{:S(2)}) copy-start(f32[1,1,24,192,128]{4,3,2,1,0:T(8,128)} %param.2) | copy-start | bytes 7077892
  5.9 14.0 %collective-permute-start.1 = (f32[24,24,128]{2,1,0:T(8,128)S(1)}, f32[24,24,128]{2,1,0:T(8,128)S(1)}, u32[]{:S(2)}, u32[]{:S(2)}) collective-permute-start(f32[24,24,128]{2,1,0:T(8,128)S(1)} %get-tuple-element.23), channel_id=1, source_target_pairs={{0,1},{1,0},{2,3},{3,2},{4,5},{5,4},{6,7},{7,6},{8,9},{9,8},{10,11... | collective-permute-start | bytes 884744 | tf_op jit(solution)/shard_map/ppermute | solution.py:359
  7.5 24.6 %collective-permute-start.3 = (f32[6,192,128]{2,1,0:T(8,128)S(1)}, f32[6,192,128]{2,1,0:T(8,128)S(1)}, u32[]{:S(2)}, u32[]{:S(2)}) collective-permute-start(f32[6,192,128]{2,1,0:T(8,128)S(1)} %get-tuple-element.27), channel_id=1, source_target_pairs={{0,28},{1,29},{2,30},{3,31},{4,0},{5,1},{6,2},{7,3},{8,4},{9,5},{1... | collective-permute-start | bytes 1769480 | tf_op jit(solution)/shard_map/ppermute | solution.py:355
  11.0 8.9 %collective-permute-start = (f32[296,128]{1,0:T(8,128)S(1)}, f32[296,128]{1,0:T(8,128)S(1)}, u32[]{:S(2)}, u32[]{:S(2)}) collective-permute-start(f32[296,128]{1,0:T(8,128)S(1)} %get-tuple-element.22), channel_id=1, source_target_pairs={{0,2},{1,3},{2,0},{3,1},{4,6},{5,7},{6,4},{7,5},{8,10},{9,11},{10,... | collective-permute-start | bytes 454664 | tf_op jit(solution)/shard_map/ppermute | solution.py:359
  21.1 1.7 %copy-start.2 = (f32[1,24,192,128]{3,2,1,0:T(8,128)S(1)}, f32[1,24,192,128]{3,2,1,0:T(8,128)}, u32[]{:S(2)}) copy-start(f32[1,24,192,128]{3,2,1,0:T(8,128)} %param.3) | copy-start | bytes 7077892
  27.9 17.6 %copy-start.3 = (f32[1,24,192,128]{3,2,1,0:T(8,128)S(1)}, f32[1,24,192,128]{3,2,1,0:T(8,128)}, u32[]{:S(2)}) copy-start(f32[1,24,192,128]{3,2,1,0:T(8,128)} %param.3) | copy-start | bytes 7077892
  27.9 17.5 %collective-permute-start.6 = (f32[6,192,128]{2,1,0:T(8,128)S(1)}, f32[6,192,128]{2,1,0:T(8,128)S(1)}, u32[]{:S(2)}, u32[]{:S(2)}) collective-permute-start(f32[6,192,128]{2,1,0:T(8,128)S(1)} %get-tuple-element.24.low_ref.refs_0_), channel_id=1, source_target_pairs={{0,28},{1,29},{2,30},{3,31},{4,0},{5,1},{6,2},{7,3},{8,4},{9,5},{1... | collective-permute-start | bytes 1769480 | tf_op jit(solution)/shard_map/ppermute | solution.py:355
  33.2 12.3 %collective-permute-start.5 = (f32[24,24,128]{2,1,0:T(8,128)S(1)}, f32[24,24,128]{2,1,0:T(8,128)S(1)}, u32[]{:S(2)}, u32[]{:S(2)}) collective-permute-start(f32[24,24,128]{2,1,0:T(8,128)S(1)} %get-tuple-element.30), channel_id=1, source_target_pairs={{0,1},{1,0},{2,3},{3,2},{4,5},{5,4},{6,7},{7,6},{8,9},{9,8},{10,11... | collective-permute-start | bytes 884744 | tf_op jit(solution)/shard_map/ppermute | solution.py:359
  34.8 10.7 %collective-permute-start.4 = (f32[296,128]{1,0:T(8,128)S(1)}, f32[296,128]{1,0:T(8,128)S(1)}, u32[]{:S(2)}, u32[]{:S(2)}) collective-permute-start(f32[296,128]{1,0:T(8,128)S(1)} %get-tuple-element.29), channel_id=1, source_target_pairs={{0,2},{1,3},{2,0},{3,1},{4,6},{5,7},{6,4},{7,5},{8,10},{9,11},{10,... | collective-permute-start | bytes 454664 | tf_op jit(solution)/shard_map/ppermute | solution.py:359
  37.5 20.7 %collective-permute-start.7 = (f32[6,192,128]{2,1,0:T(8,128)S(1)}, f32[6,192,128]{2,1,0:T(8,128)S(1)}, u32[]{:S(2)}, u32[]{:S(2)}) collective-permute-start(f32[6,192,128]{2,1,0:T(8,128)S(1)} %get-tuple-element.28.refs_2_), channel_id=1, source_target_pairs={{0,4},{1,5},{2,6},{3,7},{4,8},{5,9},{6,10},{7,11},{8,12},{9,13},{1... | collective-permute-start | bytes 1769480 | tf_op jit(solution)/shard_map/ppermute | solution.py:355
  52.5 14.0 %collective-permute-start.10 = (f32[18,48,128]{2,1,0:T(8,128)S(1)}, f32[18,48,128]{2,1,0:T(8,128)S(1)}, u32[]{:S(2)}, u32[]{:S(2)}) collective-permute-start(f32[18,48,128]{2,1,0:T(8,128)S(1)} %get-tuple-element.37), channel_id=1, source_target_pairs={{0,96},{32,64},{64,32},{96,0},{1,97},{33,65},{65,33},{97,1},{2,98}... | collective-permute-start | bytes 1327112 | tf_op jit(solution)/shard_map/ppermute | solution.py:359
  52.5 14.4 %collective-permute-start.8 = (f32[18,48,128]{2,1,0:T(8,128)S(1)}, f32[18,48,128]{2,1,0:T(8,128)S(1)}, u32[]{:S(2)}, u32[]{:S(2)}) collective-permute-start(f32[18,48,128]{2,1,0:T(8,128)S(1)} %get-tuple-element.35), channel_id=1, source_target_pairs={{0,32},{32,0},{64,96},{96,64},{1,33},{33,1},{65,97},{97,65},{2,34}... | collective-permute-start | bytes 1327112 | tf_op jit(solution)/shard_map/ppermute | solution.py:359
  55.8 22.7 %collective-permute-start.9 = (f32[18,48,128]{2,1,0:T(8,128)S(1)}, f32[18,48,128]{2,1,0:T(8,128)S(1)}, u32[]{:S(2)}, u32[]{:S(2)}) collective-permute-start(f32[18,48,128]{2,1,0:T(8,128)S(1)} %get-tuple-element.36), channel_id=1, source_target_pairs={{0,64},{32,96},{64,0},{96,32},{1,65},{33,97},{65,1},{97,33},{2,66}... | collective-permute-start | bytes 1327112 | tf_op jit(solution)/shard_map/ppermute | solution.py:359
  59.3 19.6 %collective-permute-start.11 = (f32[6,48,128]{2,1,0:T(8,128)S(1)}, f32[6,48,128]{2,1,0:T(8,128)S(1)}, u32[]{:S(2)}, u32[]{:S(2)}) collective-permute-start(f32[6,48,128]{2,1,0:T(8,128)S(1)} %get-tuple-element.39), channel_id=1, source_target_pairs={{0,32},{32,0},{64,96},{96,64},{1,33},{33,1},{65,97},{97,65},{2,34}... | collective-permute-start | bytes 442376 | tf_op jit(solution)/shard_map/ppermute | solution.py:359
  59.4 22.3 %collective-permute-start.12 = (f32[6,48,128]{2,1,0:T(8,128)S(1)}, f32[6,48,128]{2,1,0:T(8,128)S(1)}, u32[]{:S(2)}, u32[]{:S(2)}) collective-permute-start(f32[6,48,128]{2,1,0:T(8,128)S(1)} %get-tuple-element.40), channel_id=1, source_target_pairs={{0,64},{32,96},{64,0},{96,32},{1,65},{33,97},{65,1},{97,33},{2,66}... | collective-permute-start | bytes 442376 | tf_op jit(solution)/shard_map/ppermute | solution.py:359
  66.5 15.8 %collective-permute-start.13 = (f32[6,48,128]{2,1,0:T(8,128)S(1)}, f32[6,48,128]{2,1,0:T(8,128)S(1)}, u32[]{:S(2)}, u32[]{:S(2)}) collective-permute-start(f32[6,48,128]{2,1,0:T(8,128)S(1)} %get-tuple-element.41), channel_id=1, source_target_pairs={{0,96},{32,64},{64,32},{96,0},{1,97},{33,65},{65,33},{97,1},{2,98}... | collective-permute-start | bytes 442376 | tf_op jit(solution)/shard_map/ppermute | solution.py:359
